TPU v7x, 32 devices: a whole 2x2x4 slice. The times are simulated.
32 devices in a mesh: row: 4 (over z), col: 8 (over y, x, core).
Axes of the slice: x: 2, y: 2, z: 4, core: 2. Of those that a mesh axis runs over, the one named last changes fastest.
Arguments:
- embed: bfloat16 [65536, 64], P(('row', 'col')), may hold values from -6 to 6
- tiles: bfloat16 [2048, 128, 128], P(('row', 'col'))
- tile_rows: int32 [2048], P(('row', 'col')), may hold values from 0 to 511, as said below
- tile_cols: int32 [2048], P(('row', 'col')), may hold values from 0 to 511, as said below
- chg_tiles: bfloat16 [1536, 128, 128], P(('row', 'col'))
- chg_rows: int32 [1536], P(('row', 'col')), may hold values from 0 to 511, as said below
- chg_cols: int32 [1536], P(('row', 'col')), may hold values from 0 to 511, as said below
Outputs:
- embedding: float32 [65536, 64], P(('row', 'col'))
Inputs may be any that keep to these rules, and one draw needn't show every extreme that they name: Tile n lies in the row group of the device that holds it: tile_rows[n] // 128 equals (n // 64) // 8. Tile n lies in the column group of the device that holds it: tile_cols[n] // 64 equals (n // 64) % 8. `chg_rows`: one device's list names each transpose owner at most 3 times; in every draw some owner is named exactly 3 times by every device's list. `chg_cols`: read with chg_rows to give the transpose owner.
All inputs are finite; a program needn't handle non-finite values.
Results may differ from a plain program's by a relative error of at most 0.025.
Values may be sent and summed in bfloat16 or wider, within the bound.
No kernel may reach another device: no remote copies, remote signals or barrier semaphores. Data moves between devices by JAX's collectives and lax.ppermute only.
A program may use at most 192 MiB of HBM per device.

v0:
```python
import jax
import jax.numpy as jnp
from jax import lax
from jax.sharding import PartitionSpec as P

ITERS = 3
CAP = 3


def block_terms(own, own_rows, own_cols, taken, taken_rows, taken_cols, blocked, row_blocks):
    own_terms = jnp.einsum(
        "nab,nbk->nak", own, blocked[own_cols], preferred_element_type=jnp.float32
    )
    taken_terms = jnp.einsum(
        "nab,nak->nbk", taken, blocked[taken_cols], preferred_element_type=jnp.float32
    )
    return jax.ops.segment_sum(own_terms, own_rows, row_blocks) + jax.ops.segment_sum(
        taken_terms, taken_rows, row_blocks
    )


def local(embed, tiles, tile_rows, tile_cols, chg_tiles, chg_rows, chg_cols):
    rows_dev, feature_width = embed.shape
    tile_size = tiles.shape[1]
    row_count = lax.axis_size("row")
    col_count = lax.axis_size("col")
    devices = row_count * col_count
    row_blocks = rows_dev * col_count // tile_size
    col_blocks = rows_dev * row_count // tile_size
    sub_rows = rows_dev // devices
    owners = chg_cols // row_blocks * col_count + chg_rows // col_blocks
    position = jnp.arange(owners.shape[0], dtype=jnp.int32)
    earlier = position[None, :] < position[:, None]
    slot_rank = jnp.sum(jnp.logical_and(owners[:, None] == owners[None, :], earlier), axis=1)
    outgoing = (
        jnp.zeros((devices, CAP, tile_size, tile_size), jnp.bfloat16)
        .at[owners, slot_rank]
        .set(chg_tiles)
    )
    placing = jnp.stack([chg_cols % row_blocks, chg_rows % col_blocks], axis=1)
    output_slots = jnp.zeros((devices, CAP, 2), jnp.int32).at[owners, slot_rank].set(placing)
    taken, taken_places = (
        lax.all_to_all(outgoing, ("row", "col"), split_axis=0, concat_axis=0, tiled=True),
        lax.all_to_all(output_slots, ("row", "col"), split_axis=0, concat_axis=0, tiled=True),
    )
    taken = taken.reshape(devices * CAP, tile_size, tile_size)
    taken_places = taken_places.reshape(devices * CAP, 2)
    taken_rows = taken_places[:, 0]
    taken_cols = taken_places[:, 1]
    own_rows = tile_rows % row_blocks
    own_cols = tile_cols % col_blocks
    degree_terms = jax.ops.segment_sum(
        jnp.sum(jnp.abs(tiles), axis=2, dtype=jnp.float32), own_rows, row_blocks
    )
    degree_terms = degree_terms + jax.ops.segment_sum(
        jnp.sum(jnp.abs(taken), axis=1, dtype=jnp.float32), taken_rows, row_blocks
    )
    degree = 1.0 + lax.psum_scatter(
        degree_terms.astype(jnp.bfloat16), "col", scatter_dimension=0, tiled=True
    ).astype(jnp.float32).reshape(rows_dev, 1)
    nodes = rows_dev * devices
    current = embed
    final_output = embed.astype(jnp.float32)
    for iteration in range(ITERS):
        received_terms = lax.all_to_all(
            current.reshape(devices, sub_rows, feature_width),
            ("row", "col"),
            split_axis=0,
            concat_axis=0,
            tiled=True,
        )
        group = lax.all_gather(
            received_terms.reshape(rows_dev, feature_width), "row", axis=0, tiled=True
        )
        blocked = group.reshape(col_blocks, tile_size, feature_width)
        partial_value = block_terms(
            tiles, own_rows, own_cols, taken, taken_rows, taken_cols, blocked, row_blocks
        )
        summed = lax.psum_scatter(
            partial_value.reshape(row_blocks * tile_size, feature_width).astype(jnp.bfloat16),
            "col",
            scatter_dimension=0,
            tiled=True,
        ).astype(jnp.float32)
        scaled = summed / degree
        local_gram = jnp.dot(
            scaled.T, scaled, precision=lax.Precision.HIGHEST, preferred_element_type=jnp.float32
        )
        gram = lax.psum(local_gram, ("row", "col")) / nodes
        lower = jnp.linalg.cholesky(gram)
        final_output = lax.linalg.triangular_solve(
            lower, scaled, left_side=False, lower=True, transpose_a=True
        )
        current = final_output.astype(jnp.bfloat16)
    return final_output


def solution(mesh):
    placed = (
        P(("row", "col"), None),
        P(("row", "col"), None, None),
        P(("row", "col")),
        P(("row", "col")),
        P(("row", "col"), None, None),
        P(("row", "col")),
        P(("row", "col")),
    )
    return jax.shard_map(
        local, mesh=mesh, in_specs=placed, out_specs=P(("row", "col"), None), check_vma=False
    )
```

profile of v0, /device:TPU:0, one launch (start us, length us, event | category | flops | bytes accessed | tf_op | source)
XLA Modules:
  0.0 673.1 jit_solution(17728876150305119598)
XLA Ops:
  8.4 3.0 scatter_fusion.1
  12.2 7.3 %all-to-all-start.1 = ((s32[32,3,2]{1,2,0:T(2,128)}), s32[32,3,2]{1,2,0:T(2,128)S(1)}, u32[]{:S(2)}, u32[]{:S(2)}) async-start(s32[32,3,2]{1,2,0:T(2,128)} %copy.91), calls=%async_computation.1 | async-start | bytes 65536 | tf_op jit(solution)/shard_map/all_to_all | solution.py:44
  22.3 4.5 all-to-all-done.1
  26.8 2.6 all-to-all-start
  30.1 5.6 scatter_fusion.2
  37.5 2.5 all-to-all-done
  40.0 3.3 all-to-all-start.2
  52.2 55.1 %all-gather.4.cloned.1.call-done = bf16[8192,64]{0,1:T(8,128)(2,1)} async-done(((bf16[2048,64]{0,1:T(8,128)(2,1)}), bf16[8192,64]{0,1:T(8,128)(2,1)}) %all-gather.4.cloned.1.call-update) | async-done | bytes 1048592 | tf_op jit(solution)/shard_map/all_gather | solution.py:72
  107.3 2.5 copy_bitcast_fusion.5
  109.8 3.2 gather_fusion.1
  113.0 2.9 gather_fusion
  115.9 4.8 convolution_bitcast_fusion.5
  123.2 10.4 %scatter_fusion = f32[128,128,64]{1,2,0:T(8,128)} fusion(f32[128,128,64]{1,2,0:T(8,128)} %broadcast.112.clone.2, s32[64]{0:T(128)S(1)} %and_select_fusion.5, f32[64,128,64]{1,2,0:T(8,128)} %convolution_bitcast_fusion.5), kind=kCustom, calls=%fused_computation.6 | custom fusion | flops 524288 | bytes 6291712 | tf_op jit(solution)/shard_map/scatter-add | solution.py:17
  136.5 4.1 fusion.40
  143.1 15.2 %scatter_fusion.3 = f32[128,128,64]{1,2,0:T(8,128)} fusion(f32[128,128,64]{1,2,0:T(8,128)} %broadcast.112.clone.3, s32[96]{0:T(128)S(1)} %get-tuple-element.8, f32[96,128,64]{1,2,0:T(8,128)} %fusion.40), kind=kCustom, calls=%fused_computation.9 | custom fusion | flops 786432 | bytes 9437568 | tf_op jit(solution)/shard_map/scatter-add | solution.py:17
  158.3 5.3 copy_bitcast_fusion.2
  166.3 43.9 %reduce-scatter.5.cloned.1.call-done = bf16[2048,64]{0,1:T(8,128)(2,1)} async-done(((bf16[16384,64]{0,1:T(8,128)(2,1)}), bf16[2048,64]{0,1:T(8,128)(2,1)}) %reduce-scatter.5.cloned.1.call-update) | async-done | bytes 262160 | tf_op jit(solution)/shard_map/reduce_scatter | solution.py:79
  211.9 39.5 %psum.21 = f32[64,64]{0,1:T(8,128)S(1)} all-reduce(f32[64,64]{0,1:T(8,128)S(1)} %fusion.5), channel_id=1, replica_groups=mesh['row'=4,'col'=8] {'row','col'}, use_global_device_ids=true, to_apply=%region_11.12 | all-reduce | flops 4096 | bytes 32768 | tf_op jit(solution)/shard_map/psum | solution.py:89
  251.5 5.8 cholesky.59
  258.7 4.9 custom-call.11
  270.0 15.8 %all_to_all.25 = bf16[32,2,2048]{2,1,0:T(2,128)(2,1)} all-to-all(bf16[32,2,2048]{2,1,0:T(2,128)(2,1)S(1)} %reshape.234), channel_id=1, replica_groups=mesh['row'=4,'col'=8] {'row','col'}, dimensions={0} | all-to-all | bytes 524288 | tf_op jit(solution)/shard_map/all_to_all | solution.py:65
  292.6 25.6 %all-gather.6.cloned.1.call-done = bf16[8192,64]{0,1:T(8,128)(2,1)} async-done(((bf16[2048,64]{0,1:T(8,128)(2,1)}), bf16[8192,64]{0,1:T(8,128)(2,1)}) %all-gather.6.cloned.1.call-update) | async-done | bytes 1048592 | tf_op jit(solution)/shard_map/all_gather | solution.py:72
  318.2 2.5 copy_bitcast_fusion.4
  320.7 3.2 gather_fusion.3
  323.9 2.9 gather_fusion.2
  326.8 4.2 fusion.41
  331.0 2.9 convolution_bitcast_fusion.4
  336.4 15.1 %scatter_fusion.5 = f32[128,128,64]{1,2,0:T(8,128)} fusion(f32[128,128,64]{1,2,0:T(8,128)} %broadcast.112.clone.4, s32[96]{0:T(128)S(1)} %get-tuple-element.8, f32[96,128,64]{1,2,0:T(8,128)} %fusion.41), kind=kCustom, calls=%fused_computation.13 | custom fusion | flops 786432 | bytes 9437568 | tf_op jit(solution)/shard_map/scatter-add | solution.py:17
  354.0 10.4 %scatter_fusion.4 = f32[128,128,64]{1,2,0:T(8,128)} fusion(f32[128,128,64]{1,2,0:T(8,128)} %broadcast.112.clone.1, s32[64]{0:T(128)S(1)} %and_select_fusion.5, f32[64,128,64]{1,2,0:T(8,128)} %convolution_bitcast_fusion.4), kind=kCustom, calls=%fused_computation.12 | custom fusion | flops 524288 | bytes 6291712 | tf_op jit(solution)/shard_map/scatter-add | solution.py:17
  364.3 5.3 copy_bitcast_fusion.1
  369.7 41.1 %reduce-scatter.9.cloned.1.call-done = bf16[2048,64]{0,1:T(8,128)(2,1)} async-done(((bf16[16384,64]{0,1:T(8,128)(2,1)}), bf16[2048,64]{0,1:T(8,128)(2,1)}) %reduce-scatter.9.cloned.1.call-update) | async-done | bytes 262160 | tf_op jit(solution)/shard_map/reduce_scatter | solution.py:79
  412.4 39.5 %psum.22 = f32[64,64]{0,1:T(8,128)S(1)} all-reduce(f32[64,64]{0,1:T(8,128)S(1)} %fusion.6), channel_id=1, replica_groups=mesh['row'=4,'col'=8] {'row','col'}, use_global_device_ids=true, to_apply=%region_17.20 | all-reduce | flops 4096 | bytes 32768 | tf_op jit(solution)/shard_map/psum | solution.py:89
  452.0 5.8 cholesky.70
  459.1 4.9 custom-call.12
  470.4 15.9 %all_to_all.26 = bf16[32,2,2048]{2,1,0:T(2,128)(2,1)} all-to-all(bf16[32,2,2048]{2,1,0:T(2,128)(2,1)S(1)} %reshape.236), channel_id=1, replica_groups=mesh['row'=4,'col'=8] {'row','col'}, dimensions={0} | all-to-all | bytes 524288 | tf_op jit(solution)/shard_map/all_to_all | solution.py:65
  493.1 25.6 %all-gather.8.cloned.1.call-done = bf16[8192,64]{0,1:T(8,128)(2,1)} async-done(((bf16[2048,64]{0,1:T(8,128)(2,1)}), bf16[8192,64]{0,1:T(8,128)(2,1)}) %all-gather.8.cloned.1.call-update) | async-done | bytes 1048592 | tf_op jit(solution)/shard_map/all_gather | solution.py:72
  518.7 2.5 copy_bitcast_fusion.3
  521.2 3.2 gather_fusion.5
  524.4 2.9 gather_fusion.4
  527.3 4.2 fusion.42
  531.5 2.9 convolution_bitcast_fusion.3
  537.3 14.4 %scatter_fusion.7 = f32[128,128,64]{1,2,0:T(8,128)} fusion(f32[128,128,64]{1,2,0:T(8,128)} %broadcast.112.clone.5, s32[96]{0:T(128)S(1)} %get-tuple-element.8, f32[96,128,64]{1,2,0:T(8,128)S(1)} %copy-done.2), kind=kCustom, calls=%fused_computation.15 | custom fusion | flops 786432 | bytes 9437568 | tf_op jit(solution)/shard_map/scatter-add | solution.py:17
  554.1 9.0 %scatter_fusion.6 = f32[128,128,64]{1,2,0:T(8,128)} fusion(f32[128,128,64]{1,2,0:T(8,128)} %broadcast.112.clone, s32[64]{0:T(128)S(1)} %and_select_fusion.5, f32[64,128,64]{1,2,0:T(8,128)S(1)} %copy-done.6), kind=kCustom, calls=%fused_computation.14 | custom fusion | flops 524288 | bytes 6291712 | tf_op jit(solution)/shard_map/scatter-add | solution.py:17
  563.1 5.3 copy_bitcast_fusion
  568.4 41.1 %reduce-scatter.11.cloned.1.call-done = bf16[2048,64]{0,1:T(8,128)(2,1)} async-done(((bf16[16384,64]{0,1:T(8,128)(2,1)}), bf16[2048,64]{0,1:T(8,128)(2,1)}) %reduce-scatter.11.cloned.1.call-update) | async-done | bytes 262160 | tf_op jit(solution)/shard_map/reduce_scatter | solution.py:79
  611.2 39.5 %psum.23 = f32[64,64]{0,1:T(8,128)S(1)} all-reduce(f32[64,64]{0,1:T(8,128)S(1)} %fusion.7), channel_id=1, replica_groups=mesh['row'=4,'col'=8] {'row','col'}, use_global_device_ids=true, to_apply=%region_21.24 | all-reduce | flops 4096 | bytes 32768 | tf_op jit(solution)/shard_map/psum | solution.py:89
  650.8 5.8 cholesky.81
  658.0 4.9 custom-call.13
  (104 shorter events, 74.7 us)
Async XLA Ops:
  12.2 14.6 %all-to-all-start.1 = ((s32[32,3,2]{1,2,0:T(2,128)}), s32[32,3,2]{1,2,0:T(2,128)S(1)}, u32[]{:S(2)}, u32[]{:S(2)}) async-start(s32[32,3,2]{1,2,0:T(2,128)} %copy.91), calls=%async_computation.1 | async-start | bytes 65536 | tf_op jit(solution)/shard_map/all_to_all | solution.py:44
  26.8 13.2 %all-to-all-start = ((bf16[32,2,2048]{2,1,0:T(2,128)(2,1)}), bf16[32,2,2048]{2,1,0:T(2,128)(2,1)S(1)}, u32[]{:S(2)}, u32[]{:S(2)}) async-start(bf16[32,2,2048]{2,1,0:T(2,128)(2,1)} %reshape.232), calls=%async_computation | async-start | bytes 524288 | tf_op jit(solution)/shard_map/all_to_all | solution.py:65
  35.8 1.7 copy-start.3
  37.5 11.5 %copy-start.7 = (s32[64]{0:T(128)S(1)}, s32[64]{0:T(128)}, u32[]{:S(2)}) copy-start(s32[64]{0:T(128)} %param.12) | copy-start | bytes 772
  40.0 93.6 %all-to-all-start.2 = ((bf16[32,3,128,128]{3,2,1,0:T(8,128)(2,1)}), bf16[32,3,128,128]{3,2,1,0:T(8,128)(2,1)S(1)}, u32[]{:S(2)}, u32[]{:S(2)}) async-start(bf16[32,3,128,128]{3,2,1,0:T(8,128)(2,1)} %copy-done.3), calls=%async_computation.2 | async-start | bytes 6291456 | tf_op jit(solution)/shard_map/all_to_all | solution.py:43
  43.3 8.8 %copy-start.8 = (s32[64]{0:T(128)S(1)}, s32[64]{0:T(128)}, u32[]{:S(2)}) copy-start(s32[64]{0:T(128)} %param.13) | copy-start | bytes 772
  43.3 64.0 %all-gather.4.cloned.1.call-start = ((), (), s32[]{:S(2)}) async-start(), calls=%async_computation.9 | async-start | bytes 1310720 | tf_op jit(solution)/shard_map/all_gather | solution.py:72
  48.9 116.7 %reduce-scatter.7.cloned.1.call-start = ((), (), s32[]{:S(2)}) async-start(), calls=%async_computation.11 | async-start | bytes 36864 | tf_op jit(solution)/shard_map/reduce_scatter | solution.py:58
  136.2 74.0 %reduce-scatter.5.cloned.1.call-start = ((), (), s32[]{:S(2)}) async-start(), calls=%async_computation.10 | async-start | bytes 2359296 | tf_op jit(solution)/shard_map/reduce_scatter | solution.py:79
  163.6 154.6 %all-gather.6.cloned.1.call-start = ((), (), s32[]{:S(2)}) async-start(), calls=%async_computation.12 | async-start | bytes 1310720 | tf_op jit(solution)/shard_map/all_gather | solution.py:72
  292.3 118.4 %reduce-scatter.9.cloned.1.call-start = ((), (), s32[]{:S(2)}) async-start(), calls=%async_computation.13 | async-start | bytes 2359296 | tf_op jit(solution)/shard_map/reduce_scatter | solution.py:79
  326.8 4.2 copy-start
  326.8 4.2 copy-start.5
  369.6 149.1 %all-gather.8.cloned.1.call-start = ((), (), s32[]{:S(2)}) async-start(), calls=%async_computation.14 | async-start | bytes 1310720 | tf_op jit(solution)/shard_map/all_gather | solution.py:72
  492.8 116.7 %reduce-scatter.11.cloned.1.call-start = ((), (), s32[]{:S(2)}) async-start(), calls=%async_computation.15 | async-start | bytes 2359296 | tf_op jit(solution)/shard_map/reduce_scatter | solution.py:79
  527.3 4.2 copy-start.1
  527.3 4.2 copy-start.4
  534.4 2.9 copy-start.2
  551.6 2.5 copy-start.6
Sparse Core Ops, SparseCore 0:
  49.0 58.2 all-gather.3
  292.4 25.7 all-gather.5
  492.9 25.7 all-gather.7
Sparse Core Ops, SparseCore 1:
  136.3 29.2 reduce-scatter.6
  169.1 41.1 reduce-scatter.4
  369.7 41.0 reduce-scatter.8
  568.5 40.9 reduce-scatter.10
where the time goes:
time: 683 us; the launch traced here: 673 us
  waiting for transfers between devices  241 us (35%)
  blocking collectives  150 us (22%)
  other arithmetic  134 us (20%)
  local copies, waits for them, and re-layouts  84.3 us (12%)
  matrix products  33.7 us (5%)
  between operations  15.6 us (2%)
  starting transfers between devices  14.1 us (2%)
    reduce_scatter x3, waiting for transfers between devices, local(): lax.psum_scatter(partial_value.reshape(row_blocks * tile_size, feature_wi...  126 us
    psum x3, blocking collectives, local(): gram = lax.psum(local_gram, ('row', 'col')) / nodes  118 us
    all_gather x3, waiting for transfers between devices, local(): lax.all_gather(received_terms.reshape(rows_dev, feature_width), 'row', ax...  106 us
    scatter-add x3, other arithmetic, block_terms(): jax.ops.segment_sum(taken_terms, taken_rows, row_blocks)  44.7 us
    all_to_all x2, blocking collectives, local(): lax.all_to_all(current.reshape(devices, sub_rows, feature_width), ('row',...  31.7 us
    scatter-add x3, other arithmetic, block_terms(): jax.ops.segment_sum(own_terms, own_rows, row_blocks)  29.7 us
    another operation x9, other arithmetic, local(): lower = jnp.linalg.cholesky(gram)  19.6 us
    another operation x6, other arithmetic, local(): lax.linalg.triangular_solve(lower, scaled, left_side=False, lower=True, t...  16.6 us
  transfers between devices with their start and end apart: 10, of which 9 were waited for; matrix products, arithmetic and copies ran while one was open for 11% of the time, Pallas kernels for 0%

commit v1 on v0

v1 whole, which is shorter than its diff:
```python
import functools

import jax
import jax.numpy as jnp
from jax import lax
from jax.experimental import pallas as pl
from jax.experimental.pallas import tpu as pltpu
from jax.sharding import PartitionSpec as P

ITERS = 3
CAP = 3
F32 = jnp.float32
BF16 = jnp.bfloat16
VMEM = pl.BlockSpec(memory_space=pltpu.VMEM)
SMEM = pl.BlockSpec(memory_space=pltpu.SMEM)
ANY = pl.BlockSpec(memory_space=pl.ANY)
LIMIT = 32 * 1024 * 1024
BIG = 60 * 1024 * 1024


def exchange(value, axis, distance):
    size = lax.axis_size(axis)
    return lax.ppermute(value, axis, [(i, i ^ distance) for i in range(size)])


def pack_kernel(devices, row_blocks, col_blocks, col_count, rows, cols, chg, slots, places, counts, sem):
    total = slots.shape[0]

    def clear(i, carry):
        slots[i] = jnp.zeros(slots.shape[1:], slots.dtype)
        places[i] = 0
        return carry

    lax.fori_loop(0, total, clear, 0)

    def reset(i, carry):
        counts[i] = 0
        return carry

    lax.fori_loop(0, devices, reset, 0)

    def place(i, carry):
        row, col = cols[i], rows[i]
        owner = row // row_blocks * col_count + col // col_blocks
        rank = counts[owner]
        counts[owner] = rank + 1
        slot = owner * CAP + rank
        places[slot] = row % row_blocks * col_blocks + col % col_blocks
        pltpu.make_async_copy(chg.at[i], slots.at[slot], sem).start()
        return carry

    lax.fori_loop(0, chg.shape[0], place, 0)
    pltpu.make_async_copy(chg, slots.at[pl.ds(0, chg.shape[0])], sem).wait()


def degree_kernel(tile_rows, chg_cols, tiles, chg, tiles_t, degree):
    degree[...] = jnp.zeros(degree.shape, F32)

    def own(i, carry):
        tile = tiles[i].T
        tiles_t[i] = tile
        block = tile_rows[i]
        degree[pl.ds(block, 1), :] += jnp.sum(jnp.abs(tile.astype(F32)), axis=0, keepdims=True)
        return carry

    lax.fori_loop(0, tiles.shape[0], own, 0)

    def changed(i, carry):
        block = chg_cols[i]
        degree[pl.ds(block, 1), :] += jnp.sum(jnp.abs(chg[i].astype(F32)), axis=0, keepdims=True)
        return carry

    lax.fori_loop(0, chg.shape[0], changed, 0)


def merge_kernel(row_size, sub, place, *refs):
    outs = refs[-(refs[0].shape[1] // refs[-1].shape[2] // row_size) :]
    sources = refs[: len(refs) - len(outs)]
    features, tile = outs[0].shape[1:]
    groups = tile // sub
    member, family = place[0] % groups, place[0] // groups
    lane = lax.broadcasted_iota(jnp.int32, (features, tile), 1) // sub
    for distance, out in enumerate(outs):
        for r in range(row_size):
            block = r * len(outs) + jnp.bitwise_xor(family, distance)
            at = pl.ds(pl.multiple_of(block * tile, tile), tile)
            value = sources[0][:, at].astype(F32)
            for d in range(1, groups):
                g = jnp.bitwise_xor(member, d)
                moved = pltpu.roll(sources[d][:, at].astype(F32), (g - member) * sub % tile, 1)
                value = jnp.where(lane == g, moved, value)
            out[r] = value.astype(BF16)


def product_kernel(by_column, sub, row_size, core, own_rows, own_x, taken_rows, taken_x, tiles_t, taken, *rest):
    pieces, (keep, send), scratch = rest[:row_size], rest[row_size : row_size + 2], rest[row_size + 2 :]
    x_buf, own_buf, taken_buf, total, out_buf, x_sem, own_sem, taken_sem, out_sem = scratch
    per_device = pieces[0].shape[0]
    tile = own_buf.shape[1]
    x_copies = [
        pltpu.make_async_copy(piece, x_buf.at[pl.ds(i * per_device, per_device)], x_sem.at[i])
        for i, piece in enumerate(pieces)
    ]
    own_copy = pltpu.make_async_copy(tiles_t, own_buf, own_sem)
    taken_copy = pltpu.make_async_copy(taken, taken_buf, taken_sem)
    for copy in x_copies:
        copy.start()
    own_copy.start()
    taken_copy.start()

    def clear(i, carry):
        total[i] = jnp.zeros(total.shape[1:], F32)
        return carry

    lax.fori_loop(0, total.shape[0], clear, 0, unroll=8)
    for copy in x_copies:
        copy.wait()
    for copy, buf, rows, blocks in ((own_copy, own_buf, own_rows, own_x), (taken_copy, taken_buf, taken_rows, taken_x)):
        copy.wait()

        def add(i, carry, buf=buf, rows=rows, blocks=blocks):
            total[rows[i]] += jnp.dot(x_buf[blocks[i]], buf[i], preferred_element_type=F32)
            return carry

        lax.fori_loop(0, buf.shape[0], add, 0, unroll=8)
    half = out_buf.shape[1]
    groups = tile // sub
    if by_column:
        per_row = 2 * half // groups
        lane = lax.broadcasted_iota(jnp.int32, total.shape[1:], 1) // sub

        def regroup(r, carry):
            for part in range(per_row):
                for j in range(per_row):
                    base = j * groups * per_device + part + r * per_row
                    blocks = [total[base + g * per_device] for g in range(groups)]
                    for side in range(groups):
                        column = part * groups + side
                        value = blocks[0]
                        for g in range(groups):
                            shift = (g - side) * sub % tile
                            moved = pltpu.roll(blocks[g], shift, 1) if shift else blocks[g]
                            value = moved if g == 0 else jnp.where(lane == g, moved, value)
                        out_buf[column % 2, column // 2, r * per_row + j] = value.astype(BF16)
            return carry

        lax.fori_loop(0, row_size, regroup, 0)
    else:
        for chip in range(half):
            for side in range(2):

                def straight(i, carry, chip=chip, side=side):
                    out_buf[side, chip, i] = total[(2 * chip + side) * per_device + i].astype(BF16)
                    return carry

                lax.fori_loop(0, per_device, straight, 0, unroll=4)
    mine = core[0]
    keep_copy = pltpu.make_async_copy(out_buf.at[mine], keep, out_sem.at[0])
    send_copy = pltpu.make_async_copy(out_buf.at[1 - mine], send, out_sem.at[1])
    keep_copy.start()
    send_copy.start()
    keep_copy.wait()
    send_copy.wait()


def pair_kernel(chip, keep, other, *out):
    mine = chip[0]
    for i, piece in enumerate(out):
        there = jnp.bitwise_xor(mine, i + 1)

        def add(b, carry, piece=piece, there=there):
            piece[b] = (keep[there, b].astype(F32) + other[there, b].astype(F32)).astype(BF16)
            return carry

        lax.fori_loop(0, piece.shape[0], add, 0, unroll=4)


def scale_kernel(normalize, chip, keep, other, degree, inverse, *rest):
    received, (rounded, scaled) = rest[:-2], rest[-2:]
    mine = chip[0]

    def add(b, carry):
        total = keep[mine, b].astype(F32) + other[mine, b].astype(F32)
        for piece in received:
            total = total + piece[b].astype(F32)
        total = total / degree[pl.ds(b, 1), :]
        if normalize:
            total = jnp.dot(inverse[...], total, precision=lax.Precision.HIGHEST, preferred_element_type=F32)
        scaled[b] = total
        rounded[b] = total.astype(BF16)
        return carry

    lax.fori_loop(0, rounded.shape[0], add, 0, unroll=4)


def gram_kernel(scaled, gram):
    total = jnp.zeros(gram.shape, F32)
    for b in range(scaled.shape[0]):
        block = scaled[b]
        total = total + lax.dot_general(
            block, block, (((1,), (1,)), ((), ())), precision=lax.Precision.HIGHEST, preferred_element_type=F32
        )
    gram[...] = total


def final_kernel(scaled, inverse, out):
    tile = scaled.shape[2]
    for b in range(scaled.shape[0]):
        out[:, b * tile : (b + 1) * tile] = jnp.dot(
            inverse[...], scaled[b], precision=lax.Precision.HIGHEST, preferred_element_type=F32
        )


def params(limit=LIMIT):
    return pltpu.CompilerParams(vmem_limit_bytes=limit)


def sum_all(gram):
    for axis, distances in (("col", [1]), ("col", range(2, lax.axis_size("col"), 2)), ("row", range(1, lax.axis_size("row")))):
        parts = [exchange(gram, axis, d) for d in distances]
        for part in parts:
            gram = gram + part
    return gram


def inverse_factor(gram):
    lower = jnp.linalg.cholesky(gram)
    return lax.linalg.triangular_solve(lower, jnp.eye(gram.shape[0], dtype=F32), left_side=True, lower=True)


def local(embed, tiles, tile_rows, tile_cols, chg_tiles, chg_rows, chg_cols):
    rows_dev, features = embed.shape
    tile = tiles.shape[1]
    row_size, col_size = lax.axis_size("row"), lax.axis_size("col")
    devices = row_size * col_size
    per_device = rows_dev // tile
    row_blocks, col_blocks = per_device * col_size, per_device * row_size
    sub = rows_dev // devices
    groups = tile // sub
    per_row = col_size // groups
    half = col_size // 2
    nodes = rows_dev * devices
    row, col = lax.axis_index("row"), lax.axis_index("col")
    core = (col % 2).reshape(1)
    chip = (col // 2).reshape(1)
    block = jax.ShapeDtypeStruct((per_device, features, tile), BF16)
    block32 = jax.ShapeDtypeStruct((per_device, features, tile), F32)

    slots, places = pl.pallas_call(
        functools.partial(pack_kernel, devices, row_blocks, col_blocks, col_size),
        out_shape=(
            jax.ShapeDtypeStruct((devices * CAP, tile, tile), BF16),
            jax.ShapeDtypeStruct((devices * CAP,), jnp.int32),
        ),
        in_specs=[SMEM, SMEM, ANY],
        out_specs=(VMEM, SMEM),
        scratch_shapes=[pltpu.SMEM((devices,), jnp.int32), pltpu.SemaphoreType.DMA],
        compiler_params=params(),
        name="pack",
    )(chg_rows, chg_cols, chg_tiles)
    taken = lax.all_to_all(
        slots.reshape(devices, CAP, tile, tile), ("row", "col"), split_axis=0, concat_axis=0, tiled=True
    ).reshape(devices * CAP, tile, tile)
    embed, tiles, chg_tiles, places = lax.optimization_barrier((embed, tiles, chg_tiles, places))
    all_places = places[None]
    for axis, size in (("col", col_size), ("row", row_size)):
        distance = 1
        while distance < size:
            all_places = jnp.concatenate([all_places, exchange(all_places, axis, distance)], axis=0)
            distance *= 2
    me = row * col_size + col
    my_places = lax.dynamic_slice_in_dim(all_places, me * CAP, CAP, 1)
    my_places = my_places[jnp.bitwise_xor(jnp.arange(devices), me)].reshape(devices * CAP)

    def x_block(position, first):
        from_row = jnp.bitwise_xor(position % per_device // per_row, row) * per_device
        outer, inner = position // per_device, position % per_row
        if first:
            return from_row + jnp.bitwise_xor(inner, col // groups) * row_size + outer
        return from_row + outer * per_row + inner

    own_rows, own_cols = tile_rows % row_blocks, tile_cols % col_blocks
    taken_rows, taken_cols = my_places // col_blocks, my_places % col_blocks

    tiles_t, degree_terms = pl.pallas_call(
        degree_kernel,
        out_shape=(
            jax.ShapeDtypeStruct(tiles.shape, BF16),
            jax.ShapeDtypeStruct((row_blocks * row_size, tile), F32),
        ),
        in_specs=[SMEM, SMEM, VMEM, VMEM],
        out_specs=(VMEM, VMEM),
        compiler_params=params(),
        name="degree",
    )(tile_rows, chg_cols, tiles, chg_tiles)
    degree_terms = degree_terms.reshape(row_size, row_blocks, tile)
    degree = lax.dynamic_index_in_dim(degree_terms, row, 0, False)
    for d in range(1, row_size):
        degree = degree + exchange(
            lax.dynamic_index_in_dim(degree_terms, jnp.bitwise_xor(row, d), 0, False), "row", d
        )
    degree = degree + exchange(degree, "col", 1)
    degree = 1.0 + degree + sum(exchange(degree, "col", d) for d in range(2, col_size, 2))
    node_degree = lax.dynamic_slice_in_dim(degree, col * per_device, per_device, 0)
    column_degree = lax.dynamic_index_in_dim(
        degree.reshape(per_row, groups, row_size, col_size, sub), col, 3, False
    )
    column_degree = column_degree.transpose(2, 0, 1, 3).reshape(per_device, tile)

    embed_t = embed.T
    joined = pl.pallas_call(
        functools.partial(merge_kernel, row_size, sub),
        out_shape=(jax.ShapeDtypeStruct((row_size, features, tile), BF16),) * per_row,
        in_specs=[SMEM] + [VMEM] * groups,
        out_specs=(VMEM,) * per_row,
        compiler_params=params(),
        name="merge",
    )(col.reshape(1), embed_t, *[exchange(embed_t, "col", d) for d in range(1, groups)])
    current = jnp.concatenate(
        [joined[0]] + [exchange(joined[d], "col", d * groups) for d in range(1, per_row)], axis=0
    )
    inverse = jnp.eye(features, dtype=F32)
    scaled = None
    total_gram = None
    for iteration in range(ITERS):
        last = iteration == ITERS - 1
        gathered = [current] + [exchange(current, "row", d) for d in range(1, row_size)]
        if iteration:
            total_gram = sum_all(gram)
            gathered[0], total_gram = lax.optimization_barrier((gathered[0], total_gram))
        keep, send = pl.pallas_call(
            functools.partial(product_kernel, not last, sub, row_size),
            out_shape=(jax.ShapeDtypeStruct((half, *block.shape), BF16),) * 2,
            in_specs=[SMEM] * 5 + [ANY] * (2 + row_size),
            out_specs=(ANY, ANY),
            scratch_shapes=[
                pltpu.VMEM((row_size * per_device, features, tile), BF16),
                pltpu.VMEM(tiles.shape, BF16),
                pltpu.VMEM((devices * CAP, tile, tile), BF16),
                pltpu.VMEM((row_blocks, features, tile), F32),
                pltpu.VMEM((2, half, *block.shape), BF16),
                pltpu.SemaphoreType.DMA((row_size,)),
                pltpu.SemaphoreType.DMA,
                pltpu.SemaphoreType.DMA,
                pltpu.SemaphoreType.DMA((2,)),
            ],
            compiler_params=params(BIG),
            name="product",
        )(
            core, own_rows, x_block(own_cols, iteration == 0), taken_rows, x_block(taken_cols, iteration == 0),
            tiles_t, taken, *gathered,
        )
        other = exchange(send, "col", 1)
        paired = pl.pallas_call(
            pair_kernel,
            out_shape=(block,) * (half - 1),
            in_specs=[SMEM, VMEM, VMEM],
            out_specs=(VMEM,) * (half - 1),
            compiler_params=params(),
            name="pair",
        )(chip, keep, other)
        received = [exchange(piece, "col", 2 * (i + 1)) for i, piece in enumerate(paired)]
        if iteration:
            total_gram = lax.optimization_barrier((total_gram, paired[-1]))[0]
            inverse = inverse_factor(total_gram / nodes)
        current, scaled = pl.pallas_call(
            functools.partial(scale_kernel, iteration > 0),
            out_shape=(block, block32),
            in_specs=[SMEM] + [VMEM] * (4 + half - 1),
            out_specs=(VMEM, VMEM),
            compiler_params=params(),
            name="scale",
        )(chip, keep, other, node_degree if last else column_degree, inverse, *received)
        gram = pl.pallas_call(
            gram_kernel,
            out_shape=jax.ShapeDtypeStruct((features, features), F32),
            in_specs=[VMEM],
            out_specs=VMEM,
            compiler_params=params(),
            name="gram",
        )(scaled)
    inverse = inverse_factor(sum_all(gram) / nodes)
    out = pl.pallas_call(
        final_kernel,
        out_shape=jax.ShapeDtypeStruct((features, rows_dev), F32),
        in_specs=[VMEM, VMEM],
        out_specs=VMEM,
        compiler_params=params(),
        name="final",
    )(scaled, inverse)
    return out.T


def solution(mesh):
    placed = (
        P(("row", "col"), None),
        P(("row", "col"), None, None),
        P(("row", "col")),
        P(("row", "col")),
        P(("row", "col"), None, None),
        P(("row", "col")),
        P(("row", "col")),
    )
    return jax.shard_map(
        local, mesh=mesh, in_specs=placed, out_specs=P(("row", "col"), None), check_vma=False
    )
```

time: 683 us -> 328 us (0.48); the launches traced: 673 us -> 327 us
  blocking collectives: 150 us -> 0 us
  waiting for transfers between devices: 241 us -> 143 us
  other arithmetic: 134 us -> 39.7 us
  local copies, waits for them, and re-layouts: 84.3 us -> 17.8 us
  starting transfers between devices: 14.1 us -> 76.1 us
  Pallas kernels: 0 us -> 48.9 us
  matrix products: 33.7 us -> 0.76 us
  between operations: 15.6 us -> 0.62 us
    ppermute x0 -> x58, waiting for transfers between devices: none -> 143 us  [exchange(): return lax.ppermute(value, axis, [(i, i ^ distance) for i in range(size)])]
    reduce_scatter x4 -> x0, waiting for transfers between devices: 128 us -> none  [the longest x3 126 us: local(): lax.psum_scatter(partial_value.reshape(row_blocks * tile_size, feature_wi...]
    psum x3 -> x0, blocking collectives: 118 us -> none  [local(): gram = lax.psum(local_gram, ('row', 'col')) / nodes]
    all_gather x3 -> x0, waiting for transfers between devices: 106 us -> none  [local(): lax.all_gather(received_terms.reshape(rows_dev, feature_width), 'row', ax...]
    scatter-add x8 -> x0, other arithmetic: 76.2 us -> none  [the longest x3 44.7 us: block_terms(): jax.ops.segment_sum(taken_terms, taken_rows, row_blocks)]
    ppermute x0 -> x58, starting transfers between devices: none -> 68.7 us  [exchange(): return lax.ppermute(value, axis, [(i, i ^ distance) for i in range(size)])]
    pallas_call x0 -> x16, Pallas kernels: none -> 48.9 us  [the longest x3 26.6 us: local(): pl.pallas_call(functools.partial(product_kernel, not last, sub, row_size)...]
    all_to_all x2 -> x0, blocking collectives: 31.7 us -> none  [local(): lax.all_to_all(current.reshape(devices, sub_rows, feature_width), ('row',...]
  transfers between devices with their start and end apart: 10 -> 59, of which waited for: 9 -> 37; matrix products, arithmetic and copies ran while one was open for 11% -> 9% of each run, Pallas kernels for 0% -> 2%
where the time goes in v1:
time: 328 us; the launch traced here: 327 us
  waiting for transfers between devices  143 us (44%)
  starting transfers between devices  76.1 us (23%)
  Pallas kernels  48.9 us (15%)
  other arithmetic  39.7 us (12%)
  local copies, waits for them, and re-layouts  17.8 us (5%)
    ppermute x58, waiting for transfers between devices, exchange(): return lax.ppermute(value, axis, [(i, i ^ distance) for i in range(size)])  143 us
    ppermute x58, starting transfers between devices, exchange(): return lax.ppermute(value, axis, [(i, i ^ distance) for i in range(size)])  68.7 us
    pallas_call x3, Pallas kernels, local(): pl.pallas_call(functools.partial(product_kernel, not last, sub, row_size)...  26.6 us
    another operation x9, other arithmetic, inverse_factor(): lower = jnp.linalg.cholesky(gram)  19.6 us
    another operation x6, other arithmetic, inverse_factor(): lax.linalg.triangular_solve(lower, jnp.eye(gram.shape[0], dtype=F32), lef...  16.7 us
    unnamed x61, local copies, waits for them, and re-layouts  14.8 us
    all_to_all x1, starting transfers between devices, local(): lax.all_to_all(slots.reshape(devices, CAP, tile, tile), ('row', 'col'), s...  7.42 us
    pallas_call x1, Pallas kernels, local(): pl.pallas_call(degree_kernel, out_shape=(jax.ShapeDtypeStruct(tiles.shape...  7.01 us
  transfers between devices with their start and end apart: 59, of which 37 were waited for; matrix products, arithmetic and copies ran while one was open for 9% of the time, Pallas kernels for 2%

profile of v1, /device:TPU:0, one launch (start us, length us, event | category | flops | bytes accessed | tf_op | source)
XLA Modules:
  0.0 327.2 jit_solution(11298943158022311744)
XLA Ops:
  2.7 5.2 %pack.1 = (bf16[96,128,128]{2,1,0:T(8,128)(2,1)S(1)}, s32[96]{0:T(128)S(1)}) custom-call(s32[48]{0:T(128)S(1)} %copy-done.16, s32[48]{0:T(128)S(1)} %copy-done.14, bf16[48,128,128]{2,1,0:T(8,128)(2,1)S(1)} %copy-done.1), custom_call_target="tpu_custom_call" | custom-call | tf_op jit(solution)/shard_map/pack/pallas_call | solution.py:249
  7.9 1.7 copy-done.9
  9.6 7.4 %all-to-all-start = ((bf16[32,3,128,128]{3,2,1,0:T(8,128)(2,1)}), bf16[32,3,128,128]{3,2,1,0:T(8,128)(2,1)}, u32[]{:S(2)}, u32[]{:S(2)}) async-start(bf16[32,3,128,128]{3,2,1,0:T(8,128)(2,1)} %bitcast.55), calls=%async_computation | async-start | bytes 6291456 | tf_op jit(solution)/shard_map/all_to_all | solution.py:261
  18.2 1.8 collective-permute-start.1
  20.5 17.6 %collective-permute-done.1 = s32[2,96]{1,0:T(2,128)S(1)} collective-permute-done((s32[2,96]{1,0:T(2,128)S(1)}, s32[2,96]{1,0:T(2,128)S(1)}, u32[]{:S(2)}, u32[]{:S(2)}) %collective-permute-start.1) | collective-permute-done | bytes 800 | tf_op jit(solution)/shard_map/ppermute | solution.py:23
  39.8 2.1 collective-permute-done.2
  42.2 26.7 %collective-permute-done.3 = s32[8,96]{1,0:T(8,128)S(1)} collective-permute-done((s32[8,96]{1,0:T(8,128)S(1)}, s32[8,96]{1,0:T(8,128)S(1)}, u32[]{:S(2)}, u32[]{:S(2)}) %collective-permute-start.3) | collective-permute-done | bytes 3104 | tf_op jit(solution)/shard_map/ppermute | solution.py:23
  69.0 4.2 %collective-permute-start.4 = (s32[16,96]{1,0:T(8,128)S(1)}, s32[16,96]{1,0:T(8,128)S(1)}, u32[]{:S(2)}, u32[]{:S(2)}) collective-permute-start(s32[16,96]{1,0:T(8,128)S(1)} %concatenate.25), channel_id=1, source_target_pairs={{0,16},{8,24},{16,0},{24,8},{1,17},{9,25},{17,1},{25,9},{2,18},{10... | collective-permute-start | bytes 18440 | tf_op jit(solution)/shard_map/ppermute | solution.py:23
  74.8 7.0 %degree.1 = (bf16[64,128,128]{2,1,0:T(8,128)(2,1)S(1)}, f32[512,128]{1,0:T(8,128)S(1)}) custom-call(s32[64]{0:T(128)S(1)} %copy-done.17, s32[48]{0:T(128)S(1)} %copy-done.15, bf16[64,128,128]{2,1,0:T(8,128)(2,1)S(1)} %copy-done.10, bf16[48,128,128]{2,1,0:T(8,128)(2,1)S(1)} %copy-done.2), custom_call_target="tpu_custom_call" | custom-call | tf_op jit(solution)/shard_map/degree/pallas_call | solution.py:285
  83.2 5.5 %collective-permute-done.4 = s32[16,96]{1,0:T(8,128)S(1)} collective-permute-done((s32[16,96]{1,0:T(8,128)S(1)}, s32[16,96]{1,0:T(8,128)S(1)}, u32[]{:S(2)}, u32[]{:S(2)}) %collective-permute-start.4) | collective-permute-done | bytes 6176 | tf_op jit(solution)/shard_map/ppermute | solution.py:23
  94.0 1.9 collective-permute-done.7
  96.0 1.7 collective-permute-done.8
  97.7 2.0 collective-permute-start.11
  99.7 2.4 collective-permute-start.9
  103.1 5.7 %collective-permute-done.11.rest_3_ = bf16[16,64,128]{2,1,0:T(8,128)(2,1)S(1)} collective-permute-done((bf16[16,64,128]{2,1,0:T(8,128)(2,1)S(1)}, bf16[16,64,128]{2,1,0:T(8,128)(2,1)S(1)}, u32[]{:S(2)}, u32[]{:S(2)}) %collective-permute-start.11) | collective-permute-done | bytes 262176 | tf_op jit(solution)/shard_map/ppermute | solution.py:23
  108.8 11.0 %collective-permute-done.10.rest_2_ = bf16[16,64,128]{2,1,0:T(8,128)(2,1)S(1)} collective-permute-done((bf16[16,64,128]{2,1,0:T(8,128)(2,1)S(1)}, bf16[16,64,128]{2,1,0:T(8,128)(2,1)S(1)}, u32[]{:S(2)}, u32[]{:S(2)}) %collective-permute-start.10) | collective-permute-done | bytes 262176 | tf_op jit(solution)/shard_map/ppermute | solution.py:23
  120.6 9.0 %product.3 = (bf16[4,16,64,128]{3,2,1,0:T(8,128)(2,1)}, bf16[4,16,64,128]{3,2,1,0:T(8,128)(2,1)}) custom-call(s32[1]{0:T(128)} %bitcast.1.core, s32[64]{0:T(128)} %and_select_fusion.11.own_rows, s32[64]{0:T(128)} %get-tuple-element.87.own_x, s32[96]{0:T(128)} %get-tuple-element.95.taken_rows, s32[96]{0:T(128)} %get-tuple-element.83.taken_x, ...), custom_call_target="tpu_custom_call" | custom-call | tf_op jit(solution)/shard_map/product/pallas_call | solution.py:331
  129.8 1.7 collective-permute-start.15
  131.5 1.8 collective-permute-start.14
  134.3 2.4 collective-permute-done.15
  136.7 3.0 collective-permute-done.14
  148.1 2.2 collective-permute-start.22
  152.0 4.2 %collective-permute-done.20.rest_0_ = bf16[16,64,128]{2,1,0:T(8,128)(2,1)S(1)} collective-permute-done((bf16[16,64,128]{2,1,0:T(8,128)(2,1)}, bf16[16,64,128]{2,1,0:T(8,128)(2,1)S(1)}, u32[]{:S(2)}, u32[]{:S(2)}) %collective-permute-start.20) | collective-permute-done | bytes 262176 | tf_op jit(solution)/shard_map/ppermute | solution.py:23
  156.2 4.1 %collective-permute-done.21.rest_1_ = bf16[16,64,128]{2,1,0:T(8,128)(2,1)S(1)} collective-permute-done((bf16[16,64,128]{2,1,0:T(8,128)(2,1)S(1)}, bf16[16,64,128]{2,1,0:T(8,128)(2,1)S(1)}, u32[]{:S(2)}, u32[]{:S(2)}) %collective-permute-start.21) | collective-permute-done | bytes 262176 | tf_op jit(solution)/shard_map/ppermute | solution.py:23
  169.5 1.7 collective-permute-start.29
  171.8 2.2 collective-permute-start.32
  174.0 2.2 collective-permute-start.30
  176.9 2.0 collective-permute-start.27
  179.5 16.6 %collective-permute-done.28 = f32[64,64]{0,1:T(8,128)S(1)} collective-permute-done((f32[64,64]{0,1:T(8,128)S(1)}, f32[64,64]{0,1:T(8,128)S(1)}, u32[]{:S(2)}, u32[]{:S(2)}) %collective-permute-start.28) | collective-permute-done | bytes 16416 | tf_op jit(solution)/shard_map/ppermute | solution.py:23
  197.6 9.0 %product.4 = (bf16[4,16,64,128]{3,2,1,0:T(8,128)(2,1)}, bf16[4,16,64,128]{3,2,1,0:T(8,128)(2,1)}) custom-call(s32[1]{0:T(128)} %bitcast.1.core, s32[64]{0:T(128)} %and_select_fusion.11.own_rows, s32[64]{0:T(128)} %add_add_fusion.9.own_x, s32[96]{0:T(128)} %get-tuple-element.95.taken_rows, s32[96]{0:T(128)} %add_add_fusion.8.taken_x, ...), custom_call_target="tpu_custom_call" | custom-call | tf_op jit(solution)/shard_map/product/pallas_call | solution.py:331
  206.8 2.9 collective-permute-done.33.other
  213.3 5.8 %cholesky.59 = f32[64,64]{1,0:T(8,128)S(1)} custom-call(f32[64,64]{1,0:T(8,128)S(1)} %fusion.16), custom_call_target="Cholesky" | custom-call | tf_op jit(solution)/shard_map/jit(cholesky)/cholesky | solution.py:227
  222.7 4.9 %custom-call.7 = f32[1,64,64]{1,2,0:T(8,128)S(1)} custom-call(f32[1,64,64]{2,1,0:T(8,128)S(1)} %fusion.8), custom_call_target="InvertDiagBlocksLowerTriangular" | custom-call | tf_op jit(solution)/shard_map/triangular_solve/custom-call.0 | solution.py:228
  235.3 2.1 collective-permute-start.46
  237.4 2.3 collective-permute-start.44
  239.7 2.2 collective-permute-start.43
  241.9 15.2 %collective-permute-done.43 = f32[64,64]{0,1:T(8,128)S(1)} collective-permute-done((f32[64,64]{0,1:T(8,128)S(1)}, f32[64,64]{0,1:T(8,128)S(1)}, u32[]{:S(2)}, u32[]{:S(2)}) %collective-permute-start.43) | collective-permute-done | bytes 16416 | tf_op jit(solution)/shard_map/ppermute | solution.py:23
  257.1 4.3 %collective-permute-start.41 = (f32[64,64]{0,1:T(8,128)S(1)}, f32[64,64]{0,1:T(8,128)S(1)}, u32[]{:S(2)}, u32[]{:S(2)}) collective-permute-start(f32[64,64]{0,1:T(8,128)S(1)} %add_add_fusion.3), channel_id=1, source_target_pairs={{0,8},{8,0},{16,24},{24,16},{1,9},{9,1},{17,25},{25,17},{2,10},{10... | collective-permute-start | bytes 49160 | tf_op jit(solution)/shard_map/ppermute | solution.py:23
  261.4 1.9 collective-permute-done.41
  264.9 8.5 %product.5 = (bf16[4,16,64,128]{3,2,1,0:T(8,128)(2,1)}, bf16[4,16,64,128]{3,2,1,0:T(8,128)(2,1)}) custom-call(s32[1]{0:T(128)} %bitcast.1.core, s32[64]{0:T(128)} %and_select_fusion.11.own_rows, s32[64]{0:T(128)} %add_add_fusion.9.own_x, s32[96]{0:T(128)} %get-tuple-element.95.taken_rows, s32[96]{0:T(128)} %add_add_fusion.8.taken_x, ...), custom_call_target="tpu_custom_call" | custom-call | tf_op jit(solution)/shard_map/product/pallas_call | solution.py:331
  273.5 2.8 collective-permute-done.47.other
  280.1 5.8 %cholesky.70 = f32[64,64]{1,0:T(8,128)S(1)} custom-call(f32[64,64]{1,0:T(8,128)S(1)} %fusion.14), custom_call_target="Cholesky" | custom-call | tf_op jit(solution)/shard_map/jit(cholesky)/cholesky | solution.py:227
  289.3 4.9 %custom-call.8 = f32[1,64,64]{1,2,0:T(8,128)S(1)} custom-call(f32[1,64,64]{2,1,0:T(8,128)S(1)} %fusion.9), custom_call_target="InvertDiagBlocksLowerTriangular" | custom-call | tf_op jit(solution)/shard_map/triangular_solve/custom-call.0 | solution.py:228
  295.7 1.8 scale.5
  305.9 1.8 collective-permute-start.57
  307.7 1.7 collective-permute-start.56
  313.5 5.8 %cholesky.81 = f32[64,64]{1,0:T(8,128)S(1)} custom-call(f32[64,64]{1,0:T(8,128)S(1)} %fusion.12), custom_call_target="Cholesky" | custom-call | tf_op jit(solution)/shard_map/jit(cholesky)/cholesky | solution.py:227
  320.7 4.9 %custom-call.9 = f32[1,64,64]{1,2,0:T(8,128)S(1)} custom-call(f32[1,64,64]{2,1,0:T(8,128)S(1)} %fusion.10), custom_call_target="InvertDiagBlocksLowerTriangular" | custom-call | tf_op jit(solution)/shard_map/triangular_solve/custom-call.0 | solution.py:228
  (212 shorter events, 80.8 us)
Async XLA Ops:
  9.6 110.2 %all-to-all-start = ((bf16[32,3,128,128]{3,2,1,0:T(8,128)(2,1)}), bf16[32,3,128,128]{3,2,1,0:T(8,128)(2,1)}, u32[]{:S(2)}, u32[]{:S(2)}) async-start(bf16[32,3,128,128]{3,2,1,0:T(8,128)(2,1)} %bitcast.55), calls=%async_computation | async-start | bytes 6291456 | tf_op jit(solution)/shard_map/all_to_all | solution.py:261
  17.3 72.2 %collective-permute-start.5 = (bf16[64,2048]{1,0:T(8,128)(2,1)S(1)}, bf16[64,2048]{1,0:T(8,128)(2,1)S(1)}, u32[]{:S(2)}, u32[]{:S(2)}) collective-permute-start(bf16[64,2048]{1,0:T(8,128)(2,1)S(1)} %bitcast.56), channel_id=1, source_target_pairs={{0,1},{1,0},{2,3},{3,2},{4,5},{5,4},{6,7},{7,6},{8,9},{9,8},{10,11... | collective-permute-start | bytes 786440 | tf_op jit(solution)/shard_map/ppermute | solution.py:23
  18.2 19.9 %collective-permute-start.1 = (s32[2,96]{1,0:T(2,128)S(1)}, s32[2,96]{1,0:T(2,128)S(1)}, u32[]{:S(2)}, u32[]{:S(2)}) collective-permute-start(s32[2,96]{1,0:T(2,128)S(1)} %pad_add_fusion.2), channel_id=1, source_target_pairs={{0,2},{1,3},{2,0},{3,1},{4,6},{5,7},{6,4},{7,5},{8,10},{9,11},{10,... | collective-permute-start | bytes 2312 | tf_op jit(solution)/shard_map/ppermute | solution.py:23
  42.0 27.0 %collective-permute-start.3 = (s32[8,96]{1,0:T(8,128)S(1)}, s32[8,96]{1,0:T(8,128)S(1)}, u32[]{:S(2)}, u32[]{:S(2)}) collective-permute-start(s32[8,96]{1,0:T(8,128)S(1)} %pad_add_fusion), channel_id=1, source_target_pairs={{0,8},{8,0},{16,24},{24,16},{1,9},{9,1},{17,25},{25,17},{2,10},{10... | collective-permute-start | bytes 9224 | tf_op jit(solution)/shard_map/ppermute | solution.py:23
  69.0 19.7 %collective-permute-start.4 = (s32[16,96]{1,0:T(8,128)S(1)}, s32[16,96]{1,0:T(8,128)S(1)}, u32[]{:S(2)}, u32[]{:S(2)}) collective-permute-start(s32[16,96]{1,0:T(8,128)S(1)} %concatenate.25), channel_id=1, source_target_pairs={{0,16},{8,24},{16,0},{24,8},{1,17},{9,25},{17,1},{25,9},{2,18},{10... | collective-permute-start | bytes 18440 | tf_op jit(solution)/shard_map/ppermute | solution.py:23
  89.7 4.3 %collective-permute-start.6 = (bf16[4,64,128]{2,1,0:T(8,128)(2,1)S(1)}, bf16[4,64,128]{2,1,0:T(8,128)(2,1)S(1)}, u32[]{:S(2)}, u32[]{:S(2)}) collective-permute-start(bf16[4,64,128]{2,1,0:T(8,128)(2,1)S(1)} %get-tuple-element.53), channel_id=1, source_target_pairs={{0,2},{1,3},{2,0},{3,1},{4,6},{5,7},{6,4},{7,5},{8,10},{9,11},{10,... | collective-permute-start | bytes 196616 | tf_op jit(solution)/shard_map/ppermute | solution.py:23
  91.0 5.0 %collective-permute-start.7 = (bf16[4,64,128]{2,1,0:T(8,128)(2,1)S(1)}, bf16[4,64,128]{2,1,0:T(8,128)(2,1)S(1)}, u32[]{:S(2)}, u32[]{:S(2)}) collective-permute-start(bf16[4,64,128]{2,1,0:T(8,128)(2,1)S(1)} %get-tuple-element.54), channel_id=1, source_target_pairs={{0,4},{1,5},{2,6},{3,7},{4,0},{5,1},{6,2},{7,3},{8,12},{9,13},{10,... | collective-permute-start | bytes 196616 | tf_op jit(solution)/shard_map/ppermute | solution.py:23
  92.5 5.2 %collective-permute-start.8 = (bf16[4,64,128]{2,1,0:T(8,128)(2,1)S(1)}, bf16[4,64,128]{2,1,0:T(8,128)(2,1)S(1)}, u32[]{:S(2)}, u32[]{:S(2)}) collective-permute-start(bf16[4,64,128]{2,1,0:T(8,128)(2,1)S(1)} %get-tuple-element.55), channel_id=1, source_target_pairs={{0,6},{1,7},{2,4},{3,5},{4,2},{5,3},{6,0},{7,1},{8,14},{9,15},{10,... | collective-permute-start | bytes 196616 | tf_op jit(solution)/shard_map/ppermute | solution.py:23
  97.7 11.2 %collective-permute-start.11 = (bf16[16,64,128]{2,1,0:T(8,128)(2,1)S(1)}, bf16[16,64,128]{2,1,0:T(8,128)(2,1)S(1)}, u32[]{:S(2)}, u32[]{:S(2)}) collective-permute-start(bf16[16,64,128]{2,1,0:T(8,128)(2,1)S(1)} %constant_dynamic-update-slice_fusion.rest_0_), channel_id=1, source_target_pairs={{0,24},{8,16},{16,8},{24,0},{1,25},{9,17},{17,9},{25,1},{2,26},{10... | collective-permute-start | bytes 786440 | tf_op jit(solution)/shard_map/ppermute | solution.py:23
  99.7 20.1 %collective-permute-start.10 = (bf16[16,64,128]{2,1,0:T(8,128)(2,1)S(1)}, bf16[16,64,128]{2,1,0:T(8,128)(2,1)S(1)}, u32[]{:S(2)}, u32[]{:S(2)}) collective-permute-start(bf16[16,64,128]{2,1,0:T(8,128)(2,1)S(1)} %constant_dynamic-update-slice_fusion.rest_0_), channel_id=1, source_target_pairs={{0,16},{8,24},{16,0},{24,8},{1,17},{9,25},{17,1},{25,9},{2,18},{10... | collective-permute-start | bytes 786440 | tf_op jit(solution)/shard_map/ppermute | solution.py:23
  99.7 20.1 %collective-permute-start.9 = (bf16[16,64,128]{2,1,0:T(8,128)(2,1)S(1)}, bf16[16,64,128]{2,1,0:T(8,128)(2,1)S(1)}, u32[]{:S(2)}, u32[]{:S(2)}) collective-permute-start(bf16[16,64,128]{2,1,0:T(8,128)(2,1)S(1)} %constant_dynamic-update-slice_fusion.rest_0_), channel_id=1, source_target_pairs={{0,8},{8,0},{16,24},{24,16},{1,9},{9,1},{17,25},{25,17},{2,10},{10... | collective-permute-start | bytes 786440 | tf_op jit(solution)/shard_map/ppermute | solution.py:23
  129.6 15.0 %collective-permute-start.12 = (bf16[4,16,64,128]{3,2,1,0:T(8,128)(2,1)}, bf16[4,16,64,128]{3,2,1,0:T(8,128)(2,1)S(1)}, u32[]{:S(2)}, u32[]{:S(2)}) collective-permute-start(bf16[4,16,64,128]{3,2,1,0:T(8,128)(2,1)} %get-tuple-element.57), channel_id=1, source_target_pairs={{0,1},{1,0},{2,3},{3,2},{4,5},{5,4},{6,7},{7,6},{8,9},{9,8},{10,11... | collective-permute-start | bytes 3145736 | tf_op jit(solution)/shard_map/ppermute | solution.py:23
  129.7 4.5 %collective-permute-start.13 = (f32[128,128]{1,0:T(8,128)S(1)}, f32[128,128]{1,0:T(8,128)S(1)}, u32[]{:S(2)}, u32[]{:S(2)}) collective-permute-start(f32[128,128]{1,0:T(8,128)S(1)} %get-tuple-element.91), channel_id=1, source_target_pairs={{0,8},{8,0},{16,24},{24,16},{1,9},{9,1},{17,25},{25,17},{2,10},{10... | collective-permute-start | bytes 196616 | tf_op jit(solution)/shard_map/ppermute | solution.py:23
  129.8 6.9 %collective-permute-start.15 = (f32[128,128]{1,0:T(8,128)S(1)}, f32[128,128]{1,0:T(8,128)S(1)}, u32[]{:S(2)}, u32[]{:S(2)}) collective-permute-start(f32[128,128]{1,0:T(8,128)S(1)} %get-tuple-element.92), channel_id=1, source_target_pairs={{0,24},{8,16},{16,8},{24,0},{1,25},{9,17},{17,9},{25,1},{2,26},{10... | collective-permute-start | bytes 196616 | tf_op jit(solution)/shard_map/ppermute | solution.py:23
  131.5 8.1 %collective-permute-start.14 = (f32[128,128]{1,0:T(8,128)S(1)}, f32[128,128]{1,0:T(8,128)S(1)}, u32[]{:S(2)}, u32[]{:S(2)}) collective-permute-start(f32[128,128]{1,0:T(8,128)S(1)} %get-tuple-element.93), channel_id=1, source_target_pairs={{0,16},{8,24},{16,0},{24,8},{1,17},{9,25},{17,1},{25,9},{2,18},{10... | collective-permute-start | bytes 196616 | tf_op jit(solution)/shard_map/ppermute | solution.py:23
  141.0 7.0 %collective-permute-start.19 = (f32[128,128]{1,0:T(8,128)S(1)}, f32[128,128]{1,0:T(8,128)S(1)}, u32[]{:S(2)}, u32[]{:S(2)}) collective-permute-start(f32[128,128]{1,0:T(8,128)S(1)} %add.250), channel_id=1, source_target_pairs={{0,6},{1,7},{2,4},{3,5},{4,2},{5,3},{6,0},{7,1},{8,14},{9,15},{10,... | collective-permute-start | bytes 196616 | tf_op jit(solution)/shard_map/ppermute | solution.py:23
  141.8 8.4 %collective-permute-start.18 = (f32[128,128]{1,0:T(8,128)S(1)}, f32[128,128]{1,0:T(8,128)S(1)}, u32[]{:S(2)}, u32[]{:S(2)}) collective-permute-start(f32[128,128]{1,0:T(8,128)S(1)} %add.250), channel_id=1, source_target_pairs={{0,4},{1,5},{2,6},{3,7},{4,0},{5,1},{6,2},{7,3},{8,12},{9,13},{10,... | collective-permute-start | bytes 196616 | tf_op jit(solution)/shard_map/ppermute | solution.py:23
  143.2 7.0 %collective-permute-start.17 = (f32[128,128]{1,0:T(8,128)S(1)}, f32[128,128]{1,0:T(8,128)S(1)}, u32[]{:S(2)}, u32[]{:S(2)}) collective-permute-start(f32[128,128]{1,0:T(8,128)S(1)} %add.250), channel_id=1, source_target_pairs={{0,2},{1,3},{2,0},{3,1},{4,6},{5,7},{6,4},{7,5},{8,10},{9,11},{10,... | collective-permute-start | bytes 196616 | tf_op jit(solution)/shard_map/ppermute | solution.py:23
  146.7 9.5 %collective-permute-start.20 = (bf16[16,64,128]{2,1,0:T(8,128)(2,1)}, bf16[16,64,128]{2,1,0:T(8,128)(2,1)S(1)}, u32[]{:S(2)}, u32[]{:S(2)}) collective-permute-start(bf16[16,64,128]{2,1,0:T(8,128)(2,1)} %get-tuple-element.59), channel_id=1, source_target_pairs={{0,2},{1,3},{2,0},{3,1},{4,6},{5,7},{6,4},{7,5},{8,10},{9,11},{10,... | collective-permute-start | bytes 786440 | tf_op jit(solution)/shard_map/ppermute | solution.py:23
  147.4 12.9 %collective-permute-start.21 = (bf16[16,64,128]{2,1,0:T(8,128)(2,1)S(1)}, bf16[16,64,128]{2,1,0:T(8,128)(2,1)S(1)}, u32[]{:S(2)}, u32[]{:S(2)}) collective-permute-start(bf16[16,64,128]{2,1,0:T(8,128)(2,1)S(1)} %get-tuple-element.60), channel_id=1, source_target_pairs={{0,4},{1,5},{2,6},{3,7},{4,0},{5,1},{6,2},{7,3},{8,12},{9,13},{10,... | collective-permute-start | bytes 786440 | tf_op jit(solution)/shard_map/ppermute | solution.py:23
  148.1 12.2 %collective-permute-start.22 = (bf16[16,64,128]{2,1,0:T(8,128)(2,1)S(1)}, bf16[16,64,128]{2,1,0:T(8,128)(2,1)S(1)}, u32[]{:S(2)}, u32[]{:S(2)}) collective-permute-start(bf16[16,64,128]{2,1,0:T(8,128)(2,1)S(1)} %get-tuple-element.61), channel_id=1, source_target_pairs={{0,6},{1,7},{2,4},{3,5},{4,2},{5,3},{6,0},{7,1},{8,14},{9,15},{10,... | collective-permute-start | bytes 786440 | tf_op jit(solution)/shard_map/ppermute | solution.py:23
  162.8 4.8 %collective-permute-start.26 = (f32[64,64]{0,1:T(8,128)S(1)}, f32[64,64]{0,1:T(8,128)S(1)}, u32[]{:S(2)}, u32[]{:S(2)}) collective-permute-start(f32[64,64]{0,1:T(8,128)S(1)} %add.257), channel_id=1, source_target_pairs={{0,6},{1,7},{2,4},{3,5},{4,2},{5,3},{6,0},{7,1},{8,14},{9,15},{10,... | collective-permute-start | bytes 49160 | tf_op jit(solution)/shard_map/ppermute | solution.py:23
  164.2 3.9 %collective-permute-start.25 = (f32[64,64]{0,1:T(8,128)S(1)}, f32[64,64]{0,1:T(8,128)S(1)}, u32[]{:S(2)}, u32[]{:S(2)}) collective-permute-start(f32[64,64]{0,1:T(8,128)S(1)} %add.257), channel_id=1, source_target_pairs={{0,4},{1,5},{2,6},{3,7},{4,0},{5,1},{6,2},{7,3},{8,12},{9,13},{10,... | collective-permute-start | bytes 49160 | tf_op jit(solution)/shard_map/ppermute | solution.py:23
  165.6 3.9 %collective-permute-start.24 = (f32[64,64]{0,1:T(8,128)S(1)}, f32[64,64]{0,1:T(8,128)S(1)}, u32[]{:S(2)}, u32[]{:S(2)}) collective-permute-start(f32[64,64]{0,1:T(8,128)S(1)} %add.257), channel_id=1, source_target_pairs={{0,2},{1,3},{2,0},{3,1},{4,6},{5,7},{6,4},{7,5},{8,10},{9,11},{10,... | collective-permute-start | bytes 49160 | tf_op jit(solution)/shard_map/ppermute | solution.py:23
  169.5 7.4 %collective-permute-start.29 = (f32[64,64]{0,1:T(8,128)S(1)}, f32[64,64]{0,1:T(8,128)S(1)}, u32[]{:S(2)}, u32[]{:S(2)}) collective-permute-start(f32[64,64]{0,1:T(8,128)S(1)} %add_add_fusion.5), channel_id=1, source_target_pairs={{0,24},{8,16},{16,8},{24,0},{1,25},{9,17},{17,9},{25,1},{2,26},{10... | collective-permute-start | bytes 49160 | tf_op jit(solution)/shard_map/ppermute | solution.py:23
  171.8 24.3 %collective-permute-start.32 = (bf16[16,64,128]{2,1,0:T(8,128)(2,1)S(1)}, bf16[16,64,128]{2,1,0:T(8,128)(2,1)S(1)}, u32[]{:S(2)}, u32[]{:S(2)}) collective-permute-start(bf16[16,64,128]{2,1,0:T(8,128)(2,1)S(1)} %get-tuple-element.64.rest_0_), channel_id=1, source_target_pairs={{0,24},{8,16},{16,8},{24,0},{1,25},{9,17},{17,9},{25,1},{2,26},{10... | collective-permute-start | bytes 786440 | tf_op jit(solution)/shard_map/ppermute | solution.py:23
  174.0 22.1 %collective-permute-start.31 = (bf16[16,64,128]{2,1,0:T(8,128)(2,1)S(1)}, bf16[16,64,128]{2,1,0:T(8,128)(2,1)S(1)}, u32[]{:S(2)}, u32[]{:S(2)}) collective-permute-start(bf16[16,64,128]{2,1,0:T(8,128)(2,1)S(1)} %get-tuple-element.64.rest_0_), channel_id=1, source_target_pairs={{0,16},{8,24},{16,0},{24,8},{1,17},{9,25},{17,1},{25,9},{2,18},{10... | collective-permute-start | bytes 786440 | tf_op jit(solution)/shard_map/ppermute | solution.py:23
  174.0 22.2 %collective-permute-start.30 = (bf16[16,64,128]{2,1,0:T(8,128)(2,1)S(1)}, bf16[16,64,128]{2,1,0:T(8,128)(2,1)S(1)}, u32[]{:S(2)}, u32[]{:S(2)}) collective-permute-start(bf16[16,64,128]{2,1,0:T(8,128)(2,1)S(1)} %get-tuple-element.64.rest_0_), channel_id=1, source_target_pairs={{0,8},{8,0},{16,24},{24,16},{1,9},{9,1},{17,25},{25,17},{2,10},{10... | collective-permute-start | bytes 786440 | tf_op jit(solution)/shard_map/ppermute | solution.py:23
  176.2 19.9 %collective-permute-start.28 = (f32[64,64]{0,1:T(8,128)S(1)}, f32[64,64]{0,1:T(8,128)S(1)}, u32[]{:S(2)}, u32[]{:S(2)}) collective-permute-start(f32[64,64]{0,1:T(8,128)S(1)} %add_add_fusion.5), channel_id=1, source_target_pairs={{0,16},{8,24},{16,0},{24,8},{1,17},{9,25},{17,1},{25,9},{2,18},{10... | collective-permute-start | bytes 49160 | tf_op jit(solution)/shard_map/ppermute | solution.py:23
  176.9 19.2 %collective-permute-start.27 = (f32[64,64]{0,1:T(8,128)S(1)}, f32[64,64]{0,1:T(8,128)S(1)}, u32[]{:S(2)}, u32[]{:S(2)}) collective-permute-start(f32[64,64]{0,1:T(8,128)S(1)} %add_add_fusion.5), channel_id=1, source_target_pairs={{0,8},{8,0},{16,24},{24,16},{1,9},{9,1},{17,25},{25,17},{2,10},{10... | collective-permute-start | bytes 49160 | tf_op jit(solution)/shard_map/ppermute | solution.py:23
  211.8 16.6 %collective-permute-start.36 = (bf16[16,64,128]{2,1,0:T(8,128)(2,1)S(1)}, bf16[16,64,128]{2,1,0:T(8,128)(2,1)S(1)}, u32[]{:S(2)}, u32[]{:S(2)}) collective-permute-start(bf16[16,64,128]{2,1,0:T(8,128)(2,1)S(1)} %get-tuple-element.68), channel_id=1, source_target_pairs={{0,6},{1,7},{2,4},{3,5},{4,2},{5,3},{6,0},{7,1},{8,14},{9,15},{10,... | collective-permute-start | bytes 786440 | tf_op jit(solution)/shard_map/ppermute | solution.py:23
  219.9 8.3 %collective-permute-start.34 = (bf16[16,64,128]{2,1,0:T(8,128)(2,1)}, bf16[16,64,128]{2,1,0:T(8,128)(2,1)S(1)}, u32[]{:S(2)}, u32[]{:S(2)}) collective-permute-start(bf16[16,64,128]{2,1,0:T(8,128)(2,1)} %get-tuple-element.70), channel_id=1, source_target_pairs={{0,2},{1,3},{2,0},{3,1},{4,6},{5,7},{6,4},{7,5},{8,10},{9,11},{10,... | collective-permute-start | bytes 786440 | tf_op jit(solution)/shard_map/ppermute | solution.py:23
  220.7 7.8 %collective-permute-start.35 = (bf16[16,64,128]{2,1,0:T(8,128)(2,1)S(1)}, bf16[16,64,128]{2,1,0:T(8,128)(2,1)S(1)}, u32[]{:S(2)}, u32[]{:S(2)}) collective-permute-start(bf16[16,64,128]{2,1,0:T(8,128)(2,1)S(1)} %get-tuple-element.71), channel_id=1, source_target_pairs={{0,4},{1,5},{2,6},{3,7},{4,0},{5,1},{6,2},{7,3},{8,12},{9,13},{10,... | collective-permute-start | bytes 786440 | tf_op jit(solution)/shard_map/ppermute | solution.py:23
  231.8 5.6 %collective-permute-start.40 = (f32[64,64]{0,1:T(8,128)S(1)}, f32[64,64]{0,1:T(8,128)S(1)}, u32[]{:S(2)}, u32[]{:S(2)}) collective-permute-start(f32[64,64]{0,1:T(8,128)S(1)} %add.264), channel_id=1, source_target_pairs={{0,6},{1,7},{2,4},{3,5},{4,2},{5,3},{6,0},{7,1},{8,14},{9,15},{10,... | collective-permute-start | bytes 49160 | tf_op jit(solution)/shard_map/ppermute | solution.py:23
  233.4 6.3 %collective-permute-start.39 = (f32[64,64]{0,1:T(8,128)S(1)}, f32[64,64]{0,1:T(8,128)S(1)}, u32[]{:S(2)}, u32[]{:S(2)}) collective-permute-start(f32[64,64]{0,1:T(8,128)S(1)} %add.264), channel_id=1, source_target_pairs={{0,4},{1,5},{2,6},{3,7},{4,0},{5,1},{6,2},{7,3},{8,12},{9,13},{10,... | collective-permute-start | bytes 49160 | tf_op jit(solution)/shard_map/ppermute | solution.py:23
  234.5 5.2 %collective-permute-start.38 = (f32[64,64]{0,1:T(8,128)S(1)}, f32[64,64]{0,1:T(8,128)S(1)}, u32[]{:S(2)}, u32[]{:S(2)}) collective-permute-start(f32[64,64]{0,1:T(8,128)S(1)} %add.264), channel_id=1, source_target_pairs={{0,2},{1,3},{2,0},{3,1},{4,6},{5,7},{6,4},{7,5},{8,10},{9,11},{10,... | collective-permute-start | bytes 49160 | tf_op jit(solution)/shard_map/ppermute | solution.py:23
  235.3 28.1 %collective-permute-start.46 = (bf16[16,64,128]{2,1,0:T(8,128)(2,1)S(1)}, bf16[16,64,128]{2,1,0:T(8,128)(2,1)S(1)}, u32[]{:S(2)}, u32[]{:S(2)}) collective-permute-start(bf16[16,64,128]{2,1,0:T(8,128)(2,1)S(1)} %get-tuple-element.74.rest_0_), channel_id=1, source_target_pairs={{0,24},{8,16},{16,8},{24,0},{1,25},{9,17},{17,9},{25,1},{2,26},{10... | collective-permute-start | bytes 786440 | tf_op jit(solution)/shard_map/ppermute | solution.py:23
  237.4 26.0 %collective-permute-start.45 = (bf16[16,64,128]{2,1,0:T(8,128)(2,1)S(1)}, bf16[16,64,128]{2,1,0:T(8,128)(2,1)S(1)}, u32[]{:S(2)}, u32[]{:S(2)}) collective-permute-start(bf16[16,64,128]{2,1,0:T(8,128)(2,1)S(1)} %get-tuple-element.74.rest_0_), channel_id=1, source_target_pairs={{0,16},{8,24},{16,0},{24,8},{1,17},{9,25},{17,1},{25,9},{2,18},{10... | collective-permute-start | bytes 786440 | tf_op jit(solution)/shard_map/ppermute | solution.py:23
  237.4 26.0 %collective-permute-start.44 = (bf16[16,64,128]{2,1,0:T(8,128)(2,1)S(1)}, bf16[16,64,128]{2,1,0:T(8,128)(2,1)S(1)}, u32[]{:S(2)}, u32[]{:S(2)}) collective-permute-start(bf16[16,64,128]{2,1,0:T(8,128)(2,1)S(1)} %get-tuple-element.74.rest_0_), channel_id=1, source_target_pairs={{0,8},{8,0},{16,24},{24,16},{1,9},{9,1},{17,25},{25,17},{2,10},{10... | collective-permute-start | bytes 786440 | tf_op jit(solution)/shard_map/ppermute | solution.py:23
  239.7 17.4 %collective-permute-start.43 = (f32[64,64]{0,1:T(8,128)S(1)}, f32[64,64]{0,1:T(8,128)S(1)}, u32[]{:S(2)}, u32[]{:S(2)}) collective-permute-start(f32[64,64]{0,1:T(8,128)S(1)} %add_add_fusion.3), channel_id=1, source_target_pairs={{0,24},{8,16},{16,8},{24,0},{1,25},{9,17},{17,9},{25,1},{2,26},{10... | collective-permute-start | bytes 49160 | tf_op jit(solution)/shard_map/ppermute | solution.py:23
  241.9 19.6 %collective-permute-start.42 = (f32[64,64]{0,1:T(8,128)S(1)}, f32[64,64]{0,1:T(8,128)S(1)}, u32[]{:S(2)}, u32[]{:S(2)}) collective-permute-start(f32[64,64]{0,1:T(8,128)S(1)} %add_add_fusion.3), channel_id=1, source_target_pairs={{0,16},{8,24},{16,0},{24,8},{1,17},{9,25},{17,1},{25,9},{2,18},{10... | collective-permute-start | bytes 49160 | tf_op jit(solution)/shard_map/ppermute | solution.py:23
  257.1 6.2 %collective-permute-start.41 = (f32[64,64]{0,1:T(8,128)S(1)}, f32[64,64]{0,1:T(8,128)S(1)}, u32[]{:S(2)}, u32[]{:S(2)}) collective-permute-start(f32[64,64]{0,1:T(8,128)S(1)} %add_add_fusion.3), channel_id=1, source_target_pairs={{0,8},{8,0},{16,24},{24,16},{1,9},{9,1},{17,25},{25,17},{2,10},{10... | collective-permute-start | bytes 49160 | tf_op jit(solution)/shard_map/ppermute | solution.py:23
  278.5 17.2 %collective-permute-start.50 = (bf16[16,64,128]{2,1,0:T(8,128)(2,1)S(1)}, bf16[16,64,128]{2,1,0:T(8,128)(2,1)S(1)}, u32[]{:S(2)}, u32[]{:S(2)}) collective-permute-start(bf16[16,64,128]{2,1,0:T(8,128)(2,1)S(1)} %get-tuple-element.78), channel_id=1, source_target_pairs={{0,6},{1,7},{2,4},{3,5},{4,2},{5,3},{6,0},{7,1},{8,14},{9,15},{10,... | collective-permute-start | bytes 786440 | tf_op jit(solution)/shard_map/ppermute | solution.py:23
  286.7 8.3 %collective-permute-start.48 = (bf16[16,64,128]{2,1,0:T(8,128)(2,1)}, bf16[16,64,128]{2,1,0:T(8,128)(2,1)S(1)}, u32[]{:S(2)}, u32[]{:S(2)}) collective-permute-start(bf16[16,64,128]{2,1,0:T(8,128)(2,1)} %get-tuple-element.80), channel_id=1, source_target_pairs={{0,2},{1,3},{2,0},{3,1},{4,6},{5,7},{6,4},{7,5},{8,10},{9,11},{10,... | collective-permute-start | bytes 786440 | tf_op jit(solution)/shard_map/ppermute | solution.py:23
  287.9 7.8 %collective-permute-start.49 = (bf16[16,64,128]{2,1,0:T(8,128)(2,1)S(1)}, bf16[16,64,128]{2,1,0:T(8,128)(2,1)S(1)}, u32[]{:S(2)}, u32[]{:S(2)}) collective-permute-start(bf16[16,64,128]{2,1,0:T(8,128)(2,1)S(1)} %get-tuple-element.81), channel_id=1, source_target_pairs={{0,4},{1,5},{2,6},{3,7},{4,0},{5,1},{6,2},{7,3},{8,12},{9,13},{10,... | collective-permute-start | bytes 786440 | tf_op jit(solution)/shard_map/ppermute | solution.py:23
  299.8 4.8 %collective-permute-start.54 = (f32[64,64]{0,1:T(8,128)S(1)}, f32[64,64]{0,1:T(8,128)S(1)}, u32[]{:S(2)}, u32[]{:S(2)}) collective-permute-start(f32[64,64]{0,1:T(8,128)S(1)} %add.272), channel_id=1, source_target_pairs={{0,6},{1,7},{2,4},{3,5},{4,2},{5,3},{6,0},{7,1},{8,14},{9,15},{10,... | collective-permute-start | bytes 49160 | tf_op jit(solution)/shard_map/ppermute | solution.py:23
  305.9 5.8 %collective-permute-start.57 = (f32[64,64]{0,1:T(8,128)S(1)}, f32[64,64]{0,1:T(8,128)S(1)}, u32[]{:S(2)}, u32[]{:S(2)}) collective-permute-start(f32[64,64]{0,1:T(8,128)S(1)} %add_add_fusion.1), channel_id=1, source_target_pairs={{0,24},{8,16},{16,8},{24,0},{1,25},{9,17},{17,9},{25,1},{2,26},{10... | collective-permute-start | bytes 49160 | tf_op jit(solution)/shard_map/ppermute | solution.py:23
  307.7 4.8 %collective-permute-start.56 = (f32[64,64]{0,1:T(8,128)S(1)}, f32[64,64]{0,1:T(8,128)S(1)}, u32[]{:S(2)}, u32[]{:S(2)}) collective-permute-start(f32[64,64]{0,1:T(8,128)S(1)} %add_add_fusion.1), channel_id=1, source_target_pairs={{0,16},{8,24},{16,0},{24,8},{1,17},{9,25},{17,1},{25,9},{2,18},{10... | collective-permute-start | bytes 49160 | tf_op jit(solution)/shard_map/ppermute | solution.py:23
  (40 other events, 372.7 us)

commit v2 on v1

v2 whole, which is shorter than its diff:
```python
import functools

import jax
import jax.numpy as jnp
from jax import lax
from jax.experimental import pallas as pl
from jax.experimental.pallas import tpu as pltpu
from jax.sharding import PartitionSpec as P

ITERS = 3
CAP = 3
F32 = jnp.float32
BF16 = jnp.bfloat16
VMEM = pl.BlockSpec(memory_space=pltpu.VMEM)
SMEM = pl.BlockSpec(memory_space=pltpu.SMEM)
ANY = pl.BlockSpec(memory_space=pl.ANY)
LIMIT = 32 * 1024 * 1024
BIG = 60 * 1024 * 1024
NONE = pl.CostEstimate(flops=0, bytes_accessed=0, transcendentals=0)


def exchange(value, axis, distance):
    size = lax.axis_size(axis)
    return lax.ppermute(value, axis, [(i, i ^ distance) for i in range(size)])


def pack_kernel(devices, row_blocks, col_blocks, col_count, rows_in, cols_in, chg, slots, places, rows, cols, counts, sems):
    listed = chg.shape[0]
    loads = [pltpu.make_async_copy(rows_in, rows, sems.at[0]), pltpu.make_async_copy(cols_in, cols, sems.at[1])]
    for load in loads:
        load.start()

    def clear(i, carry):
        slots[i] = jnp.zeros(slots.shape[1:], slots.dtype)
        return carry

    lax.fori_loop(0, slots.shape[0], clear, 0, unroll=4)

    def reset(i, carry):
        counts[i] = 0
        for k in range(CAP):
            places[i * CAP + k] = 0
        return carry

    lax.fori_loop(0, devices, reset, 0, unroll=4)
    for load in loads:
        load.wait()

    def place(i, carry):
        row, col = cols[i], rows[i]
        owner = lax.div(row, row_blocks) * col_count + lax.div(col, col_blocks)
        rank = counts[owner]
        counts[owner] = rank + 1
        slot = owner * CAP + rank
        places[slot] = lax.rem(row, row_blocks) * col_blocks + lax.rem(col, col_blocks)
        pltpu.make_async_copy(chg.at[i], slots.at[slot], sems.at[2]).start()
        return carry

    lax.fori_loop(0, listed, place, 0, unroll=4)

    pltpu.make_async_copy(chg, slots.at[pl.ds(0, listed)], sems.at[2]).wait()


def degree_kernel(tile_rows, tiles, tiles_t, degree):
    degree[...] = jnp.zeros(degree.shape, F32)

    def own(i, carry):
        tile = tiles[i].T
        tiles_t[i] = tile
        degree[pl.ds(tile_rows[i], 1), :] += jnp.sum(jnp.abs(tile.astype(F32)), axis=0, keepdims=True)
        return carry

    lax.fori_loop(0, tiles.shape[0], own, 0, unroll=4)


def two_parts(value):
    high = value.astype(BF16)
    return high, (value - high.astype(F32)).astype(BF16)


def one_part(block, at, rows):
    return block[at : at + rows].astype(F32) + block[at + rows : at + 2 * rows].astype(F32)


def merge_kernel(row_size, sub, place, notes, *refs):
    outs = refs[-(refs[0].shape[1] // refs[-1].shape[2] // row_size) :]
    sources = refs[: len(refs) - len(outs)]
    features, tile = outs[0].shape[1:]
    groups = tile // sub
    member, family = place[0] % groups, place[0] // groups
    lane = lax.broadcasted_iota(jnp.int32, (features, tile), 1) // sub
    for distance, out in enumerate(outs):
        for r in range(row_size):
            block = r * len(outs) + jnp.bitwise_xor(family, distance)
            at = pl.ds(pl.multiple_of(block * tile, tile), tile)
            value = sources[0][:, at].astype(F32)
            for d in range(1, groups):
                g = jnp.bitwise_xor(member, d)
                moved = pltpu.roll(sources[d][:, at].astype(F32), (g - member) * sub % tile, 1)
                value = jnp.where(lane == g, moved, value)
            out[r] = value.astype(BF16)
        out[row_size] = jnp.zeros(out.shape[1:], BF16)
        out[row_size, : notes.shape[1], :] = notes[distance]


def product_kernel(by_column, first, sub, per_device, row_size, held, core, own_rows, own_x, taken_rows, taken_x, *rest):
    if first:
        own_degree, rest = rest[0], rest[1:]
    tiles_t, taken, rest = rest[0], rest[1], rest[2:]
    pieces, (keep, send), scratch = rest[:held], rest[held : held + 2], rest[held + 2 :]
    x_buf, own_buf, taken_buf, total, out_buf, degree, part_buf, x_sem, own_sem, taken_sem, out_sem = scratch
    tile = own_buf.shape[1]
    x_copies = [
        pltpu.make_async_copy(piece.at[pl.ds(0, per_device)], x_buf.at[pl.ds(i * per_device, per_device)], x_sem.at[i])
        for i, piece in enumerate(pieces)
    ]
    own_copy = pltpu.make_async_copy(tiles_t, own_buf, own_sem)
    taken_copy = pltpu.make_async_copy(taken, taken_buf, taken_sem)
    for copy in x_copies:
        copy.start()
    own_copy.start()
    taken_copy.start()

    def clear(i, carry):
        total[i] = jnp.zeros(total.shape[1:], F32)
        return carry

    lax.fori_loop(0, total.shape[0], clear, 0, unroll=8)
    if first:
        degree[...] = own_degree[...]
    for copy in x_copies:
        copy.wait()
    for copy, buf, rows, blocks in ((own_copy, own_buf, own_rows, own_x), (taken_copy, taken_buf, taken_rows, taken_x)):
        copy.wait()

        def add(i, carry, buf=buf, rows=rows, blocks=blocks):
            total[rows[i]] += jnp.dot(x_buf[blocks[i]], buf[i], preferred_element_type=F32)
            if first and buf is taken_buf:
                degree[pl.ds(rows[i], 1), :] += jnp.sum(jnp.abs(buf[i].astype(F32)), axis=0, keepdims=True)
            return carry

        lax.fori_loop(0, buf.shape[0], add, 0, unroll=8)
    half = out_buf.shape[1]
    groups = tile // sub
    if by_column:
        per_row = 2 * half // groups
        lane = lax.broadcasted_iota(jnp.int32, total.shape[1:], 1) // sub

        def regroup(r, carry):
            for part in range(per_row):
                for j in range(per_row):
                    base = j * groups * per_device + part + r * per_row
                    blocks = [total[base + g * per_device] for g in range(groups)]
                    for side in range(groups):
                        column = part * groups + side
                        value = blocks[0]
                        for g in range(groups):
                            shift = (g - side) * sub % tile
                            moved = pltpu.roll(blocks[g], shift, 1) if shift else blocks[g]
                            value = moved if g == 0 else jnp.where(lane == g, moved, value)
                        out_buf[column % 2, column // 2, r * per_row + j] = value.astype(BF16)
            return carry

        lax.fori_loop(0, row_size, regroup, 0)
    else:
        for chip in range(half):
            for side in range(2):

                def straight(i, carry, chip=chip, side=side):
                    out_buf[side, chip, i] = total[(2 * chip + side) * per_device + i].astype(BF16)
                    return carry

                lax.fori_loop(0, per_device, straight, 0, unroll=4)
    if first:
        per_row = 2 * half // groups
        lane = lax.broadcasted_iota(jnp.int32, (row_size, tile), 1) // sub
        for column in range(2 * half):
            part, side = column // groups, column % groups
            for j in range(per_row):
                value = None
                for g in range(groups):
                    block = degree[pl.ds((j * groups + g) * per_device + part, row_size, stride=per_row), :]
                    shift = (g - side) * sub % tile
                    moved = pltpu.roll(block, shift, 1) if shift else block
                    value = moved if g == 0 else jnp.where(lane == g, moved, value)
                part_buf[pl.ds(j, row_size, stride=per_row), :] = value
            by_node = degree[column * per_device : (column + 1) * per_device, :]
            values = two_parts(part_buf[...]) + two_parts(by_node)
            out_buf[column % 2, column // 2, per_device] = jnp.concatenate(values, axis=0)
    mine = core[0]
    keep_copy = pltpu.make_async_copy(out_buf.at[mine], keep, out_sem.at[0])
    send_copy = pltpu.make_async_copy(out_buf.at[1 - mine], send, out_sem.at[1])
    keep_copy.start()
    send_copy.start()
    keep_copy.wait()
    send_copy.wait()


def pair_kernel(per_device, chip, keep, other, *out):
    mine = chip[0]
    for i, piece in enumerate(out):
        there = jnp.bitwise_xor(mine, i + 1)

        def add(b, carry, piece=piece, there=there):
            piece[b] = (keep[there, b].astype(F32) + other[there, b].astype(F32)).astype(BF16)
            return carry

        lax.fori_loop(0, per_device, add, 0, unroll=4)
        if piece.shape[0] > per_device:
            here, sent = keep[there, per_device], other[there, per_device]
            values = []
            for at in (0, 2 * per_device):
                values += two_parts(one_part(here, at, per_device) + one_part(sent, at, per_device))
            piece[per_device] = jnp.concatenate(values, axis=0)


def scale_kernel(normalize, last, first, chip, keep, other, *rest):
    mine = chip[0]
    if first:
        received, (out, scaled, degrees) = rest[:-3], rest[-3:]
        per_device = out.shape[0]
        parts = [keep[mine, per_device], other[mine, per_device]] + [piece[per_device] for piece in received]
        for i in range(2):
            degrees[i] = 1.0 + sum(one_part(part, 2 * i * per_device, per_device) for part in parts)
        degree = degrees.at[0]
        gram = jnp.zeros((1, 1), F32)
    else:
        degrees, inverse, rest = rest[0], rest[1], rest[2:]
        received, (out, scaled) = rest[:-2], rest[-2:]
        degree = degrees.at[1 if last else 0]
        gram = jnp.zeros(inverse.shape, F32)

    def add(b, gram):
        total = keep[mine, b].astype(F32) + other[mine, b].astype(F32)
        for piece in received:
            total = total + piece[b].astype(F32)
        total = total / degree[pl.ds(b, 1), :]
        if normalize:
            total = jnp.dot(inverse[...], total, precision=lax.Precision.HIGHEST, preferred_element_type=F32)
        scaled[b] = total
        if last:
            return gram + lax.dot_general(
                total, total, (((1,), (1,)), ((), ())), precision=lax.Precision.HIGHEST, preferred_element_type=F32
            )
        out[b] = total.astype(BF16)
        return gram

    gram = lax.fori_loop(0, scaled.shape[0], add, gram, unroll=4)
    if last:
        out[...] = gram


def gram_kernel(scaled, gram):
    total = jnp.zeros(gram.shape, F32)
    for b in range(scaled.shape[0]):
        block = scaled[b]
        total = total + lax.dot_general(
            block, block, (((1,), (1,)), ((), ())), precision=lax.Precision.HIGHEST, preferred_element_type=F32
        )
    gram[...] = total


def inverse_factor(gram):
    size, step = gram.shape[0], 8
    row = lax.broadcasted_iota(jnp.int32, (size, size), 0)
    lane = lax.broadcasted_iota(jnp.int32, (size, size), 1)
    both = jnp.concatenate([gram, (row == lane).astype(F32)], axis=1)
    rows = [both[i : i + step] for i in range(0, size, step)]
    within = lax.broadcasted_iota(jnp.int32, rows[0].shape, 0)
    for p in range(len(rows)):
        cols = {
            i: [jnp.broadcast_to(rows[i][:, p * step + k : p * step + k + 1], rows[i].shape) for k in range(step)]
            for i in range(p, len(rows))
        }
        for k in range(step):
            pivot = [cols[p][l][k : k + 1] for l in range(step)]
            pivot_row = rows[p][k : k + 1]
            one = 1.0 / pivot[k]
            for i in range(p, len(rows)):
                scale = cols[i][k] * one
                if i == p:
                    scale = jnp.where(within > k, scale, 0.0)
                for l in range(k + 1, step):
                    cols[i][l] = cols[i][l] - scale * pivot[l]
                rows[i] = rows[i] - scale * pivot_row
    both = jnp.concatenate(rows, axis=0)
    pivots = jnp.sum(jnp.where(row == lane, both[:, :size], 0.0), axis=1, keepdims=True)
    return both[:, size:] * lax.rsqrt(pivots)


def factor_kernel(nodes, *refs):
    grams, inverse = refs[:-1], refs[-1]
    inverse[...] = inverse_factor(sum(g[...] for g in grams) / nodes)


def final_kernel(nodes, scaled, *refs):
    grams, out = refs[:-1], refs[-1]
    inverse = inverse_factor(sum(g[...] for g in grams) / nodes)
    tile = scaled.shape[2]
    for b in range(scaled.shape[0]):
        out[:, b * tile : (b + 1) * tile] = jnp.dot(
            inverse, scaled[b], precision=lax.Precision.HIGHEST, preferred_element_type=F32
        )


def params(limit=LIMIT):
    return pltpu.CompilerParams(vmem_limit_bytes=limit)


def plane_parts(gram):
    gram = gram + exchange(gram, "col", 1)
    return [gram] + [exchange(gram, "col", d) for d in range(2, lax.axis_size("col"), 2)]


def along_row(gram):
    return [gram] + [exchange(gram, "row", d) for d in range(1, lax.axis_size("row"))]


def after(value, *marks):
    return lax.optimization_barrier((value, *marks))[0]


def local(embed, tiles, tile_rows, tile_cols, chg_tiles, chg_rows, chg_cols):
    rows_dev, features = embed.shape
    tile = tiles.shape[1]
    row_size, col_size = lax.axis_size("row"), lax.axis_size("col")
    devices = row_size * col_size
    per_device = rows_dev // tile
    row_blocks, col_blocks = per_device * col_size, per_device * row_size
    sub = rows_dev // devices
    groups = tile // sub
    per_row = col_size // groups
    half = col_size // 2
    note_rows = -(-groups * row_size * CAP * 2 // (16 * tile)) * 16
    nodes = rows_dev * devices
    row, col = lax.axis_index("row"), lax.axis_index("col")
    core = (col % 2).reshape(1)
    chip = (col // 2).reshape(1)
    block = jax.ShapeDtypeStruct((per_device, features, tile), BF16)
    block32 = jax.ShapeDtypeStruct((per_device, features, tile), F32)

    slots, places = pl.pallas_call(
        functools.partial(pack_kernel, devices, row_blocks, col_blocks, col_size),
        out_shape=(
            jax.ShapeDtypeStruct((devices * CAP, tile, tile), BF16),
            jax.ShapeDtypeStruct((devices * CAP,), jnp.int32),
        ),
        in_specs=[ANY, ANY, ANY],
        out_specs=(VMEM, SMEM),
        scratch_shapes=[
            pltpu.SMEM(chg_rows.shape, jnp.int32),
            pltpu.SMEM(chg_rows.shape, jnp.int32),
            pltpu.SMEM((devices,), jnp.int32),
            pltpu.SemaphoreType.DMA((3,)),
        ],
        compiler_params=params(BIG),
        cost_estimate=NONE,
        name="pack",
    )(chg_rows, chg_cols, chg_tiles)
    member, family = col % groups, col // groups
    group_places = jnp.stack([places] + [exchange(places, "col", d) for d in range(1, groups)])
    group_places = group_places.reshape(groups, row_size, col_size, CAP)
    notes = []
    for d in range(per_row):
        there = lax.dynamic_index_in_dim(group_places, jnp.bitwise_xor(family, d) * groups + member, 2, False)
        there = jnp.stack([there // col_blocks, there % col_blocks], axis=-1).reshape(-1)
        notes.append(jnp.pad(there, (0, note_rows * tile - there.size)).reshape(note_rows, tile))
    notes = jnp.stack(notes).astype(BF16)
    embed_t = embed.T
    joined = pl.pallas_call(
        functools.partial(merge_kernel, row_size, sub),
        out_shape=(jax.ShapeDtypeStruct((row_size + 1, features, tile), BF16),) * per_row,
        in_specs=[SMEM] + [VMEM] * (1 + groups),
        out_specs=(VMEM,) * per_row,
        compiler_params=params(),
        cost_estimate=NONE,
        name="merge",
    )(col.reshape(1), notes, embed_t, *[exchange(embed_t, "col", d) for d in range(1, groups)])
    joined = [joined[0]] + [exchange(joined[d], "col", d * groups) for d in range(1, per_row)]
    notes = jnp.concatenate([piece[row_size, :note_rows] for piece in joined], axis=0)
    notes = jnp.pad(notes, ((0, -notes.shape[0] % features), (0, 0))).reshape(-1, features, tile)
    current = jnp.concatenate([piece[:row_size] for piece in joined] + [notes], axis=0)
    steps = [(current, current)]
    for d in range(1, row_size):
        left, right = steps[-1]
        steps.append((
            lax.ppermute(left, "row", [(i, i + 1) for i in range(row_size - 1)]),
            lax.ppermute(right, "row", [(i + 1, i) for i in range(row_size - 1)]),
        ))
    gathered = [current] + [piece for pair in steps[1:] for piece in pair]

    def slot_of(source):
        away = jnp.abs(source - row)
        return jnp.where(away == 0, 0, 2 * away - 1 + (source > row))

    taken = lax.all_to_all(
        slots.reshape(devices, CAP, tile, tile), ("row", "col"), split_axis=0, concat_axis=0, tiled=True
    ).reshape(devices * CAP, tile, tile)
    notes = jnp.stack([piece[per_device:] for piece in gathered])[slot_of(jnp.arange(row_size))]
    notes = notes.reshape(row_size, -1, tile)[:, : per_row * note_rows].reshape(row_size, per_row, note_rows * tile)
    notes = notes[:, :, : groups * row_size * CAP * 2].reshape(row_size, per_row, groups, row_size, CAP, 2)
    notes = lax.dynamic_index_in_dim(notes, row, 3, False).reshape(row_size, col_size, CAP, 2)
    notes = notes[:, jnp.bitwise_xor(jnp.arange(col_size), col)].reshape(devices * CAP, 2).astype(jnp.int32)

    def x_block(position, first):
        source = position % per_device // per_row
        outer, inner = position // per_device, position % per_row
        if first:
            return slot_of(source) * per_device + jnp.bitwise_xor(inner, family) * row_size + outer
        return jnp.bitwise_xor(source, row) * per_device + outer * per_row + inner

    own_rows, own_cols = tile_rows % row_blocks, tile_cols % col_blocks
    taken_rows, taken_cols = notes[:, 0], notes[:, 1]

    tiles_t, own_degree = pl.pallas_call(
        degree_kernel,
        out_shape=(
            jax.ShapeDtypeStruct(tiles.shape, BF16),
            jax.ShapeDtypeStruct((row_blocks, tile), F32),
        ),
        in_specs=[SMEM, VMEM],
        out_specs=(VMEM, VMEM),
        compiler_params=params(),
        cost_estimate=NONE,
        name="degree",
    )(after(own_rows, joined[0]), tiles)
    for iteration in range(ITERS):
        first, last = iteration == 0, iteration == ITERS - 1
        blocks = per_device + 1 if first else per_device
        shape = (blocks, features, tile)
        if iteration:
            gathered = [current] + [exchange(current, "row", d) for d in range(1, row_size)]
        keep, send = pl.pallas_call(
            functools.partial(product_kernel, not last, first, sub, per_device, row_size, len(gathered)),
            out_shape=(jax.ShapeDtypeStruct((half, *shape), BF16),) * 2,
            in_specs=[SMEM] * 5 + [VMEM] * first + [ANY] * (2 + len(gathered)),
            out_specs=(ANY, ANY),
            scratch_shapes=[
                pltpu.VMEM((len(gathered) * per_device, features, tile), BF16),
                pltpu.VMEM(tiles.shape, BF16),
                pltpu.VMEM((devices * CAP, tile, tile), BF16),
                pltpu.VMEM((row_blocks, features, tile), F32),
                pltpu.VMEM((2, half, *shape), BF16),
                pltpu.VMEM((row_blocks, tile), F32),
                pltpu.VMEM((per_device, tile), F32),
                pltpu.SemaphoreType.DMA((len(gathered),)),
                pltpu.SemaphoreType.DMA,
                pltpu.SemaphoreType.DMA,
                pltpu.SemaphoreType.DMA((2,)),
            ],
            compiler_params=params(BIG),
            cost_estimate=NONE,
            name="product",
        )(
            core, own_rows, x_block(own_cols, iteration == 0), taken_rows, x_block(taken_cols, iteration == 0),
            *([own_degree] if first else []), tiles_t, taken, *gathered,
        )
        other = exchange(send, "col", 1)
        if iteration:
            gram = pl.pallas_call(
                gram_kernel,
                out_shape=jax.ShapeDtypeStruct((features, features), F32),
                in_specs=[VMEM],
                out_specs=VMEM,
                compiler_params=params(),
                cost_estimate=NONE,
                name="gram",
            )(after(scaled, keep))
            grams = along_row(sum(plane_parts(gram)))
        paired = pl.pallas_call(
            functools.partial(pair_kernel, per_device),
            out_shape=(jax.ShapeDtypeStruct(shape, BF16),) * (half - 1),
            in_specs=[SMEM, VMEM, VMEM],
            out_specs=(VMEM,) * (half - 1),
            compiler_params=params(),
            cost_estimate=NONE,
            name="pair",
        )(chip, keep, other)
        received = [exchange(piece, "col", 2 * (i + 1)) for i, piece in enumerate(paired)]
        if iteration:
            inverse = pl.pallas_call(
                functools.partial(factor_kernel, nodes),
                out_shape=jax.ShapeDtypeStruct((features, features), F32),
                in_specs=[VMEM] * len(grams),
                out_specs=VMEM,
                compiler_params=params(),
                cost_estimate=NONE,
                name="factor",
            )(*grams)
        square = jax.ShapeDtypeStruct((features, features), F32)
        both = jax.ShapeDtypeStruct((2, per_device, tile), F32)
        current, scaled, *found = pl.pallas_call(
            functools.partial(scale_kernel, not first, last, first),
            out_shape=(square if last else block, block32) + ((both,) if first else ()),
            in_specs=[SMEM] + [VMEM] * ((2 if first else 4) + half - 1),
            out_specs=(VMEM,) * (3 if first else 2),
            compiler_params=params(),
            cost_estimate=NONE,
            name="scale",
        )(chip, keep, other, *([] if first else [degrees, inverse]), *received)
        if first:
            degrees = found[0]
    out = pl.pallas_call(
        functools.partial(final_kernel, nodes),
        out_shape=jax.ShapeDtypeStruct((features, rows_dev), F32),
        in_specs=[VMEM] * (1 + row_size),
        out_specs=VMEM,
        compiler_params=params(),
        cost_estimate=NONE,
        name="final",
    )(scaled, *along_row(sum(plane_parts(current))))
    return out.T


def solution(mesh):
    placed = (
        P(("row", "col"), None),
        P(("row", "col"), None, None),
        P(("row", "col")),
        P(("row", "col")),
        P(("row", "col"), None, None),
        P(("row", "col")),
        P(("row", "col")),
    )
    return jax.shard_map(
        local, mesh=mesh, in_specs=placed, out_specs=P(("row", "col"), None), check_vma=False
    )
```

time: 328 us -> 279 us (0.85)
  other arithmetic: 39.7 us -> 2.67 us
  waiting for transfers between devices: 143 us -> 126 us
  starting transfers between devices: 76.1 us -> 88 us
  local copies, waits for them, and re-layouts: 17.8 us -> 13 us
    ppermute x58 -> x44, waiting for transfers between devices: 143 us -> 97 us  [exchange(): return lax.ppermute(value, axis, [(i, i ^ distance) for i in range(size)])]
    ppermute x0 -> x6, starting transfers between devices: none -> 36.2 us  [the longest x3 32.4 us: local(): lax.ppermute(left, 'row', [(i, i + 1) for i in range(row_size - 1)])]
    another operation x15 -> x8, other arithmetic: 36.3 us -> 0.22 us  [the longest x1 0.11 us: local(): jnp.stack([places] + [exchange(places, 'col', d) for d in range(1, groups)])]
    ppermute x0 -> x6, waiting for transfers between devices: none -> 29.3 us  [the longest x3 17.3 us: local(): lax.ppermute(left, 'row', [(i, i + 1) for i in range(row_size - 1)])]
    ppermute x58 -> x44, starting transfers between devices: 68.7 us -> 44.7 us  [exchange(): return lax.ppermute(value, axis, [(i, i ^ distance) for i in range(size)])]
    pallas_call x10 -> x12, Pallas kernels: 33.8 us -> 39.9 us  [the longest x3 27.3 us: local(): pl.pallas_call(functools.partial(product_kernel, not last, first, sub, pe...]
    unnamed x61 -> x66, local copies, waits for them, and re-layouts: 14.8 us -> 8.87 us
    pallas_call x1, Pallas kernels: 7.01 us -> 2.18 us  [local(): pl.pallas_call(degree_kernel, out_shape=(jax.ShapeDtypeStruct(tiles.shape...]
  transfers between devices with their start and end apart: 59 -> 51, of which waited for: 37 -> 27; matrix products, arithmetic and copies ran while one was open for 9% -> 3% of each run, Pallas kernels for 2% -> 4%
where the time goes in v2:
time: 279 us
  waiting for transfers between devices  126 us (45%)
  starting transfers between devices  88 us (32%)
  Pallas kernels  47.9 us (17%)
  local copies, waits for them, and re-layouts  13 us (5%)
    ppermute x44, waiting for transfers between devices, exchange(): return lax.ppermute(value, axis, [(i, i ^ distance) for i in range(size)])  97 us
    ppermute x44, starting transfers between devices, exchange(): return lax.ppermute(value, axis, [(i, i ^ distance) for i in range(size)])  44.7 us
    ppermute x3, starting transfers between devices, local(): lax.ppermute(left, 'row', [(i, i + 1) for i in range(row_size - 1)])  32.4 us
    pallas_call x3, Pallas kernels, local(): pl.pallas_call(functools.partial(product_kernel, not last, first, sub, pe...  27.3 us
    ppermute x3, waiting for transfers between devices, local(): lax.ppermute(left, 'row', [(i, i + 1) for i in range(row_size - 1)])  17.3 us
    ppermute x3, waiting for transfers between devices, local(): lax.ppermute(right, 'row', [(i + 1, i) for i in range(row_size - 1)])  12 us
    unnamed x66, local copies, waits for them, and re-layouts  8.87 us
    all_to_all x1, starting transfers between devices, local(): lax.all_to_all(slots.reshape(devices, CAP, tile, tile), ('row', 'col'), s...  7.08 us
  transfers between devices with their start and end apart: 51, of which 27 were waited for; matrix products, arithmetic and copies ran while one was open for 3% of the time, Pallas kernels for 4%

profile of v2, /device:TPU:0, one launch (start us, length us, event | category | flops | bytes accessed | tf_op | source)
XLA Modules:
  0.0 278.7 jit_solution(13270905406691265114)
XLA Ops:
  0.5 3.8 %pack.1 = (bf16[96,128,128]{2,1,0:T(8,128)(2,1)}, s32[96]{0:T(128)}) custom-call(s32[48]{0:T(128)} %rows_in.1, s32[48]{0:T(128)} %cols_in.1, bf16[48,128,128]{2,1,0:T(8,128)(2,1)} %chg.1), custom_call_target="tpu_custom_call" | custom-call | tf_op jit(solution)/shard_map/pack/pallas_call | solution.py:342
  4.4 7.1 %all-to-all-start = ((bf16[32,3,128,128]{3,2,1,0:T(8,128)(2,1)}), bf16[32,3,128,128]{3,2,1,0:T(8,128)(2,1)}, u32[]{:S(2)}, u32[]{:S(2)}) async-start(bf16[32,3,128,128]{3,2,1,0:T(8,128)(2,1)} %bitcast.178), calls=%async_computation | async-start | bytes 6291456 | tf_op jit(solution)/shard_map/all_to_all | solution.py:396
  14.9 1.8 collective-permute-start.2
  16.6 1.5 collective-permute-start.3
  18.5 17.6 %collective-permute-done.2 = bf16[5,64,128]{2,1,0:T(8,128)(2,1)S(1)} collective-permute-done((bf16[5,64,128]{2,1,0:T(8,128)(2,1)S(1)}, bf16[5,64,128]{2,1,0:T(8,128)(2,1)S(1)}, u32[]{:S(2)}, u32[]{:S(2)}) %collective-permute-start.2) | collective-permute-done | bytes 81952 | tf_op jit(solution)/shard_map/ppermute | solution.py:24
  36.1 2.2 collective-permute-done.4
  39.6 4.6 %collective-permute-start.5 = (bf16[17,64,128]{2,1,0:T(8,128)(2,1)S(1)}, bf16[17,64,128]{2,1,0:T(8,128)(2,1)S(1)}, u32[]{:S(2)}, u32[]{:S(2)}) collective-permute-start(bf16[17,64,128]{2,1,0:T(8,128)(2,1)S(1)} %constant_dynamic-update-slice_fusion.rest_3_), channel_id=1, source_target_pairs={{0,8},{8,16},{16,24},{1,9},{9,17},{17,25},{2,10},{10,18},{18,26},{... | collective-permute-start | bytes 835592 | tf_op jit(solution)/shard_map/ppermute | solution.py:387
  44.2 2.2 degree.1
  48.4 7.6 %collective-permute-done.6.rest_5_ = bf16[17,64,128]{2,1,0:T(8,128)(2,1)S(1)} collective-permute-done((bf16[17,64,128]{2,1,0:T(8,128)(2,1)S(1)}, bf16[17,64,128]{2,1,0:T(8,128)(2,1)S(1)}, u32[]{:S(2)}, u32[]{:S(2)}) %collective-permute-start.6) | collective-permute-done | bytes 278560 | tf_op jit(solution)/shard_map/ppermute | solution.py:388
  57.3 12.7 %collective-permute-done.5.rest_4_ = bf16[17,64,128]{2,1,0:T(8,128)(2,1)S(1)} collective-permute-done((bf16[17,64,128]{2,1,0:T(8,128)(2,1)S(1)}, bf16[17,64,128]{2,1,0:T(8,128)(2,1)S(1)}, u32[]{:S(2)}, u32[]{:S(2)}) %collective-permute-start.5) | collective-permute-done | bytes 278560 | tf_op jit(solution)/shard_map/ppermute | solution.py:387
  70.0 23.1 %collective-permute-start.7 = (bf16[17,64,128]{2,1,0:T(8,128)(2,1)S(1)}, bf16[17,64,128]{2,1,0:T(8,128)(2,1)S(1)}, u32[]{:S(2)}, u32[]{:S(2)}) collective-permute-start(bf16[17,64,128]{2,1,0:T(8,128)(2,1)S(1)} %collective-permute-done.5.rest_4_), channel_id=1, source_target_pairs={{0,8},{8,16},{16,24},{1,9},{9,17},{17,25},{2,10},{10,18},{18,26},{... | collective-permute-start | bytes 835592 | tf_op jit(solution)/shard_map/ppermute | solution.py:387
  93.1 4.5 %collective-permute-done.8.rest_7_ = bf16[17,64,128]{2,1,0:T(8,128)(2,1)S(1)} collective-permute-done((bf16[17,64,128]{2,1,0:T(8,128)(2,1)S(1)}, bf16[17,64,128]{2,1,0:T(8,128)(2,1)S(1)}, u32[]{:S(2)}, u32[]{:S(2)}) %collective-permute-start.8) | collective-permute-done | bytes 278560 | tf_op jit(solution)/shard_map/ppermute | solution.py:388
  98.8 4.7 %collective-permute-start.9 = (bf16[17,64,128]{2,1,0:T(8,128)(2,1)S(1)}, bf16[17,64,128]{2,1,0:T(8,128)(2,1)S(1)}, u32[]{:S(2)}, u32[]{:S(2)}) collective-permute-start(bf16[17,64,128]{2,1,0:T(8,128)(2,1)S(1)} %collective-permute-done.7.rest_6_), channel_id=1, source_target_pairs={{0,8},{8,16},{16,24},{1,9},{9,17},{17,25},{2,10},{10,18},{18,26},{... | collective-permute-start | bytes 835592 | tf_op jit(solution)/shard_map/ppermute | solution.py:387
  103.6 4.6 %collective-permute-done.9.rest_8_ = bf16[17,64,128]{2,1,0:T(8,128)(2,1)S(1)} collective-permute-done((bf16[17,64,128]{2,1,0:T(8,128)(2,1)S(1)}, bf16[17,64,128]{2,1,0:T(8,128)(2,1)S(1)}, u32[]{:S(2)}, u32[]{:S(2)}) %collective-permute-start.9) | collective-permute-done | bytes 278560 | tf_op jit(solution)/shard_map/ppermute | solution.py:387
  111.4 9.7 %product.3 = (bf16[4,17,64,128]{3,2,1,0:T(8,128)(2,1)}, bf16[4,17,64,128]{3,2,1,0:T(8,128)(2,1)}) custom-call(s32[1]{0:T(128)} %bitcast.1.core, s32[64]{0:T(128)} %copy-done.11, s32[64]{0:T(128)} %get-tuple-element.75.own_x, s32[96]{0:T(128)} %slice_bitcast_fusion.10.taken_rows, s32[96]{0:T(128)} %get-tuple-element.71.taken_x, f32[128,128]{1,0:T(8,128)} %copy-done.10, ...), custom_call_target="tpu_custom_call" | custom-call | tf_op jit(solution)/shard_map/product/pallas_call | solution.py:433
  121.2 3.0 %collective-permute-done.11.other = bf16[4,17,64,128]{3,2,1,0:T(8,128)(2,1)S(1)} collective-permute-done((bf16[4,17,64,128]{3,2,1,0:T(8,128)(2,1)}, bf16[4,17,64,128]{3,2,1,0:T(8,128)(2,1)S(1)}, u32[]{:S(2)}, u32[]{:S(2)}) %collective-permute-start.11) | collective-permute-done | bytes 1114144 | tf_op jit(solution)/shard_map/ppermute | solution.py:24
  125.6 1.5 collective-permute-start.12
  127.1 1.4 collective-permute-start.13
  129.2 6.0 %collective-permute-done.12.rest_0_ = bf16[17,64,128]{2,1,0:T(8,128)(2,1)S(1)} collective-permute-done((bf16[17,64,128]{2,1,0:T(8,128)(2,1)S(1)}, bf16[17,64,128]{2,1,0:T(8,128)(2,1)S(1)}, u32[]{:S(2)}, u32[]{:S(2)}) %collective-permute-start.12) | collective-permute-done | bytes 278560 | tf_op jit(solution)/shard_map/ppermute | solution.py:24
  135.2 6.3 %collective-permute-done.13.rest_1_ = bf16[17,64,128]{2,1,0:T(8,128)(2,1)S(1)} collective-permute-done((bf16[17,64,128]{2,1,0:T(8,128)(2,1)S(1)}, bf16[17,64,128]{2,1,0:T(8,128)(2,1)S(1)}, u32[]{:S(2)}, u32[]{:S(2)}) %collective-permute-start.13) | collective-permute-done | bytes 278560 | tf_op jit(solution)/shard_map/ppermute | solution.py:24
  141.7 3.1 %collective-permute-start.17 = (bf16[16,64,128]{2,1,0:T(8,128)(2,1)S(1)}, bf16[16,64,128]{2,1,0:T(8,128)(2,1)S(1)}, u32[]{:S(2)}, u32[]{:S(2)}) collective-permute-start(bf16[16,64,128]{2,1,0:T(8,128)(2,1)S(1)} %get-tuple-element.52.rest_2_), channel_id=1, source_target_pairs={{0,24},{8,16},{16,8},{24,0},{1,25},{9,17},{17,9},{25,1},{2,26},{10... | collective-permute-start | bytes 786440 | tf_op jit(solution)/shard_map/ppermute | solution.py:24
  147.3 5.6 %collective-permute-done.17.rest_5_ = bf16[16,64,128]{2,1,0:T(8,128)(2,1)S(1)} collective-permute-done((bf16[16,64,128]{2,1,0:T(8,128)(2,1)S(1)}, bf16[16,64,128]{2,1,0:T(8,128)(2,1)S(1)}, u32[]{:S(2)}, u32[]{:S(2)}) %collective-permute-start.17) | collective-permute-done | bytes 262176 | tf_op jit(solution)/shard_map/ppermute | solution.py:24
  152.9 14.7 %collective-permute-done.16.rest_4_ = bf16[16,64,128]{2,1,0:T(8,128)(2,1)S(1)} collective-permute-done((bf16[16,64,128]{2,1,0:T(8,128)(2,1)S(1)}, bf16[16,64,128]{2,1,0:T(8,128)(2,1)S(1)}, u32[]{:S(2)}, u32[]{:S(2)}) %collective-permute-start.16) | collective-permute-done | bytes 262176 | tf_op jit(solution)/shard_map/ppermute | solution.py:24
  169.1 9.1 %product.4 = (bf16[4,16,64,128]{3,2,1,0:T(8,128)(2,1)}, bf16[4,16,64,128]{3,2,1,0:T(8,128)(2,1)}) custom-call(s32[1]{0:T(128)} %bitcast.1.core, s32[64]{0:T(128)} %copy-done.11, s32[64]{0:T(128)} %add_add_fusion.4.own_x, s32[96]{0:T(128)} %slice_bitcast_fusion.10.taken_rows, s32[96]{0:T(128)} %add_add_fusion.3.taken_x, bf16[64,128,128]{2,1,0:T(8,128)(2,1)} %copy-done, ...), custom_call_target="tpu_custom_call" | custom-call | tf_op jit(solution)/shard_map/product/pallas_call | solution.py:433
  181.0 1.5 collective-permute-start.22
  185.9 1.5 collective-permute-start.26
  189.5 2.5 collective-permute-start.25
  192.0 3.3 %collective-permute-done.25.refs_3_ = f32[64,64]{1,0:T(8,128)S(1)} collective-permute-done((f32[64,64]{1,0:T(8,128)S(1)}, f32[64,64]{1,0:T(8,128)S(1)}, u32[]{:S(2)}, u32[]{:S(2)}) %collective-permute-start.25) | collective-permute-done | bytes 16416 | tf_op jit(solution)/shard_map/ppermute | solution.py:24
  195.3 1.5 collective-permute-done.24.refs_2_
  196.8 2.4 collective-permute-done.23.refs_1_
  199.2 1.9 factor.2.rest_1_
  202.2 2.9 %collective-permute-start.31 = (bf16[16,64,128]{2,1,0:T(8,128)(2,1)S(1)}, bf16[16,64,128]{2,1,0:T(8,128)(2,1)S(1)}, u32[]{:S(2)}, u32[]{:S(2)}) collective-permute-start(bf16[16,64,128]{2,1,0:T(8,128)(2,1)S(1)} %get-tuple-element.61.rest_2_), channel_id=1, source_target_pairs={{0,24},{8,16},{16,8},{24,0},{1,25},{9,17},{17,9},{25,1},{2,26},{10... | collective-permute-start | bytes 786440 | tf_op jit(solution)/shard_map/ppermute | solution.py:24
  205.1 1.5 collective-permute-start.29
  206.7 6.7 %collective-permute-done.31.rest_5_ = bf16[16,64,128]{2,1,0:T(8,128)(2,1)S(1)} collective-permute-done((bf16[16,64,128]{2,1,0:T(8,128)(2,1)S(1)}, bf16[16,64,128]{2,1,0:T(8,128)(2,1)S(1)}, u32[]{:S(2)}, u32[]{:S(2)}) %collective-permute-start.31) | collective-permute-done | bytes 262176 | tf_op jit(solution)/shard_map/ppermute | solution.py:24
  213.3 10.6 %collective-permute-done.30.rest_4_ = bf16[16,64,128]{2,1,0:T(8,128)(2,1)S(1)} collective-permute-done((bf16[16,64,128]{2,1,0:T(8,128)(2,1)S(1)}, bf16[16,64,128]{2,1,0:T(8,128)(2,1)S(1)}, u32[]{:S(2)}, u32[]{:S(2)}) %collective-permute-start.30) | collective-permute-done | bytes 262176 | tf_op jit(solution)/shard_map/ppermute | solution.py:24
  225.4 8.5 %product.5 = (bf16[4,16,64,128]{3,2,1,0:T(8,128)(2,1)}, bf16[4,16,64,128]{3,2,1,0:T(8,128)(2,1)}) custom-call(s32[1]{0:T(128)} %bitcast.1.core, s32[64]{0:T(128)} %copy-done.11, s32[64]{0:T(128)} %add_add_fusion.4.own_x, s32[96]{0:T(128)} %slice_bitcast_fusion.10.taken_rows, s32[96]{0:T(128)} %add_add_fusion.3.taken_x, bf16[64,128,128]{2,1,0:T(8,128)(2,1)} %copy-done, ...), custom_call_target="tpu_custom_call" | custom-call | tf_op jit(solution)/shard_map/product/pallas_call | solution.py:433
  236.8 1.5 collective-permute-start.36
  241.7 1.5 collective-permute-start.40
  245.3 2.0 collective-permute-start.39
  247.3 3.7 %collective-permute-done.39.refs_3_ = f32[64,64]{1,0:T(8,128)S(1)} collective-permute-done((f32[64,64]{1,0:T(8,128)S(1)}, f32[64,64]{1,0:T(8,128)S(1)}, u32[]{:S(2)}, u32[]{:S(2)}) %collective-permute-start.39) | collective-permute-done | bytes 16416 | tf_op jit(solution)/shard_map/ppermute | solution.py:24
  252.2 2.8 %collective-permute-done.37.refs_1_ = f32[64,64]{1,0:T(8,128)S(1)} collective-permute-done((f32[64,64]{1,0:T(8,128)S(1)}, f32[64,64]{1,0:T(8,128)S(1)}, u32[]{:S(2)}, u32[]{:S(2)}) %collective-permute-start.37) | collective-permute-done | bytes 16416 | tf_op jit(solution)/shard_map/ppermute | solution.py:24
  255.0 1.9 factor.3.rest_1_
  256.9 3.5 %scale.5 = (f32[64,64]{1,0:T(8,128)S(1)}, f32[16,64,128]{2,1,0:T(8,128)S(1)}) custom-call(s32[1]{0:T(128)} %bitcast.chip, bf16[4,16,64,128]{3,2,1,0:T(8,128)(2,1)S(1)} %copy-done.3, bf16[4,16,64,128]{3,2,1,0:T(8,128)(2,1)S(1)} %collective-permute-done.32.other, f32[2,16,128]{2,1,0:T(8,128)S(1)} %get-tuple-element.55.rest_0_, f32[64,64]{1,0:T(8,128)S(1)} %factor.3.rest_1_, ...), custom_call_target="tpu_custom_call" | custom-call | tf_op jit(solution)/shard_map/scale/pallas_call | solution.py:492
  261.7 1.5 collective-permute-start.46
  268.5 2.1 collective-permute-start.49
  270.6 2.4 collective-permute-start.47
  273.0 1.5 collective-permute-done.49.refs_3_
  275.4 3.3 %final.1 = f32[64,2048]{1,0:T(8,128)} custom-call(f32[16,64,128]{2,1,0:T(8,128)S(1)} %get-tuple-element.69.scaled, f32[64,64]{1,0:T(8,128)S(1)} %add_add_fusion.refs_0_, f32[64,64]{1,0:T(8,128)S(1)} %collective-permute-done.47.refs_1_, f32[64,64]{1,0:T(8,128)S(1)} %collective-permute-done.48.refs_2_, f32[64,64]{1,0:T(8,128)S(1)} %collective-permute-done.49.refs_3_), custom_call_target="tpu_custom_call" | custom-call | tf_op jit(solution)/shard_map/final/pallas_call | solution.py:503
  (197 shorter events, 47.1 us)
Async XLA Ops:
  0.0 14.7 %collective-permute-start.1 = (bf16[64,2048]{1,0:T(8,128)(2,1)}, bf16[64,2048]{1,0:T(8,128)(2,1)S(1)}, u32[]{:S(2)}, u32[]{:S(2)}) collective-permute-start(bf16[64,2048]{1,0:T(8,128)(2,1)} %bitcast.176), channel_id=1, source_target_pairs={{0,1},{1,0},{2,3},{3,2},{4,5},{5,4},{6,7},{7,6},{8,9},{9,8},{10,11... | collective-permute-start | bytes 786440 | tf_op jit(solution)/shard_map/ppermute | solution.py:24
  4.4 106.9 %all-to-all-start = ((bf16[32,3,128,128]{3,2,1,0:T(8,128)(2,1)}), bf16[32,3,128,128]{3,2,1,0:T(8,128)(2,1)}, u32[]{:S(2)}, u32[]{:S(2)}) async-start(bf16[32,3,128,128]{3,2,1,0:T(8,128)(2,1)} %bitcast.178), calls=%async_computation | async-start | bytes 6291456 | tf_op jit(solution)/shard_map/all_to_all | solution.py:396
  14.9 21.2 %collective-permute-start.2 = (bf16[5,64,128]{2,1,0:T(8,128)(2,1)S(1)}, bf16[5,64,128]{2,1,0:T(8,128)(2,1)S(1)}, u32[]{:S(2)}, u32[]{:S(2)}) collective-permute-start(bf16[5,64,128]{2,1,0:T(8,128)(2,1)S(1)} %get-tuple-element.40), channel_id=1, source_target_pairs={{0,2},{1,3},{2,0},{3,1},{4,6},{5,7},{6,4},{7,5},{8,10},{9,11},{10,... | collective-permute-start | bytes 245768 | tf_op jit(solution)/shard_map/ppermute | solution.py:24
  16.6 19.4 %collective-permute-start.3 = (bf16[5,64,128]{2,1,0:T(8,128)(2,1)S(1)}, bf16[5,64,128]{2,1,0:T(8,128)(2,1)S(1)}, u32[]{:S(2)}, u32[]{:S(2)}) collective-permute-start(bf16[5,64,128]{2,1,0:T(8,128)(2,1)S(1)} %get-tuple-element.41), channel_id=1, source_target_pairs={{0,4},{1,5},{2,6},{3,7},{4,0},{5,1},{6,2},{7,3},{8,12},{9,13},{10,... | collective-permute-start | bytes 245768 | tf_op jit(solution)/shard_map/ppermute | solution.py:24
  18.2 20.1 %collective-permute-start.4 = (bf16[5,64,128]{2,1,0:T(8,128)(2,1)S(1)}, bf16[5,64,128]{2,1,0:T(8,128)(2,1)S(1)}, u32[]{:S(2)}, u32[]{:S(2)}) collective-permute-start(bf16[5,64,128]{2,1,0:T(8,128)(2,1)S(1)} %get-tuple-element.42), channel_id=1, source_target_pairs={{0,6},{1,7},{2,4},{3,5},{4,2},{5,3},{6,0},{7,1},{8,14},{9,15},{10,... | collective-permute-start | bytes 245768 | tf_op jit(solution)/shard_map/ppermute | solution.py:24
  38.3 17.7 %collective-permute-start.6 = (bf16[17,64,128]{2,1,0:T(8,128)(2,1)S(1)}, bf16[17,64,128]{2,1,0:T(8,128)(2,1)S(1)}, u32[]{:S(2)}, u32[]{:S(2)}) collective-permute-start(bf16[17,64,128]{2,1,0:T(8,128)(2,1)S(1)} %constant_dynamic-update-slice_fusion.rest_3_), channel_id=1, source_target_pairs={{8,0},{16,8},{24,16},{9,1},{17,9},{25,17},{10,2},{18,10},{26,18},{... | collective-permute-start | bytes 835592 | tf_op jit(solution)/shard_map/ppermute | solution.py:388
  39.6 30.3 %collective-permute-start.5 = (bf16[17,64,128]{2,1,0:T(8,128)(2,1)S(1)}, bf16[17,64,128]{2,1,0:T(8,128)(2,1)S(1)}, u32[]{:S(2)}, u32[]{:S(2)}) collective-permute-start(bf16[17,64,128]{2,1,0:T(8,128)(2,1)S(1)} %constant_dynamic-update-slice_fusion.rest_3_), channel_id=1, source_target_pairs={{0,8},{8,16},{16,24},{1,9},{9,17},{17,25},{2,10},{10,18},{18,26},{... | collective-permute-start | bytes 835592 | tf_op jit(solution)/shard_map/ppermute | solution.py:387
  56.0 41.5 %collective-permute-start.8 = (bf16[17,64,128]{2,1,0:T(8,128)(2,1)S(1)}, bf16[17,64,128]{2,1,0:T(8,128)(2,1)S(1)}, u32[]{:S(2)}, u32[]{:S(2)}) collective-permute-start(bf16[17,64,128]{2,1,0:T(8,128)(2,1)S(1)} %collective-permute-done.6.rest_5_), channel_id=1, source_target_pairs={{8,0},{16,8},{24,16},{9,1},{17,9},{25,17},{10,2},{18,10},{26,18},{... | collective-permute-start | bytes 835592 | tf_op jit(solution)/shard_map/ppermute | solution.py:388
  70.0 28.9 %collective-permute-start.7 = (bf16[17,64,128]{2,1,0:T(8,128)(2,1)S(1)}, bf16[17,64,128]{2,1,0:T(8,128)(2,1)S(1)}, u32[]{:S(2)}, u32[]{:S(2)}) collective-permute-start(bf16[17,64,128]{2,1,0:T(8,128)(2,1)S(1)} %collective-permute-done.5.rest_4_), channel_id=1, source_target_pairs={{0,8},{8,16},{16,24},{1,9},{9,17},{17,25},{2,10},{10,18},{18,26},{... | collective-permute-start | bytes 835592 | tf_op jit(solution)/shard_map/ppermute | solution.py:387
  97.5 10.7 %collective-permute-start.10 = (bf16[17,64,128]{2,1,0:T(8,128)(2,1)S(1)}, bf16[17,64,128]{2,1,0:T(8,128)(2,1)S(1)}, u32[]{:S(2)}, u32[]{:S(2)}) collective-permute-start(bf16[17,64,128]{2,1,0:T(8,128)(2,1)S(1)} %collective-permute-done.8.rest_7_), channel_id=1, source_target_pairs={{8,0},{16,8},{24,16},{9,1},{17,9},{25,17},{10,2},{18,10},{26,18},{... | collective-permute-start | bytes 835592 | tf_op jit(solution)/shard_map/ppermute | solution.py:388
  98.8 9.4 %collective-permute-start.9 = (bf16[17,64,128]{2,1,0:T(8,128)(2,1)S(1)}, bf16[17,64,128]{2,1,0:T(8,128)(2,1)S(1)}, u32[]{:S(2)}, u32[]{:S(2)}) collective-permute-start(bf16[17,64,128]{2,1,0:T(8,128)(2,1)S(1)} %collective-permute-done.7.rest_6_), channel_id=1, source_target_pairs={{0,8},{8,16},{16,24},{1,9},{9,17},{17,25},{2,10},{10,18},{18,26},{... | collective-permute-start | bytes 835592 | tf_op jit(solution)/shard_map/ppermute | solution.py:387
  121.1 3.0 %collective-permute-start.11 = (bf16[4,17,64,128]{3,2,1,0:T(8,128)(2,1)}, bf16[4,17,64,128]{3,2,1,0:T(8,128)(2,1)S(1)}, u32[]{:S(2)}, u32[]{:S(2)}) collective-permute-start(bf16[4,17,64,128]{3,2,1,0:T(8,128)(2,1)} %get-tuple-element.48), channel_id=1, source_target_pairs={{0,1},{1,0},{2,3},{3,2},{4,5},{5,4},{6,7},{7,6},{8,9},{9,8},{10,11... | collective-permute-start | bytes 3342344 | tf_op jit(solution)/shard_map/ppermute | solution.py:24
  125.6 9.6 %collective-permute-start.12 = (bf16[17,64,128]{2,1,0:T(8,128)(2,1)S(1)}, bf16[17,64,128]{2,1,0:T(8,128)(2,1)S(1)}, u32[]{:S(2)}, u32[]{:S(2)}) collective-permute-start(bf16[17,64,128]{2,1,0:T(8,128)(2,1)S(1)} %get-tuple-element.49), channel_id=1, source_target_pairs={{0,2},{1,3},{2,0},{3,1},{4,6},{5,7},{6,4},{7,5},{8,10},{9,11},{10,... | collective-permute-start | bytes 835592 | tf_op jit(solution)/shard_map/ppermute | solution.py:24
  127.1 14.4 %collective-permute-start.13 = (bf16[17,64,128]{2,1,0:T(8,128)(2,1)S(1)}, bf16[17,64,128]{2,1,0:T(8,128)(2,1)S(1)}, u32[]{:S(2)}, u32[]{:S(2)}) collective-permute-start(bf16[17,64,128]{2,1,0:T(8,128)(2,1)S(1)} %get-tuple-element.50), channel_id=1, source_target_pairs={{0,4},{1,5},{2,6},{3,7},{4,0},{5,1},{6,2},{7,3},{8,12},{9,13},{10,... | collective-permute-start | bytes 835592 | tf_op jit(solution)/shard_map/ppermute | solution.py:24
  128.5 13.0 %collective-permute-start.14 = (bf16[17,64,128]{2,1,0:T(8,128)(2,1)S(1)}, bf16[17,64,128]{2,1,0:T(8,128)(2,1)S(1)}, u32[]{:S(2)}, u32[]{:S(2)}) collective-permute-start(bf16[17,64,128]{2,1,0:T(8,128)(2,1)S(1)} %get-tuple-element.51), channel_id=1, source_target_pairs={{0,6},{1,7},{2,4},{3,5},{4,2},{5,3},{6,0},{7,1},{8,14},{9,15},{10,... | collective-permute-start | bytes 835592 | tf_op jit(solution)/shard_map/ppermute | solution.py:24
  141.7 11.2 %collective-permute-start.17 = (bf16[16,64,128]{2,1,0:T(8,128)(2,1)S(1)}, bf16[16,64,128]{2,1,0:T(8,128)(2,1)S(1)}, u32[]{:S(2)}, u32[]{:S(2)}) collective-permute-start(bf16[16,64,128]{2,1,0:T(8,128)(2,1)S(1)} %get-tuple-element.52.rest_2_), channel_id=1, source_target_pairs={{0,24},{8,16},{16,8},{24,0},{1,25},{9,17},{17,9},{25,1},{2,26},{10... | collective-permute-start | bytes 786440 | tf_op jit(solution)/shard_map/ppermute | solution.py:24
  144.8 22.8 %collective-permute-start.16 = (bf16[16,64,128]{2,1,0:T(8,128)(2,1)S(1)}, bf16[16,64,128]{2,1,0:T(8,128)(2,1)S(1)}, u32[]{:S(2)}, u32[]{:S(2)}) collective-permute-start(bf16[16,64,128]{2,1,0:T(8,128)(2,1)S(1)} %get-tuple-element.52.rest_2_), channel_id=1, source_target_pairs={{0,16},{8,24},{16,0},{24,8},{1,17},{9,25},{17,1},{25,9},{2,18},{10... | collective-permute-start | bytes 786440 | tf_op jit(solution)/shard_map/ppermute | solution.py:24
  145.7 22.0 %collective-permute-start.15 = (bf16[16,64,128]{2,1,0:T(8,128)(2,1)S(1)}, bf16[16,64,128]{2,1,0:T(8,128)(2,1)S(1)}, u32[]{:S(2)}, u32[]{:S(2)}) collective-permute-start(bf16[16,64,128]{2,1,0:T(8,128)(2,1)S(1)} %get-tuple-element.52.rest_2_), channel_id=1, source_target_pairs={{0,8},{8,0},{16,24},{24,16},{1,9},{9,1},{17,25},{25,17},{2,10},{10... | collective-permute-start | bytes 786440 | tf_op jit(solution)/shard_map/ppermute | solution.py:24
  178.2 6.3 %collective-permute-start.18 = (bf16[4,16,64,128]{3,2,1,0:T(8,128)(2,1)}, bf16[4,16,64,128]{3,2,1,0:T(8,128)(2,1)S(1)}, u32[]{:S(2)}, u32[]{:S(2)}) collective-permute-start(bf16[4,16,64,128]{3,2,1,0:T(8,128)(2,1)} %get-tuple-element.54), channel_id=1, source_target_pairs={{0,1},{1,0},{2,3},{3,2},{4,5},{5,4},{6,7},{7,6},{8,9},{9,8},{10,11... | collective-permute-start | bytes 3145736 | tf_op jit(solution)/shard_map/ppermute | solution.py:24
  181.0 7.1 %collective-permute-start.22 = (f32[64,64]{1,0:T(8,128)S(1)}, f32[64,64]{1,0:T(8,128)S(1)}, u32[]{:S(2)}, u32[]{:S(2)}) collective-permute-start(f32[64,64]{1,0:T(8,128)S(1)} %add.312), channel_id=1, source_target_pairs={{0,6},{1,7},{2,4},{3,5},{4,2},{5,3},{6,0},{7,1},{8,14},{9,15},{10,... | collective-permute-start | bytes 49160 | tf_op jit(solution)/shard_map/ppermute | solution.py:24
  182.5 7.0 %collective-permute-start.21 = (f32[64,64]{1,0:T(8,128)S(1)}, f32[64,64]{1,0:T(8,128)S(1)}, u32[]{:S(2)}, u32[]{:S(2)}) collective-permute-start(f32[64,64]{1,0:T(8,128)S(1)} %add.312), channel_id=1, source_target_pairs={{0,4},{1,5},{2,6},{3,7},{4,0},{5,1},{6,2},{7,3},{8,12},{9,13},{10,... | collective-permute-start | bytes 49160 | tf_op jit(solution)/shard_map/ppermute | solution.py:24
  183.9 5.6 %collective-permute-start.20 = (f32[64,64]{1,0:T(8,128)S(1)}, f32[64,64]{1,0:T(8,128)S(1)}, u32[]{:S(2)}, u32[]{:S(2)}) collective-permute-start(f32[64,64]{1,0:T(8,128)S(1)} %add.312), channel_id=1, source_target_pairs={{0,2},{1,3},{2,0},{3,1},{4,6},{5,7},{6,4},{7,5},{8,10},{9,11},{10,... | collective-permute-start | bytes 49160 | tf_op jit(solution)/shard_map/ppermute | solution.py:24
  185.9 15.2 %collective-permute-start.26 = (bf16[16,64,128]{2,1,0:T(8,128)(2,1)S(1)}, bf16[16,64,128]{2,1,0:T(8,128)(2,1)S(1)}, u32[]{:S(2)}, u32[]{:S(2)}) collective-permute-start(bf16[16,64,128]{2,1,0:T(8,128)(2,1)S(1)} %get-tuple-element.58), channel_id=1, source_target_pairs={{0,2},{1,3},{2,0},{3,1},{4,6},{5,7},{6,4},{7,5},{8,10},{9,11},{10,... | collective-permute-start | bytes 786440 | tf_op jit(solution)/shard_map/ppermute | solution.py:24
  187.4 13.7 %collective-permute-start.27 = (bf16[16,64,128]{2,1,0:T(8,128)(2,1)S(1)}, bf16[16,64,128]{2,1,0:T(8,128)(2,1)S(1)}, u32[]{:S(2)}, u32[]{:S(2)}) collective-permute-start(bf16[16,64,128]{2,1,0:T(8,128)(2,1)S(1)} %get-tuple-element.59), channel_id=1, source_target_pairs={{0,4},{1,5},{2,6},{3,7},{4,0},{5,1},{6,2},{7,3},{8,12},{9,13},{10,... | collective-permute-start | bytes 786440 | tf_op jit(solution)/shard_map/ppermute | solution.py:24
  188.1 13.0 %collective-permute-start.28 = (bf16[16,64,128]{2,1,0:T(8,128)(2,1)S(1)}, bf16[16,64,128]{2,1,0:T(8,128)(2,1)S(1)}, u32[]{:S(2)}, u32[]{:S(2)}) collective-permute-start(bf16[16,64,128]{2,1,0:T(8,128)(2,1)S(1)} %get-tuple-element.60), channel_id=1, source_target_pairs={{0,6},{1,7},{2,4},{3,5},{4,2},{5,3},{6,0},{7,1},{8,14},{9,15},{10,... | collective-permute-start | bytes 786440 | tf_op jit(solution)/shard_map/ppermute | solution.py:24
  189.5 5.8 %collective-permute-start.25 = (f32[64,64]{1,0:T(8,128)S(1)}, f32[64,64]{1,0:T(8,128)S(1)}, u32[]{:S(2)}, u32[]{:S(2)}) collective-permute-start(f32[64,64]{1,0:T(8,128)S(1)} %add_add_fusion.2.refs_0_), channel_id=1, source_target_pairs={{0,24},{8,16},{16,8},{24,0},{1,25},{9,17},{17,9},{25,1},{2,26},{10... | collective-permute-start | bytes 49160 | tf_op jit(solution)/shard_map/ppermute | solution.py:24
  192.0 4.8 %collective-permute-start.24 = (f32[64,64]{1,0:T(8,128)S(1)}, f32[64,64]{1,0:T(8,128)S(1)}, u32[]{:S(2)}, u32[]{:S(2)}) collective-permute-start(f32[64,64]{1,0:T(8,128)S(1)} %add_add_fusion.2.refs_0_), channel_id=1, source_target_pairs={{0,16},{8,24},{16,0},{24,8},{1,17},{9,25},{17,1},{25,9},{2,18},{10... | collective-permute-start | bytes 49160 | tf_op jit(solution)/shard_map/ppermute | solution.py:24
  195.3 3.9 %collective-permute-start.23 = (f32[64,64]{1,0:T(8,128)S(1)}, f32[64,64]{1,0:T(8,128)S(1)}, u32[]{:S(2)}, u32[]{:S(2)}) collective-permute-start(f32[64,64]{1,0:T(8,128)S(1)} %add_add_fusion.2.refs_0_), channel_id=1, source_target_pairs={{0,8},{8,0},{16,24},{24,16},{1,9},{9,1},{17,25},{25,17},{2,10},{10... | collective-permute-start | bytes 49160 | tf_op jit(solution)/shard_map/ppermute | solution.py:24
  202.2 11.1 %collective-permute-start.31 = (bf16[16,64,128]{2,1,0:T(8,128)(2,1)S(1)}, bf16[16,64,128]{2,1,0:T(8,128)(2,1)S(1)}, u32[]{:S(2)}, u32[]{:S(2)}) collective-permute-start(bf16[16,64,128]{2,1,0:T(8,128)(2,1)S(1)} %get-tuple-element.61.rest_2_), channel_id=1, source_target_pairs={{0,24},{8,16},{16,8},{24,0},{1,25},{9,17},{17,9},{25,1},{2,26},{10... | collective-permute-start | bytes 786440 | tf_op jit(solution)/shard_map/ppermute | solution.py:24
  205.1 18.8 %collective-permute-start.30 = (bf16[16,64,128]{2,1,0:T(8,128)(2,1)S(1)}, bf16[16,64,128]{2,1,0:T(8,128)(2,1)S(1)}, u32[]{:S(2)}, u32[]{:S(2)}) collective-permute-start(bf16[16,64,128]{2,1,0:T(8,128)(2,1)S(1)} %get-tuple-element.61.rest_2_), channel_id=1, source_target_pairs={{0,16},{8,24},{16,0},{24,8},{1,17},{9,25},{17,1},{25,9},{2,18},{10... | collective-permute-start | bytes 786440 | tf_op jit(solution)/shard_map/ppermute | solution.py:24
  205.1 18.8 %collective-permute-start.29 = (bf16[16,64,128]{2,1,0:T(8,128)(2,1)S(1)}, bf16[16,64,128]{2,1,0:T(8,128)(2,1)S(1)}, u32[]{:S(2)}, u32[]{:S(2)}) collective-permute-start(bf16[16,64,128]{2,1,0:T(8,128)(2,1)S(1)} %get-tuple-element.61.rest_2_), channel_id=1, source_target_pairs={{0,8},{8,0},{16,24},{24,16},{1,9},{9,1},{17,25},{25,17},{2,10},{10... | collective-permute-start | bytes 786440 | tf_op jit(solution)/shard_map/ppermute | solution.py:24
  234.0 6.3 %collective-permute-start.32 = (bf16[4,16,64,128]{3,2,1,0:T(8,128)(2,1)}, bf16[4,16,64,128]{3,2,1,0:T(8,128)(2,1)S(1)}, u32[]{:S(2)}, u32[]{:S(2)}) collective-permute-start(bf16[4,16,64,128]{3,2,1,0:T(8,128)(2,1)} %get-tuple-element.63), channel_id=1, source_target_pairs={{0,1},{1,0},{2,3},{3,2},{4,5},{5,4},{6,7},{7,6},{8,9},{9,8},{10,11... | collective-permute-start | bytes 3145736 | tf_op jit(solution)/shard_map/ppermute | solution.py:24
  235.0 1.8 collective-permute-start.33
  236.8 7.1 %collective-permute-start.36 = (f32[64,64]{1,0:T(8,128)S(1)}, f32[64,64]{1,0:T(8,128)S(1)}, u32[]{:S(2)}, u32[]{:S(2)}) collective-permute-start(f32[64,64]{1,0:T(8,128)S(1)} %add.316), channel_id=1, source_target_pairs={{0,6},{1,7},{2,4},{3,5},{4,2},{5,3},{6,0},{7,1},{8,14},{9,15},{10,... | collective-permute-start | bytes 49160 | tf_op jit(solution)/shard_map/ppermute | solution.py:24
  238.3 7.0 %collective-permute-start.35 = (f32[64,64]{1,0:T(8,128)S(1)}, f32[64,64]{1,0:T(8,128)S(1)}, u32[]{:S(2)}, u32[]{:S(2)}) collective-permute-start(f32[64,64]{1,0:T(8,128)S(1)} %add.316), channel_id=1, source_target_pairs={{0,4},{1,5},{2,6},{3,7},{4,0},{5,1},{6,2},{7,3},{8,12},{9,13},{10,... | collective-permute-start | bytes 49160 | tf_op jit(solution)/shard_map/ppermute | solution.py:24
  239.7 5.6 %collective-permute-start.34 = (f32[64,64]{1,0:T(8,128)S(1)}, f32[64,64]{1,0:T(8,128)S(1)}, u32[]{:S(2)}, u32[]{:S(2)}) collective-permute-start(f32[64,64]{1,0:T(8,128)S(1)} %add.316), channel_id=1, source_target_pairs={{0,2},{1,3},{2,0},{3,1},{4,6},{5,7},{6,4},{7,5},{8,10},{9,11},{10,... | collective-permute-start | bytes 49160 | tf_op jit(solution)/shard_map/ppermute | solution.py:24
  241.7 15.2 %collective-permute-start.40 = (bf16[16,64,128]{2,1,0:T(8,128)(2,1)S(1)}, bf16[16,64,128]{2,1,0:T(8,128)(2,1)S(1)}, u32[]{:S(2)}, u32[]{:S(2)}) collective-permute-start(bf16[16,64,128]{2,1,0:T(8,128)(2,1)S(1)} %get-tuple-element.66), channel_id=1, source_target_pairs={{0,2},{1,3},{2,0},{3,1},{4,6},{5,7},{6,4},{7,5},{8,10},{9,11},{10,... | collective-permute-start | bytes 786440 | tf_op jit(solution)/shard_map/ppermute | solution.py:24
  243.2 13.7 %collective-permute-start.41 = (bf16[16,64,128]{2,1,0:T(8,128)(2,1)S(1)}, bf16[16,64,128]{2,1,0:T(8,128)(2,1)S(1)}, u32[]{:S(2)}, u32[]{:S(2)}) collective-permute-start(bf16[16,64,128]{2,1,0:T(8,128)(2,1)S(1)} %get-tuple-element.67), channel_id=1, source_target_pairs={{0,4},{1,5},{2,6},{3,7},{4,0},{5,1},{6,2},{7,3},{8,12},{9,13},{10,... | collective-permute-start | bytes 786440 | tf_op jit(solution)/shard_map/ppermute | solution.py:24
  243.9 13.1 %collective-permute-start.42 = (bf16[16,64,128]{2,1,0:T(8,128)(2,1)S(1)}, bf16[16,64,128]{2,1,0:T(8,128)(2,1)S(1)}, u32[]{:S(2)}, u32[]{:S(2)}) collective-permute-start(bf16[16,64,128]{2,1,0:T(8,128)(2,1)S(1)} %get-tuple-element.68), channel_id=1, source_target_pairs={{0,6},{1,7},{2,4},{3,5},{4,2},{5,3},{6,0},{7,1},{8,14},{9,15},{10,... | collective-permute-start | bytes 786440 | tf_op jit(solution)/shard_map/ppermute | solution.py:24
  245.3 5.8 %collective-permute-start.39 = (f32[64,64]{1,0:T(8,128)S(1)}, f32[64,64]{1,0:T(8,128)S(1)}, u32[]{:S(2)}, u32[]{:S(2)}) collective-permute-start(f32[64,64]{1,0:T(8,128)S(1)} %add_add_fusion.1.refs_0_), channel_id=1, source_target_pairs={{0,24},{8,16},{16,8},{24,0},{1,25},{9,17},{17,9},{25,1},{2,26},{10... | collective-permute-start | bytes 49160 | tf_op jit(solution)/shard_map/ppermute | solution.py:24
  247.3 4.8 %collective-permute-start.38 = (f32[64,64]{1,0:T(8,128)S(1)}, f32[64,64]{1,0:T(8,128)S(1)}, u32[]{:S(2)}, u32[]{:S(2)}) collective-permute-start(f32[64,64]{1,0:T(8,128)S(1)} %add_add_fusion.1.refs_0_), channel_id=1, source_target_pairs={{0,16},{8,24},{16,0},{24,8},{1,17},{9,25},{17,1},{25,9},{2,18},{10... | collective-permute-start | bytes 49160 | tf_op jit(solution)/shard_map/ppermute | solution.py:24
  251.1 3.9 %collective-permute-start.37 = (f32[64,64]{1,0:T(8,128)S(1)}, f32[64,64]{1,0:T(8,128)S(1)}, u32[]{:S(2)}, u32[]{:S(2)}) collective-permute-start(f32[64,64]{1,0:T(8,128)S(1)} %add_add_fusion.1.refs_0_), channel_id=1, source_target_pairs={{0,8},{8,0},{16,24},{24,16},{1,9},{9,1},{17,25},{25,17},{2,10},{10... | collective-permute-start | bytes 49160 | tf_op jit(solution)/shard_map/ppermute | solution.py:24
  261.7 4.8 %collective-permute-start.46 = (f32[64,64]{1,0:T(8,128)S(1)}, f32[64,64]{1,0:T(8,128)S(1)}, u32[]{:S(2)}, u32[]{:S(2)}) collective-permute-start(f32[64,64]{1,0:T(8,128)S(1)} %add.320), channel_id=1, source_target_pairs={{0,6},{1,7},{2,4},{3,5},{4,2},{5,3},{6,0},{7,1},{8,14},{9,15},{10,... | collective-permute-start | bytes 49160 | tf_op jit(solution)/shard_map/ppermute | solution.py:24
  263.2 3.9 %collective-permute-start.45 = (f32[64,64]{1,0:T(8,128)S(1)}, f32[64,64]{1,0:T(8,128)S(1)}, u32[]{:S(2)}, u32[]{:S(2)}) collective-permute-start(f32[64,64]{1,0:T(8,128)S(1)} %add.320), channel_id=1, source_target_pairs={{0,4},{1,5},{2,6},{3,7},{4,0},{5,1},{6,2},{7,3},{8,12},{9,13},{10,... | collective-permute-start | bytes 49160 | tf_op jit(solution)/shard_map/ppermute | solution.py:24
  264.6 3.9 %collective-permute-start.44 = (f32[64,64]{1,0:T(8,128)S(1)}, f32[64,64]{1,0:T(8,128)S(1)}, u32[]{:S(2)}, u32[]{:S(2)}) collective-permute-start(f32[64,64]{1,0:T(8,128)S(1)} %add.320), channel_id=1, source_target_pairs={{0,2},{1,3},{2,0},{3,1},{4,6},{5,7},{6,4},{7,5},{8,10},{9,11},{10,... | collective-permute-start | bytes 49160 | tf_op jit(solution)/shard_map/ppermute | solution.py:24
  268.5 5.9 %collective-permute-start.49 = (f32[64,64]{1,0:T(8,128)S(1)}, f32[64,64]{1,0:T(8,128)S(1)}, u32[]{:S(2)}, u32[]{:S(2)}) collective-permute-start(f32[64,64]{1,0:T(8,128)S(1)} %add_add_fusion.refs_0_), channel_id=1, source_target_pairs={{0,24},{8,16},{16,8},{24,0},{1,25},{9,17},{17,9},{25,1},{2,26},{10... | collective-permute-start | bytes 49160 | tf_op jit(solution)/shard_map/ppermute | solution.py:24
  270.6 4.8 %collective-permute-start.48 = (f32[64,64]{1,0:T(8,128)S(1)}, f32[64,64]{1,0:T(8,128)S(1)}, u32[]{:S(2)}, u32[]{:S(2)}) collective-permute-start(f32[64,64]{1,0:T(8,128)S(1)} %add_add_fusion.refs_0_), channel_id=1, source_target_pairs={{0,16},{8,24},{16,0},{24,8},{1,17},{9,25},{17,1},{25,9},{2,18},{10... | collective-permute-start | bytes 49160 | tf_op jit(solution)/shard_map/ppermute | solution.py:24
  270.6 4.8 %collective-permute-start.47 = (f32[64,64]{1,0:T(8,128)S(1)}, f32[64,64]{1,0:T(8,128)S(1)}, u32[]{:S(2)}, u32[]{:S(2)}) collective-permute-start(f32[64,64]{1,0:T(8,128)S(1)} %add_add_fusion.refs_0_), channel_id=1, source_target_pairs={{0,8},{8,0},{16,24},{24,16},{1,9},{9,1},{17,25},{25,17},{2,10},{10... | collective-permute-start | bytes 49160 | tf_op jit(solution)/shard_map/ppermute | solution.py:24
  (31 other events, 488.3 us)

commit v3 on v2

v3 whole, which is shorter than its diff:
```python
import functools

import jax
import jax.numpy as jnp
from jax import lax
from jax.experimental import pallas as pl
from jax.experimental.pallas import tpu as pltpu
from jax.sharding import PartitionSpec as P

ITERS = 3
CAP = 3
F32 = jnp.float32
BF16 = jnp.bfloat16
VMEM = pl.BlockSpec(memory_space=pltpu.VMEM)
SMEM = pl.BlockSpec(memory_space=pltpu.SMEM)
ANY = pl.BlockSpec(memory_space=pl.ANY)
MIB = 1024 * 1024
LIMIT = 12 * MIB
BIG = 60 * MIB
NONE = pl.CostEstimate(flops=0, bytes_accessed=0, transcendentals=0)


def exchange(value, axis, distance):
    size = lax.axis_size(axis)
    return lax.ppermute(value, axis, [(i, i ^ distance) for i in range(size)])


def pack_kernel(devices, row_blocks, col_blocks, col_count, rows_in, cols_in, chg, slots, rows, cols, places, counts, sems):
    listed, tile = chg.shape[:2]
    loads = [pltpu.make_async_copy(rows_in, rows, sems.at[0]), pltpu.make_async_copy(cols_in, cols, sems.at[1])]
    for load in loads:
        load.start()

    def clear(i, carry):
        slots[i] = jnp.zeros(slots.shape[1:], slots.dtype)
        counts[i] = 0
        for k in range(2 * CAP):
            places[2 * CAP * i + k] = 0
        return carry

    lax.fori_loop(0, devices, clear, 0)
    for load in loads:
        load.wait()

    def place(i, carry):
        row, col = cols[i], rows[i]
        owner = lax.div(row, row_blocks) * col_count + lax.div(col, col_blocks)
        rank = counts[owner]
        counts[owner] = rank + 1
        at = 2 * (owner * CAP + rank)
        places[at] = lax.rem(row, row_blocks)
        places[at + 1] = lax.rem(col, col_blocks)
        there = pl.ds(pl.multiple_of(rank * tile, tile), tile)
        pltpu.make_async_copy(chg.at[i], slots.at[owner, there], sems.at[2]).start()
        return carry

    lax.fori_loop(0, listed, place, 0, unroll=4)
    pltpu.make_async_copy(chg, chg, sems.at[2]).wait()
    lane = lax.broadcasted_iota(jnp.int32, (16, tile), 1)

    def note(i, carry):
        value = jnp.zeros(lane.shape, jnp.int32)
        for k in range(2 * CAP):
            value = jnp.where(lane == k, places[2 * CAP * i + k], value)
        slots[i, CAP * tile :] = value.astype(F32).astype(BF16)
        return carry

    lax.fori_loop(0, devices, note, 0, unroll=2)


def stock_kernel(tile_rows, tiles, *refs):
    pieces, (stock, degree) = refs[:-2], refs[-2:]
    tile, count = tiles.shape[1], tiles.shape[0]
    features = stock.shape[1]
    per_tile = tile // features
    degree[...] = jnp.zeros(degree.shape, F32)

    def own(i, carry):
        value = tiles[i].T
        for k in range(per_tile):
            stock[i * per_tile + k] = value[k * features : (k + 1) * features]
        degree[pl.ds(tile_rows[i], 1), :] += jnp.sum(jnp.abs(value.astype(F32)), axis=0, keepdims=True)
        return carry

    lax.fori_loop(0, count, own, 0, unroll=4)
    at = count * per_tile
    for piece in pieces:
        stock[at : at + piece.shape[0]] = piece[...]
        at += piece.shape[0]
    high, low = two_parts(degree[...])
    for part in (high, low):
        for k in range(0, part.shape[0], features):
            stock[at] = part[k : k + features]
            at += 1


def two_parts(value):
    high = value.astype(BF16)
    return high, (value - high.astype(F32)).astype(BF16)


def one_part(block, at, rows):
    return block[at : at + rows].astype(F32) + block[at + rows : at + 2 * rows].astype(F32)


def merge_kernel(row_size, sub, place, *refs):
    features, tile = refs[-1].shape[1:]
    groups = tile // sub
    sources, outs = refs[: row_size * groups], refs[row_size * groups :]
    member, family = place[0] % groups, place[0] // groups
    lane = lax.broadcasted_iota(jnp.int32, (features, tile), 1) // sub
    for distance, out in enumerate(outs):
        for source in range(row_size):

            def join(r, carry, distance=distance, out=out, source=source):
                block = r * len(outs) + jnp.bitwise_xor(family, distance)
                at = pl.ds(pl.multiple_of(block * tile, tile), tile)
                value = sources[source * groups][:, at].astype(F32)
                for d in range(1, groups):
                    g = jnp.bitwise_xor(member, d)
                    moved = pltpu.roll(sources[source * groups + d][:, at].astype(F32), (g - member) * sub % tile, 1)
                    value = jnp.where(lane == g, moved, value)
                out[source * row_size + r] = value.astype(BF16)
                return carry

            lax.fori_loop(0, row_size, join, 0, unroll=4)


def product_kernel(by_column, first, sub, per_device, row_size, chips, held, place, own_rows, own_x, *rest):
    if not first:
        numbers, grams, rest = rest[0], rest[1 : 1 + chips], rest[1 + chips :]
    stock, taken, rest = rest[0], rest[1], rest[2:]
    pieces, outs, found, scratch = rest[:held], rest[held : held + 2], rest[held + 2], rest[held + 3 :]
    x_buf, total, degree, part_buf = scratch[:4]
    half, (features, tile) = outs[0].shape[0], stock.shape[1:]
    per_tile = tile // features
    tile_count = own_rows.shape[0]
    groups = tile // sub
    per_row = 2 * half // groups
    total[...] = jnp.zeros(total.shape, F32)
    if first:
        number_buf, numbers, sems = scratch[4:]
        x_start, x_blocks = tile_count * per_tile, per_device * row_size
        parts, rows = stock.shape[0] - (x_start + x_blocks), degree.shape[0]
        own_degree = stock[x_start + x_blocks :].reshape(parts * features, tile).astype(F32)
        degree[...] = own_degree[:rows] + own_degree[rows:]
        note = taken[:, CAP * tile :].astype(F32)[:, 0, :].astype(jnp.int32)
        lane = lax.broadcasted_iota(jnp.int32, note.shape, 1)
        per_row_bits, per_device_bits = per_row.bit_length() - 1, per_device.bit_length() - 1
        inner, outer = jnp.bitwise_and(note, per_row - 1), jnp.right_shift(note, per_device_bits)
        source = jnp.bitwise_xor(jnp.right_shift(jnp.bitwise_and(note, per_device - 1), per_row_bits), place[2])
        block = (jnp.bitwise_xor(inner, place[1]) * row_size + source) * row_size + outer
        even = jnp.bitwise_and(lane, 1) == 0
        number_buf[...] = jnp.where(even, note, block)
        found[...] = jnp.where(even, note, source * per_device + outer * per_row + inner)
        numbers_copy = pltpu.make_async_copy(number_buf, numbers, sems)
        numbers_copy.start()
    else:
        found[...] = sum(gram[...] for gram in grams)
        for i, piece in enumerate(pieces):
            x_buf[i * per_device : (i + 1) * per_device] = piece[...]

    def x_block(block):
        return stock[x_start + block] if first else x_buf[block]

    def add_own(i, carry):
        value = stock[pl.ds(i * per_tile, per_tile)].reshape(tile, tile)
        total[own_rows[i]] += jnp.dot(x_block(own_x[i]), value, preferred_element_type=F32)
        return carry

    lax.fori_loop(0, tile_count, add_own, 0, unroll=8)
    if first:
        numbers_copy.wait()

    def add_taken(i, carry):
        for k in range(CAP):
            row, block = numbers[i, 2 * k], numbers[i, 2 * k + 1]
            value = taken[i, k * tile : (k + 1) * tile]
            if first:
                degree[pl.ds(row, 1), :] += jnp.sum(jnp.abs(value.astype(F32)), axis=0, keepdims=True)
            total[row] += jnp.dot(x_block(block), value, preferred_element_type=F32)
        return carry

    lax.fori_loop(0, taken.shape[0], add_taken, 0, unroll=4)

    def write(mine):
        lane = lax.broadcasted_iota(jnp.int32, total.shape[1:], 1) // sub

        def regroup(r, carry):
            for part in range(per_row):
                for j in range(per_row):
                    base = j * groups * per_device + part + r * per_row
                    blocks = [total[base + g * per_device] for g in range(groups)]
                    for side in range(groups):
                        column = part * groups + side
                        value = blocks[0]
                        for g in range(groups):
                            shift = (g - side) * sub % tile
                            moved = pltpu.roll(blocks[g], shift, 1) if shift else blocks[g]
                            value = moved if g == 0 else jnp.where(lane == g, moved, value)
                        outs[(column + mine) % 2][column // 2, r * per_row + j] = value.astype(BF16)
            return carry

        def straight(i, carry):
            for column in range(2 * half):
                outs[(column + mine) % 2][column // 2, i] = total[column * per_device + i].astype(BF16)
            return carry

        if by_column:
            lax.fori_loop(0, row_size, regroup, 0)
        else:
            lax.fori_loop(0, per_device, straight, 0)
        if not first:
            return
        lane = lax.broadcasted_iota(jnp.int32, (row_size, tile), 1) // sub
        for column in range(2 * half):
            part, side = column // groups, column % groups
            for j in range(per_row):
                value = None
                for g in range(groups):
                    block = degree[pl.ds((j * groups + g) * per_device + part, row_size, stride=per_row), :]
                    shift = (g - side) * sub % tile
                    moved = pltpu.roll(block, shift, 1) if shift else block
                    value = moved if g == 0 else jnp.where(lane == g, moved, value)
                part_buf[pl.ds(j, row_size, stride=per_row), :] = value
            by_node = degree[column * per_device : (column + 1) * per_device, :]
            values = two_parts(part_buf[...]) + two_parts(by_node)
            outs[(column + mine) % 2][column // 2, per_device] = jnp.concatenate(values, axis=0)

    for mine in range(2):
        pl.when(place[0] == mine)(functools.partial(write, mine))


def pair_kernel(per_device, chip, keep, other, *out):
    for i, piece in enumerate(out):
        there = jnp.bitwise_xor(chip[0], (i + 1) % len(out))

        def add(b, carry, piece=piece, there=there):
            piece[b] = (keep[there, b].astype(F32) + other[there, b].astype(F32)).astype(piece.dtype)
            return carry

        lax.fori_loop(0, per_device, add, 0, unroll=4)
        if piece.shape[0] > per_device:
            here, sent = keep[there, per_device], other[there, per_device]
            for at in (0, 2 * per_device):
                value = one_part(here, at, per_device) + one_part(sent, at, per_device)
                high, low = two_parts(value)
                piece[per_device, at : at + per_device] = high.astype(piece.dtype)
                piece[per_device, at + per_device : at + 2 * per_device] = low.astype(piece.dtype)


def scale_kernel(normalize, last, first, own, *rest):
    if first:
        received, (out, scaled, degrees) = rest[:-3], rest[-3:]
        per_device = out.shape[0]
        parts = [own[per_device]] + [piece[per_device] for piece in received]
        for i in range(2):
            degrees[i] = 1.0 + sum(one_part(part, 2 * i * per_device, per_device) for part in parts)
        degree = degrees.at[0]
        gram = jnp.zeros((1, 1), F32)
    else:
        degrees, inverse, rest = rest[0], rest[1], rest[2:]
        received, (out, scaled) = rest[:-2], rest[-2:]
        degree = degrees.at[1 if last else 0]
        gram = jnp.zeros(inverse.shape, F32)

    def add(b, gram):
        total = own[b]
        for piece in received:
            total = total + piece[b].astype(F32)
        total = total / degree[pl.ds(b, 1), :]
        if normalize:
            total = jnp.dot(inverse[...], total, precision=lax.Precision.HIGHEST, preferred_element_type=F32)
        scaled[b] = total
        if last:
            return gram + lax.dot_general(
                total, total, (((1,), (1,)), ((), ())), precision=lax.Precision.HIGHEST, preferred_element_type=F32
            )
        out[b] = total.astype(BF16)
        return gram

    gram = lax.fori_loop(0, scaled.shape[0], add, gram, unroll=scaled.shape[0] if last else 4)
    if last:
        out[...] = gram


def gram_kernel(scaled, mark, gram):
    total = jnp.zeros(gram.shape, F32)
    for b in range(scaled.shape[0]):
        block = scaled[b]
        total = total + lax.dot_general(
            block, block, (((1,), (1,)), ((), ())), precision=lax.Precision.HIGHEST, preferred_element_type=F32
        )
    gram[...] = total


def inverse_factor(gram):
    size, step = gram.shape[0], 8
    row = lax.broadcasted_iota(jnp.int32, (size, size), 0)
    lane = lax.broadcasted_iota(jnp.int32, (size, size), 1)
    both = jnp.concatenate([gram, (row == lane).astype(F32)], axis=1)
    rows = [both[i : i + step] for i in range(0, size, step)]
    within = lax.broadcasted_iota(jnp.int32, rows[0].shape, 0)
    for p in range(len(rows)):
        cols = {
            i: [jnp.broadcast_to(rows[i][:, p * step + k : p * step + k + 1], rows[i].shape) for k in range(step)]
            for i in range(p, len(rows))
        }
        for k in range(step):
            pivot = [cols[p][l][k : k + 1] for l in range(step)]
            pivot_row = rows[p][k : k + 1]
            one = 1.0 / pivot[k]
            for i in range(p, len(rows)):
                scale = cols[i][k] * one
                if i == p:
                    scale = jnp.where(within > k, scale, 0.0)
                for l in range(k + 1, step):
                    cols[i][l] = cols[i][l] - scale * pivot[l]
                rows[i] = rows[i] - scale * pivot_row
    both = jnp.concatenate(rows, axis=0)
    pivots = jnp.sum(jnp.where(row == lane, both[:, :size], 0.0), axis=1, keepdims=True)
    return both[:, size:] * lax.rsqrt(pivots)


def factor_kernel(nodes, *refs):
    grams, inverse = refs[:-1], refs[-1]
    inverse[...] = inverse_factor(sum(g[...] for g in grams) / nodes)


def final_kernel(nodes, scaled, *refs):
    grams, out = refs[:-1], refs[-1]
    inverse = inverse_factor(sum(g[...] for g in grams) / nodes)
    tile = scaled.shape[2]
    for b in range(scaled.shape[0]):
        out[:, b * tile : (b + 1) * tile] = jnp.dot(
            inverse, scaled[b], precision=lax.Precision.HIGHEST, preferred_element_type=F32
        )


def params(limit=LIMIT):
    return pltpu.CompilerParams(vmem_limit_bytes=limit)


def chip_parts(gram):
    return [gram] + [exchange(gram, "col", d) for d in range(2, lax.axis_size("col"), 2)]


def along_row(gram):
    return [gram] + [exchange(gram, "row", d) for d in range(1, lax.axis_size("row"))]


def local(embed, tiles, tile_rows, tile_cols, chg_tiles, chg_rows, chg_cols):
    rows_dev, features = embed.shape
    tile = tiles.shape[1]
    row_size, col_size = lax.axis_size("row"), lax.axis_size("col")
    devices = row_size * col_size
    per_device = rows_dev // tile
    row_blocks, col_blocks = per_device * col_size, per_device * row_size
    sub = rows_dev // devices
    groups = tile // sub
    per_row = col_size // groups
    half = col_size // 2
    product_limit = 2 * (tiles.size + 3 * devices * CAP * tile * tile // 2 + 8 * row_blocks * features * tile) + 6 * MIB
    nodes = rows_dev * devices
    row, col = lax.axis_index("row"), lax.axis_index("col")
    chip = (col // 2).reshape(1)
    block = jax.ShapeDtypeStruct((per_device, features, tile), BF16)
    block32 = jax.ShapeDtypeStruct((per_device, features, tile), F32)

    member, family = col % groups, col // groups
    embed_t = embed.T
    raw = [embed_t] + [exchange(embed_t, "row", d) for d in range(1, row_size)]
    slots = pl.pallas_call(
        functools.partial(pack_kernel, devices, row_blocks, col_blocks, col_size),
        out_shape=jax.ShapeDtypeStruct((devices, CAP * tile + 16, tile), BF16),
        in_specs=[ANY, ANY, ANY],
        out_specs=VMEM,
        scratch_shapes=[
            pltpu.SMEM(chg_rows.shape, jnp.int32),
            pltpu.SMEM(chg_rows.shape, jnp.int32),
            pltpu.SMEM((devices * CAP * 2,), jnp.int32),
            pltpu.SMEM((devices,), jnp.int32),
            pltpu.SemaphoreType.DMA((3,)),
        ],
        compiler_params=params(BIG),
        cost_estimate=NONE,
        name="pack",
    )(chg_rows, chg_cols, chg_tiles)
    gathered = pl.pallas_call(
        functools.partial(merge_kernel, row_size, sub),
        out_shape=(jax.ShapeDtypeStruct((row_size * row_size, features, tile), BF16),) * per_row,
        in_specs=[SMEM] + [VMEM] * (row_size * groups),
        out_specs=(VMEM,) * per_row,
        compiler_params=params(2 * rows_dev * features * row_size * (groups + row_size) + 8 * MIB),
        cost_estimate=NONE,
        name="merge",
    )(
        col.reshape(1),
        *[piece if d == 0 else exchange(piece, "col", d) for piece in raw for d in range(groups)],
    )
    gathered = [gathered[0]] + [exchange(gathered[d], "col", d * groups) for d in range(1, per_row)]
    slots = lax.optimization_barrier((slots, *raw[1:]))[0]
    taken = lax.all_to_all(slots, ("row", "col"), split_axis=0, concat_axis=0, tiled=True)

    def x_block(position, first):
        source = position % per_device // per_row
        outer, inner = position // per_device, position % per_row
        if first:
            return (jnp.bitwise_xor(inner, family) * row_size + jnp.bitwise_xor(source, row)) * row_size + outer
        return jnp.bitwise_xor(source, row) * per_device + outer * per_row + inner

    own_rows, own_cols = tile_rows % row_blocks, tile_cols % col_blocks
    per_tile = tile // features
    stock_blocks = tiles.shape[0] * per_tile + col_blocks + 2 * row_blocks // features
    stock = pl.pallas_call(
        stock_kernel,
        out_shape=jax.ShapeDtypeStruct((stock_blocks, features, tile), BF16),
        in_specs=[SMEM] + [VMEM] * (1 + len(gathered)),
        out_specs=VMEM,
        scratch_shapes=[pltpu.VMEM((row_blocks, tile), F32)],
        compiler_params=params(4 * tiles.size + 4 * stock_blocks * features * tile + 4 * MIB),
        cost_estimate=NONE,
        name="stock",
    )(own_rows, tiles, *gathered)

    place = jnp.stack([col % 2, family, row])
    square = jax.ShapeDtypeStruct((features, features), F32)
    numbers_shape = jax.ShapeDtypeStruct((devices, tile), jnp.int32)
    for iteration in range(ITERS):
        first, last = iteration == 0, iteration == ITERS - 1
        blocks = per_device + 1 if first else per_device
        shape = (blocks, features, tile)
        if iteration:
            gathered = [current] + [exchange(current, "row", d) for d in range(1, row_size)]
            gram = pl.pallas_call(
                gram_kernel,
                out_shape=jax.ShapeDtypeStruct((features, features), F32),
                in_specs=[VMEM, VMEM],
                out_specs=VMEM,
                compiler_params=params(),
                cost_estimate=NONE,
                name="gram",
            )(scaled, gathered[1])
            grams = chip_parts(gram + exchange(gram, "col", 1))
        keep, send, found = pl.pallas_call(
            functools.partial(product_kernel, not last, first, sub, per_device, row_size, half, 0 if first else len(gathered)),
            out_shape=(jax.ShapeDtypeStruct((half, *shape), BF16),) * 2 + (numbers_shape if first else square,),
            in_specs=[SMEM] * 3 + ([VMEM] * 2 if first else [SMEM] + [VMEM] * (2 + half + row_size)),
            out_specs=(VMEM, VMEM, VMEM),
            scratch_shapes=[
                pltpu.VMEM((1 if first else col_blocks, features, tile), BF16),
                pltpu.VMEM((row_blocks, features, tile), F32),
                pltpu.VMEM((row_blocks, tile), F32),
                pltpu.VMEM((per_device, tile), F32),
            ] + first * [
                pltpu.VMEM((devices, tile), jnp.int32),
                pltpu.SMEM((devices, tile), jnp.int32),
                pltpu.SemaphoreType.DMA,
            ],
            compiler_params=params(product_limit),
            cost_estimate=NONE,
            name="product",
        )(
            place, own_rows, x_block(own_cols, first),
            *([] if first else [numbers, *grams]), stock, taken, *([] if first else gathered),
        )
        other = exchange(send, "col", 1)
        if iteration:
            grams = along_row(found)
        else:
            numbers = found
        paired = pl.pallas_call(
            functools.partial(pair_kernel, per_device),
            out_shape=(jax.ShapeDtypeStruct(shape, BF16),) * (half - 1) + (jax.ShapeDtypeStruct(shape, F32),),
            in_specs=[SMEM, VMEM, VMEM],
            out_specs=(VMEM,) * half,
            compiler_params=params(),
            cost_estimate=NONE,
            name="pair",
        )(chip, keep, other)
        received = [exchange(piece, "col", 2 * (i + 1)) for i, piece in enumerate(paired[:-1])]
        if iteration:
            inverse = pl.pallas_call(
                functools.partial(factor_kernel, nodes),
                out_shape=jax.ShapeDtypeStruct((features, features), F32),
                in_specs=[VMEM] * len(grams),
                out_specs=VMEM,
                compiler_params=params(),
                cost_estimate=NONE,
                name="factor",
            )(*grams)
        both = jax.ShapeDtypeStruct((2, per_device, tile), F32)
        current, scaled, *rest = pl.pallas_call(
            functools.partial(scale_kernel, not first, last, first),
            out_shape=(square if last else block, block32) + ((both,) if first else ()),
            in_specs=[VMEM] * ((1 if first else 3) + half - 1),
            out_specs=(VMEM,) * (3 if first else 2),
            compiler_params=params(),
            cost_estimate=NONE,
            name="scale",
        )(paired[-1], *([] if first else [degrees, inverse]), *received)
        if first:
            degrees = rest[0]
    out = pl.pallas_call(
        functools.partial(final_kernel, nodes),
        out_shape=jax.ShapeDtypeStruct((features, rows_dev), F32),
        in_specs=[VMEM] * (1 + row_size),
        out_specs=VMEM,
        compiler_params=params(),
        cost_estimate=NONE,
        name="final",
    )(scaled, *along_row(sum(chip_parts(current + exchange(current, "col", 1)))))
    return out.T


def solution(mesh):
    placed = (
        P(("row", "col"), None),
        P(("row", "col"), None, None),
        P(("row", "col")),
        P(("row", "col")),
        P(("row", "col"), None, None),
        P(("row", "col")),
        P(("row", "col")),
    )
    return jax.shard_map(
        local, mesh=mesh, in_specs=placed, out_specs=P(("row", "col"), None), check_vma=False
    )
```

time: 279 us -> 252 us (0.903)
  starting transfers between devices: 88 us -> 52 us
  waiting for transfers between devices: 126 us -> 158 us
  Pallas kernels: 47.9 us -> 38.4 us
  local copies, waits for them, and re-layouts: 13 us -> 3.63 us
    ppermute x6 -> x0, starting transfers between devices: 36.2 us -> none  [the longest x3 32.4 us: local(): lax.ppermute(left, 'row', [(i, i + 1) for i in range(row_size - 1)])]
    ppermute x44 -> x49, waiting for transfers between devices: 97 us -> 133 us  [exchange(): return lax.ppermute(value, axis, [(i, i ^ distance) for i in range(size)])]
    ppermute x6 -> x0, waiting for transfers between devices: 29.3 us -> none  [the longest x3 17.3 us: local(): lax.ppermute(left, 'row', [(i, i + 1) for i in range(row_size - 1)])]
    all_to_all x1, waiting for transfers between devices: 0.01 us -> 24.6 us  [local(): lax.all_to_all(slots, ('row', 'col'), split_axis=0, concat_axis=0, tiled=...]
    pallas_call x3, Pallas kernels: 27.3 us -> 16.4 us  [local(): pl.pallas_call(functools.partial(product_kernel, not last, first, sub, pe...]
    unnamed x66 -> x12, local copies, waits for them, and re-layouts: 8.87 us -> 3.63 us
    ppermute x44 -> x49, starting transfers between devices: 44.7 us -> 47.3 us  [exchange(): return lax.ppermute(value, axis, [(i, i ^ distance) for i in range(size)])]
  transfers between devices with their start and end apart: 51 -> 50, of which waited for: 27 -> 34; matrix products, arithmetic and copies ran while one was open for 3% -> 0% of each run, Pallas kernels for 4% -> 6%
where the time goes in v3:
time: 252 us
  waiting for transfers between devices  158 us (63%)
  starting transfers between devices  52 us (21%)
  Pallas kernels  38.4 us (15%)
  local copies, waits for them, and re-layouts  3.63 us (1%)
    ppermute x49, waiting for transfers between devices, exchange(): return lax.ppermute(value, axis, [(i, i ^ distance) for i in range(size)])  133 us
    ppermute x49, starting transfers between devices, exchange(): return lax.ppermute(value, axis, [(i, i ^ distance) for i in range(size)])  47.3 us
    all_to_all x1, waiting for transfers between devices, local(): lax.all_to_all(slots, ('row', 'col'), split_axis=0, concat_axis=0, tiled=...  24.6 us
    pallas_call x3, Pallas kernels, local(): pl.pallas_call(functools.partial(product_kernel, not last, first, sub, pe...  16.4 us
  transfers between devices with their start and end apart: 50, of which 34 were waited for; matrix products, arithmetic and copies ran while one was open for 0% of the time, Pallas kernels for 6%

profile of v3, /device:TPU:0, one launch (start us, length us, event | category | flops | bytes accessed | tf_op | source)
XLA Modules:
  0.0 252.0 jit_solution(2444065328050898683)
XLA Ops:
  0.0 5.0 %collective-permute-start.5 = (bf16[64,2048]{1,0:T(8,128)(2,1)}, bf16[64,2048]{1,0:T(8,128)(2,1)}, u32[]{:S(2)}, u32[]{:S(2)}) collective-permute-start(bf16[64,2048]{1,0:T(8,128)(2,1)} %bitcast.6), channel_id=1, source_target_pairs={{0,24},{8,16},{16,8},{24,0},{1,25},{9,17},{17,9},{25,1},{2,26},{10... | collective-permute-start | bytes 786440 | tf_op jit(solution)/shard_map/ppermute | solution.py:25
  5.6 4.1 %pack.1 = bf16[32,400,128]{2,1,0:T(8,128)(2,1)} custom-call(s32[48]{0:T(128)} %rows_in.1, s32[48]{0:T(128)} %cols_in.1, bf16[48,128,128]{2,1,0:T(8,128)(2,1)} %chg.1), custom_call_target="tpu_custom_call" | custom-call | tf_op jit(solution)/shard_map/pack/pallas_call | solution.py:373
  9.8 2.9 %collective-permute-done.5.refs_6_ = bf16[64,2048]{1,0:T(8,128)(2,1)} collective-permute-done((bf16[64,2048]{1,0:T(8,128)(2,1)}, bf16[64,2048]{1,0:T(8,128)(2,1)}, u32[]{:S(2)}, u32[]{:S(2)}) %collective-permute-start.5) | collective-permute-done | bytes 262176 | tf_op jit(solution)/shard_map/ppermute | solution.py:25
  12.6 15.0 %collective-permute-done.3.refs_4_ = bf16[64,2048]{1,0:T(8,128)(2,1)} collective-permute-done((bf16[64,2048]{1,0:T(8,128)(2,1)}, bf16[64,2048]{1,0:T(8,128)(2,1)}, u32[]{:S(2)}, u32[]{:S(2)}) %collective-permute-start.3) | collective-permute-done | bytes 262176 | tf_op jit(solution)/shard_map/ppermute | solution.py:25
  27.7 4.7 %all-to-all-start = ((bf16[32,400,128]{2,1,0:T(8,128)(2,1)}), bf16[32,400,128]{2,1,0:T(8,128)(2,1)S(1)}, u32[]{:S(2)}, u32[]{:S(2)}) async-start(bf16[32,400,128]{2,1,0:T(8,128)(2,1)} %pack.1), calls=%async_computation | async-start | bytes 6553600 | tf_op jit(solution)/shard_map/all_to_all | solution.py:403
  35.5 2.0 merge.1
  37.5 1.8 collective-permute-start.7
  39.4 1.5 collective-permute-start.8
  41.2 21.0 %collective-permute-done.7.refs_1_ = bf16[16,64,128]{2,1,0:T(8,128)(2,1)S(1)} collective-permute-done((bf16[16,64,128]{2,1,0:T(8,128)(2,1)S(1)}, bf16[16,64,128]{2,1,0:T(8,128)(2,1)S(1)}, u32[]{:S(2)}, u32[]{:S(2)}) %collective-permute-start.7) | collective-permute-done | bytes 262176 | tf_op jit(solution)/shard_map/ppermute | solution.py:25
  62.2 3.4 %collective-permute-done.8.refs_2_ = bf16[16,64,128]{2,1,0:T(8,128)(2,1)S(1)} collective-permute-done((bf16[16,64,128]{2,1,0:T(8,128)(2,1)S(1)}, bf16[16,64,128]{2,1,0:T(8,128)(2,1)S(1)}, u32[]{:S(2)}, u32[]{:S(2)}) %collective-permute-start.8) | collective-permute-done | bytes 262176 | tf_op jit(solution)/shard_map/ppermute | solution.py:25
  65.7 12.7 %collective-permute-done.9.refs_3_ = bf16[16,64,128]{2,1,0:T(8,128)(2,1)S(1)} collective-permute-done((bf16[16,64,128]{2,1,0:T(8,128)(2,1)S(1)}, bf16[16,64,128]{2,1,0:T(8,128)(2,1)S(1)}, u32[]{:S(2)}, u32[]{:S(2)}) %collective-permute-start.9) | collective-permute-done | bytes 262176 | tf_op jit(solution)/shard_map/ppermute | solution.py:25
  78.3 2.2 stock.1.rest_0_.rest_5_
  80.6 1.7 copy-done
  82.3 24.6 %all-to-all-done.rest_1_.rest_6_ = bf16[32,400,128]{2,1,0:T(8,128)(2,1)S(1)} async-done(((bf16[32,400,128]{2,1,0:T(8,128)(2,1)}), bf16[32,400,128]{2,1,0:T(8,128)(2,1)S(1)}, u32[]{:S(2)}, u32[]{:S(2)}) %all-to-all-start) | async-done | bytes 3276832 | tf_op jit(solution)/shard_map/all_to_all | solution.py:403
  106.9 1.9 copy-done.1
  108.8 5.6 %product.3 = (bf16[4,17,64,128]{3,2,1,0:T(8,128)(2,1)S(1)}, bf16[4,17,64,128]{3,2,1,0:T(8,128)(2,1)S(1)}, s32[32,128]{1,0:T(8,128)S(1)}) custom-call(s32[3]{0:T(128)S(1)} %pad_add_fusion.place, s32[64]{0:T(128)S(1)} %get-tuple-element.75.tile_rows.own_rows, s32[64]{0:T(128)S(1)} %get-tuple-element.71.own_x, bf16[196,64,128]{2,1,0:T(8,128)(2,1)S(1)} %copy-done.1, ...), custom_call_target="tpu_custom_call" | custom-call | tf_op jit(solution)/shard_map/product/pallas_call | solution.py:445
  114.4 2.7 %collective-permute-done.10.other = bf16[4,17,64,128]{3,2,1,0:T(8,128)(2,1)S(1)} collective-permute-done((bf16[4,17,64,128]{3,2,1,0:T(8,128)(2,1)S(1)}, bf16[4,17,64,128]{3,2,1,0:T(8,128)(2,1)S(1)}, u32[]{:S(2)}, u32[]{:S(2)}) %collective-permute-start.10) | collective-permute-done | bytes 1114144 | tf_op jit(solution)/shard_map/ppermute | solution.py:25
  118.6 1.6 collective-permute-start.12
  121.1 6.0 %collective-permute-done.11.rest_0_ = bf16[17,64,128]{2,1,0:T(8,128)(2,1)S(1)} collective-permute-done((bf16[17,64,128]{2,1,0:T(8,128)(2,1)S(1)}, bf16[17,64,128]{2,1,0:T(8,128)(2,1)S(1)}, u32[]{:S(2)}, u32[]{:S(2)}) %collective-permute-start.11) | collective-permute-done | bytes 278560 | tf_op jit(solution)/shard_map/ppermute | solution.py:25
  127.1 5.9 %collective-permute-done.12.rest_1_ = bf16[17,64,128]{2,1,0:T(8,128)(2,1)S(1)} collective-permute-done((bf16[17,64,128]{2,1,0:T(8,128)(2,1)S(1)}, bf16[17,64,128]{2,1,0:T(8,128)(2,1)S(1)}, u32[]{:S(2)}, u32[]{:S(2)}) %collective-permute-start.12) | collective-permute-done | bytes 278560 | tf_op jit(solution)/shard_map/ppermute | solution.py:25
  133.3 1.8 collective-permute-start.20
  135.0 1.7 collective-permute-start.19
  136.7 9.1 %collective-permute-done.14.mark.rest_8_ = bf16[16,64,128]{2,1,0:T(8,128)(2,1)S(1)} collective-permute-done((bf16[16,64,128]{2,1,0:T(8,128)(2,1)S(1)}, bf16[16,64,128]{2,1,0:T(8,128)(2,1)S(1)}, u32[]{:S(2)}, u32[]{:S(2)}) %collective-permute-start.14) | collective-permute-done | bytes 262176 | tf_op jit(solution)/shard_map/ppermute | solution.py:25
  149.0 1.7 collective-permute-start.17
  151.6 6.9 %collective-permute-done.19.rest_9_ = bf16[16,64,128]{2,1,0:T(8,128)(2,1)S(1)} collective-permute-done((bf16[16,64,128]{2,1,0:T(8,128)(2,1)S(1)}, bf16[16,64,128]{2,1,0:T(8,128)(2,1)S(1)}, u32[]{:S(2)}, u32[]{:S(2)}) %collective-permute-start.19) | collective-permute-done | bytes 262176 | tf_op jit(solution)/shard_map/ppermute | solution.py:25
  158.5 5.6 %product.4 = (bf16[4,16,64,128]{3,2,1,0:T(8,128)(2,1)S(1)}, bf16[4,16,64,128]{3,2,1,0:T(8,128)(2,1)S(1)}, f32[64,64]{1,0:T(8,128)S(1)}) custom-call(s32[3]{0:T(128)S(1)} %pad_add_fusion.place, s32[64]{0:T(128)S(1)} %get-tuple-element.75.tile_rows.own_rows, s32[64]{0:T(128)S(1)} %add_add_fusion.1.own_x, s32[32,128]{1,0:T(8,128)S(1)} %get-tuple-element.43.rest_0_, ...), custom_call_target="tpu_custom_call" | custom-call | tf_op jit(solution)/shard_map/product/pallas_call | solution.py:445
  164.2 2.6 %collective-permute-done.21.other = bf16[4,16,64,128]{3,2,1,0:T(8,128)(2,1)S(1)} collective-permute-done((bf16[4,16,64,128]{3,2,1,0:T(8,128)(2,1)S(1)}, bf16[4,16,64,128]{3,2,1,0:T(8,128)(2,1)S(1)}, u32[]{:S(2)}, u32[]{:S(2)}) %collective-permute-start.21) | collective-permute-done | bytes 1048608 | tf_op jit(solution)/shard_map/ppermute | solution.py:25
  167.2 1.6 collective-permute-start.25
  170.7 2.1 collective-permute-start.24
  172.8 3.6 %collective-permute-done.24.refs_3_ = f32[64,64]{1,0:T(8,128)S(1)} collective-permute-done((f32[64,64]{1,0:T(8,128)S(1)}, f32[64,64]{1,0:T(8,128)S(1)}, u32[]{:S(2)}, u32[]{:S(2)}) %collective-permute-start.24) | collective-permute-done | bytes 16416 | tf_op jit(solution)/shard_map/ppermute | solution.py:25
  177.7 2.6 %collective-permute-done.22.refs_1_ = f32[64,64]{1,0:T(8,128)S(1)} collective-permute-done((f32[64,64]{1,0:T(8,128)S(1)}, f32[64,64]{1,0:T(8,128)S(1)}, u32[]{:S(2)}, u32[]{:S(2)}) %collective-permute-start.22) | collective-permute-done | bytes 16416 | tf_op jit(solution)/shard_map/ppermute | solution.py:25
  180.3 1.9 factor.2.rest_1_
  183.6 1.9 collective-permute-start.34
  185.6 1.5 collective-permute-start.33
  187.1 8.0 %collective-permute-done.28.mark.rest_8_ = bf16[16,64,128]{2,1,0:T(8,128)(2,1)S(1)} collective-permute-done((bf16[16,64,128]{2,1,0:T(8,128)(2,1)S(1)}, bf16[16,64,128]{2,1,0:T(8,128)(2,1)S(1)}, u32[]{:S(2)}, u32[]{:S(2)}) %collective-permute-start.28) | collective-permute-done | bytes 262176 | tf_op jit(solution)/shard_map/ppermute | solution.py:25
  197.3 2.4 collective-permute-start.32
  200.8 7.6 %collective-permute-done.33.rest_9_ = bf16[16,64,128]{2,1,0:T(8,128)(2,1)S(1)} collective-permute-done((bf16[16,64,128]{2,1,0:T(8,128)(2,1)S(1)}, bf16[16,64,128]{2,1,0:T(8,128)(2,1)S(1)}, u32[]{:S(2)}, u32[]{:S(2)}) %collective-permute-start.33) | collective-permute-done | bytes 262176 | tf_op jit(solution)/shard_map/ppermute | solution.py:25
  208.4 5.2 %product.5 = (bf16[4,16,64,128]{3,2,1,0:T(8,128)(2,1)S(1)}, bf16[4,16,64,128]{3,2,1,0:T(8,128)(2,1)S(1)}, f32[64,64]{1,0:T(8,128)S(1)}) custom-call(s32[3]{0:T(128)S(1)} %pad_add_fusion.place, s32[64]{0:T(128)S(1)} %get-tuple-element.75.tile_rows.own_rows, s32[64]{0:T(128)S(1)} %add_add_fusion.1.own_x, s32[32,128]{1,0:T(8,128)S(1)} %get-tuple-element.43.rest_0_, ...), custom_call_target="tpu_custom_call" | custom-call | tf_op jit(solution)/shard_map/product/pallas_call | solution.py:445
  213.7 2.6 %collective-permute-done.35.other = bf16[4,16,64,128]{3,2,1,0:T(8,128)(2,1)S(1)} collective-permute-done((bf16[4,16,64,128]{3,2,1,0:T(8,128)(2,1)S(1)}, bf16[4,16,64,128]{3,2,1,0:T(8,128)(2,1)S(1)}, u32[]{:S(2)}, u32[]{:S(2)}) %collective-permute-start.35) | collective-permute-done | bytes 1048608 | tf_op jit(solution)/shard_map/ppermute | solution.py:25
  220.2 1.8 collective-permute-start.38
  222.1 3.9 %collective-permute-done.38.refs_3_ = f32[64,64]{1,0:T(8,128)S(1)} collective-permute-done((f32[64,64]{1,0:T(8,128)S(1)}, f32[64,64]{1,0:T(8,128)S(1)}, u32[]{:S(2)}, u32[]{:S(2)}) %collective-permute-start.38) | collective-permute-done | bytes 16416 | tf_op jit(solution)/shard_map/ppermute | solution.py:25
  226.9 3.0 %collective-permute-done.36.refs_1_ = f32[64,64]{1,0:T(8,128)S(1)} collective-permute-done((f32[64,64]{1,0:T(8,128)S(1)}, f32[64,64]{1,0:T(8,128)S(1)}, u32[]{:S(2)}, u32[]{:S(2)}) %collective-permute-start.36) | collective-permute-done | bytes 16416 | tf_op jit(solution)/shard_map/ppermute | solution.py:25
  229.9 1.9 factor.3.rest_1_
  231.8 2.5 %scale.5 = (f32[64,64]{1,0:T(8,128)S(1)}, f32[16,64,128]{2,1,0:T(8,128)S(1)}) custom-call(f32[16,64,128]{2,1,0:T(8,128)S(1)} %get-tuple-element.64.own, f32[2,16,128]{2,1,0:T(8,128)S(1)} %get-tuple-element.55.rest_0_, f32[64,64]{1,0:T(8,128)S(1)} %factor.3.rest_1_, bf16[16,64,128]{2,1,0:T(8,128)(2,1)S(1)} %collective-permute-done.39.rest_2_, ...), custom_call_target="tpu_custom_call" | custom-call | tf_op jit(solution)/shard_map/scale/pallas_call | solution.py:493
  235.6 1.9 collective-permute-start.45
  242.0 1.8 collective-permute-start.48
  243.8 2.7 %collective-permute-start.46 = (f32[64,64]{1,0:T(8,128)S(1)}, f32[64,64]{1,0:T(8,128)S(1)}, u32[]{:S(2)}, u32[]{:S(2)}) collective-permute-start(f32[64,64]{1,0:T(8,128)S(1)} %add_add_fusion.refs_0_), channel_id=1, source_target_pairs={{0,8},{8,0},{16,24},{24,16},{1,9},{9,1},{17,25},{25,17},{2,10},{10... | collective-permute-start | bytes 49160 | tf_op jit(solution)/shard_map/ppermute | solution.py:25
  248.7 3.3 %final.1 = f32[64,2048]{1,0:T(8,128)} custom-call(f32[16,64,128]{2,1,0:T(8,128)S(1)} %get-tuple-element.69.scaled, f32[64,64]{1,0:T(8,128)S(1)} %add_add_fusion.refs_0_, f32[64,64]{1,0:T(8,128)S(1)} %collective-permute-done.46.refs_1_, f32[64,64]{1,0:T(8,128)S(1)} %collective-permute-done.47.refs_2_, f32[64,64]{1,0:T(8,128)S(1)} %collective-permute-done.48.refs_3_), custom_call_target="tpu_custom_call" | custom-call | tf_op jit(solution)/shard_map/final/pallas_call | solution.py:504
  (88 shorter events, 31.8 us)
Async XLA Ops:
  0.0 12.6 %collective-permute-start.5 = (bf16[64,2048]{1,0:T(8,128)(2,1)}, bf16[64,2048]{1,0:T(8,128)(2,1)}, u32[]{:S(2)}, u32[]{:S(2)}) collective-permute-start(bf16[64,2048]{1,0:T(8,128)(2,1)} %bitcast.6), channel_id=1, source_target_pairs={{0,24},{8,16},{16,8},{24,0},{1,25},{9,17},{17,9},{25,1},{2,26},{10... | collective-permute-start | bytes 786440 | tf_op jit(solution)/shard_map/ppermute | solution.py:25
  5.0 22.6 %collective-permute-start.3 = (bf16[64,2048]{1,0:T(8,128)(2,1)}, bf16[64,2048]{1,0:T(8,128)(2,1)}, u32[]{:S(2)}, u32[]{:S(2)}) collective-permute-start(bf16[64,2048]{1,0:T(8,128)(2,1)} %bitcast.7), channel_id=1, source_target_pairs={{0,16},{8,24},{16,0},{24,8},{1,17},{9,25},{17,1},{25,9},{2,18},{10... | collective-permute-start | bytes 786440 | tf_op jit(solution)/shard_map/ppermute | solution.py:25
  5.1 22.6 %collective-permute-start.1 = (bf16[64,2048]{1,0:T(8,128)(2,1)}, bf16[64,2048]{1,0:T(8,128)(2,1)}, u32[]{:S(2)}, u32[]{:S(2)}) collective-permute-start(bf16[64,2048]{1,0:T(8,128)(2,1)} %bitcast.8), channel_id=1, source_target_pairs={{0,8},{8,0},{16,24},{24,16},{1,9},{9,1},{17,25},{25,17},{2,10},{10... | collective-permute-start | bytes 786440 | tf_op jit(solution)/shard_map/ppermute | solution.py:25
  27.7 79.2 %all-to-all-start = ((bf16[32,400,128]{2,1,0:T(8,128)(2,1)}), bf16[32,400,128]{2,1,0:T(8,128)(2,1)S(1)}, u32[]{:S(2)}, u32[]{:S(2)}) async-start(bf16[32,400,128]{2,1,0:T(8,128)(2,1)} %pack.1), calls=%async_computation | async-start | bytes 6553600 | tf_op jit(solution)/shard_map/all_to_all | solution.py:403
  32.4 1.7 collective-permute-start
  32.8 2.0 collective-permute-start.6
  33.0 2.1 collective-permute-start.4
  33.3 2.2 collective-permute-start.2
  37.5 24.7 %collective-permute-start.7 = (bf16[16,64,128]{2,1,0:T(8,128)(2,1)S(1)}, bf16[16,64,128]{2,1,0:T(8,128)(2,1)S(1)}, u32[]{:S(2)}, u32[]{:S(2)}) collective-permute-start(bf16[16,64,128]{2,1,0:T(8,128)(2,1)S(1)} %get-tuple-element.39), channel_id=1, source_target_pairs={{0,2},{1,3},{2,0},{3,1},{4,6},{5,7},{6,4},{7,5},{8,10},{9,11},{10,... | collective-permute-start | bytes 786440 | tf_op jit(solution)/shard_map/ppermute | solution.py:25
  39.4 26.3 %collective-permute-start.8 = (bf16[16,64,128]{2,1,0:T(8,128)(2,1)S(1)}, bf16[16,64,128]{2,1,0:T(8,128)(2,1)S(1)}, u32[]{:S(2)}, u32[]{:S(2)}) collective-permute-start(bf16[16,64,128]{2,1,0:T(8,128)(2,1)S(1)} %get-tuple-element.40), channel_id=1, source_target_pairs={{0,4},{1,5},{2,6},{3,7},{4,0},{5,1},{6,2},{7,3},{8,12},{9,13},{10,... | collective-permute-start | bytes 786440 | tf_op jit(solution)/shard_map/ppermute | solution.py:25
  40.8 37.5 %collective-permute-start.9 = (bf16[16,64,128]{2,1,0:T(8,128)(2,1)S(1)}, bf16[16,64,128]{2,1,0:T(8,128)(2,1)S(1)}, u32[]{:S(2)}, u32[]{:S(2)}) collective-permute-start(bf16[16,64,128]{2,1,0:T(8,128)(2,1)S(1)} %get-tuple-element.41), channel_id=1, source_target_pairs={{0,6},{1,7},{2,4},{3,5},{4,2},{5,3},{6,0},{7,1},{8,14},{9,15},{10,... | collective-permute-start | bytes 786440 | tf_op jit(solution)/shard_map/ppermute | solution.py:25
  114.4 2.8 %collective-permute-start.10 = (bf16[4,17,64,128]{3,2,1,0:T(8,128)(2,1)S(1)}, bf16[4,17,64,128]{3,2,1,0:T(8,128)(2,1)S(1)}, u32[]{:S(2)}, u32[]{:S(2)}) collective-permute-start(bf16[4,17,64,128]{3,2,1,0:T(8,128)(2,1)S(1)} %get-tuple-element.45), channel_id=1, source_target_pairs={{0,1},{1,0},{2,3},{3,2},{4,5},{5,4},{6,7},{7,6},{8,9},{9,8},{10,11... | collective-permute-start | bytes 3342344 | tf_op jit(solution)/shard_map/ppermute | solution.py:25
  117.5 9.6 %collective-permute-start.11 = (bf16[17,64,128]{2,1,0:T(8,128)(2,1)S(1)}, bf16[17,64,128]{2,1,0:T(8,128)(2,1)S(1)}, u32[]{:S(2)}, u32[]{:S(2)}) collective-permute-start(bf16[17,64,128]{2,1,0:T(8,128)(2,1)S(1)} %get-tuple-element.47), channel_id=1, source_target_pairs={{0,2},{1,3},{2,0},{3,1},{4,6},{5,7},{6,4},{7,5},{8,10},{9,11},{10,... | collective-permute-start | bytes 835592 | tf_op jit(solution)/shard_map/ppermute | solution.py:25
  118.6 14.4 %collective-permute-start.12 = (bf16[17,64,128]{2,1,0:T(8,128)(2,1)S(1)}, bf16[17,64,128]{2,1,0:T(8,128)(2,1)S(1)}, u32[]{:S(2)}, u32[]{:S(2)}) collective-permute-start(bf16[17,64,128]{2,1,0:T(8,128)(2,1)S(1)} %get-tuple-element.48), channel_id=1, source_target_pairs={{0,4},{1,5},{2,6},{3,7},{4,0},{5,1},{6,2},{7,3},{8,12},{9,13},{10,... | collective-permute-start | bytes 835592 | tf_op jit(solution)/shard_map/ppermute | solution.py:25
  120.2 12.8 %collective-permute-start.13 = (bf16[17,64,128]{2,1,0:T(8,128)(2,1)S(1)}, bf16[17,64,128]{2,1,0:T(8,128)(2,1)S(1)}, u32[]{:S(2)}, u32[]{:S(2)}) collective-permute-start(bf16[17,64,128]{2,1,0:T(8,128)(2,1)S(1)} %get-tuple-element.49), channel_id=1, source_target_pairs={{0,6},{1,7},{2,4},{3,5},{4,2},{5,3},{6,0},{7,1},{8,14},{9,15},{10,... | collective-permute-start | bytes 835592 | tf_op jit(solution)/shard_map/ppermute | solution.py:25
  133.2 12.7 %collective-permute-start.14 = (bf16[16,64,128]{2,1,0:T(8,128)(2,1)S(1)}, bf16[16,64,128]{2,1,0:T(8,128)(2,1)S(1)}, u32[]{:S(2)}, u32[]{:S(2)}) collective-permute-start(bf16[16,64,128]{2,1,0:T(8,128)(2,1)S(1)} %get-tuple-element.51.rest_7_), channel_id=1, source_target_pairs={{0,8},{8,0},{16,24},{24,16},{1,9},{9,1},{17,25},{25,17},{2,10},{10... | collective-permute-start | bytes 786440 | tf_op jit(solution)/shard_map/ppermute | solution.py:25
  133.3 18.3 %collective-permute-start.20 = (bf16[16,64,128]{2,1,0:T(8,128)(2,1)S(1)}, bf16[16,64,128]{2,1,0:T(8,128)(2,1)S(1)}, u32[]{:S(2)}, u32[]{:S(2)}) collective-permute-start(bf16[16,64,128]{2,1,0:T(8,128)(2,1)S(1)} %get-tuple-element.51.rest_7_), channel_id=1, source_target_pairs={{0,24},{8,16},{16,8},{24,0},{1,25},{9,17},{17,9},{25,1},{2,26},{10... | collective-permute-start | bytes 786440 | tf_op jit(solution)/shard_map/ppermute | solution.py:25
  135.0 23.4 %collective-permute-start.19 = (bf16[16,64,128]{2,1,0:T(8,128)(2,1)S(1)}, bf16[16,64,128]{2,1,0:T(8,128)(2,1)S(1)}, u32[]{:S(2)}, u32[]{:S(2)}) collective-permute-start(bf16[16,64,128]{2,1,0:T(8,128)(2,1)S(1)} %get-tuple-element.51.rest_7_), channel_id=1, source_target_pairs={{0,16},{8,24},{16,0},{24,8},{1,17},{9,25},{17,1},{25,9},{2,18},{10... | collective-permute-start | bytes 786440 | tf_op jit(solution)/shard_map/ppermute | solution.py:25
  146.8 1.3 collective-permute-start.15
  148.1 10.4 %collective-permute-start.18 = (f32[64,64]{1,0:T(8,128)S(1)}, f32[64,64]{1,0:T(8,128)S(1)}, u32[]{:S(2)}, u32[]{:S(2)}) collective-permute-start(f32[64,64]{1,0:T(8,128)S(1)} %add.74.rest_1_), channel_id=1, source_target_pairs={{0,6},{1,7},{2,4},{3,5},{4,2},{5,3},{6,0},{7,1},{8,14},{9,15},{10,... | collective-permute-start | bytes 49160 | tf_op jit(solution)/shard_map/ppermute | solution.py:25
  149.0 9.5 %collective-permute-start.17 = (f32[64,64]{1,0:T(8,128)S(1)}, f32[64,64]{1,0:T(8,128)S(1)}, u32[]{:S(2)}, u32[]{:S(2)}) collective-permute-start(f32[64,64]{1,0:T(8,128)S(1)} %add.74.rest_1_), channel_id=1, source_target_pairs={{0,4},{1,5},{2,6},{3,7},{4,0},{5,1},{6,2},{7,3},{8,12},{9,13},{10,... | collective-permute-start | bytes 49160 | tf_op jit(solution)/shard_map/ppermute | solution.py:25
  150.7 7.8 %collective-permute-start.16 = (f32[64,64]{1,0:T(8,128)S(1)}, f32[64,64]{1,0:T(8,128)S(1)}, u32[]{:S(2)}, u32[]{:S(2)}) collective-permute-start(f32[64,64]{1,0:T(8,128)S(1)} %add.74.rest_1_), channel_id=1, source_target_pairs={{0,2},{1,3},{2,0},{3,1},{4,6},{5,7},{6,4},{7,5},{8,10},{9,11},{10,... | collective-permute-start | bytes 49160 | tf_op jit(solution)/shard_map/ppermute | solution.py:25
  164.1 2.7 %collective-permute-start.21 = (bf16[4,16,64,128]{3,2,1,0:T(8,128)(2,1)S(1)}, bf16[4,16,64,128]{3,2,1,0:T(8,128)(2,1)S(1)}, u32[]{:S(2)}, u32[]{:S(2)}) collective-permute-start(bf16[4,16,64,128]{3,2,1,0:T(8,128)(2,1)S(1)} %get-tuple-element.53), channel_id=1, source_target_pairs={{0,1},{1,0},{2,3},{3,2},{4,5},{5,4},{6,7},{7,6},{8,9},{9,8},{10,11... | collective-permute-start | bytes 3145736 | tf_op jit(solution)/shard_map/ppermute | solution.py:25
  167.2 15.1 %collective-permute-start.25 = (bf16[16,64,128]{2,1,0:T(8,128)(2,1)S(1)}, bf16[16,64,128]{2,1,0:T(8,128)(2,1)S(1)}, u32[]{:S(2)}, u32[]{:S(2)}) collective-permute-start(bf16[16,64,128]{2,1,0:T(8,128)(2,1)S(1)} %get-tuple-element.57), channel_id=1, source_target_pairs={{0,2},{1,3},{2,0},{3,1},{4,6},{5,7},{6,4},{7,5},{8,10},{9,11},{10,... | collective-permute-start | bytes 786440 | tf_op jit(solution)/shard_map/ppermute | solution.py:25
  168.8 13.7 %collective-permute-start.26 = (bf16[16,64,128]{2,1,0:T(8,128)(2,1)S(1)}, bf16[16,64,128]{2,1,0:T(8,128)(2,1)S(1)}, u32[]{:S(2)}, u32[]{:S(2)}) collective-permute-start(bf16[16,64,128]{2,1,0:T(8,128)(2,1)S(1)} %get-tuple-element.58), channel_id=1, source_target_pairs={{0,4},{1,5},{2,6},{3,7},{4,0},{5,1},{6,2},{7,3},{8,12},{9,13},{10,... | collective-permute-start | bytes 786440 | tf_op jit(solution)/shard_map/ppermute | solution.py:25
  169.3 13.2 %collective-permute-start.27 = (bf16[16,64,128]{2,1,0:T(8,128)(2,1)S(1)}, bf16[16,64,128]{2,1,0:T(8,128)(2,1)S(1)}, u32[]{:S(2)}, u32[]{:S(2)}) collective-permute-start(bf16[16,64,128]{2,1,0:T(8,128)(2,1)S(1)} %get-tuple-element.59), channel_id=1, source_target_pairs={{0,6},{1,7},{2,4},{3,5},{4,2},{5,3},{6,0},{7,1},{8,14},{9,15},{10,... | collective-permute-start | bytes 786440 | tf_op jit(solution)/shard_map/ppermute | solution.py:25
  170.7 5.7 %collective-permute-start.24 = (f32[64,64]{1,0:T(8,128)S(1)}, f32[64,64]{1,0:T(8,128)S(1)}, u32[]{:S(2)}, u32[]{:S(2)}) collective-permute-start(f32[64,64]{1,0:T(8,128)S(1)} %get-tuple-element.56.refs_0_), channel_id=1, source_target_pairs={{0,24},{8,16},{16,8},{24,0},{1,25},{9,17},{17,9},{25,1},{2,26},{10... | collective-permute-start | bytes 49160 | tf_op jit(solution)/shard_map/ppermute | solution.py:25
  172.8 4.9 %collective-permute-start.23 = (f32[64,64]{1,0:T(8,128)S(1)}, f32[64,64]{1,0:T(8,128)S(1)}, u32[]{:S(2)}, u32[]{:S(2)}) collective-permute-start(f32[64,64]{1,0:T(8,128)S(1)} %get-tuple-element.56.refs_0_), channel_id=1, source_target_pairs={{0,16},{8,24},{16,0},{24,8},{1,17},{9,25},{17,1},{25,9},{2,18},{10... | collective-permute-start | bytes 49160 | tf_op jit(solution)/shard_map/ppermute | solution.py:25
  176.4 3.9 %collective-permute-start.22 = (f32[64,64]{1,0:T(8,128)S(1)}, f32[64,64]{1,0:T(8,128)S(1)}, u32[]{:S(2)}, u32[]{:S(2)}) collective-permute-start(f32[64,64]{1,0:T(8,128)S(1)} %get-tuple-element.56.refs_0_), channel_id=1, source_target_pairs={{0,8},{8,0},{16,24},{24,16},{1,9},{9,1},{17,25},{25,17},{2,10},{10... | collective-permute-start | bytes 49160 | tf_op jit(solution)/shard_map/ppermute | solution.py:25
  183.5 11.6 %collective-permute-start.28 = (bf16[16,64,128]{2,1,0:T(8,128)(2,1)S(1)}, bf16[16,64,128]{2,1,0:T(8,128)(2,1)S(1)}, u32[]{:S(2)}, u32[]{:S(2)}) collective-permute-start(bf16[16,64,128]{2,1,0:T(8,128)(2,1)S(1)} %get-tuple-element.61.rest_7_), channel_id=1, source_target_pairs={{0,8},{8,0},{16,24},{24,16},{1,9},{9,1},{17,25},{25,17},{2,10},{10... | collective-permute-start | bytes 786440 | tf_op jit(solution)/shard_map/ppermute | solution.py:25
  183.6 17.2 %collective-permute-start.34 = (bf16[16,64,128]{2,1,0:T(8,128)(2,1)S(1)}, bf16[16,64,128]{2,1,0:T(8,128)(2,1)S(1)}, u32[]{:S(2)}, u32[]{:S(2)}) collective-permute-start(bf16[16,64,128]{2,1,0:T(8,128)(2,1)S(1)} %get-tuple-element.61.rest_7_), channel_id=1, source_target_pairs={{0,24},{8,16},{16,8},{24,0},{1,25},{9,17},{17,9},{25,1},{2,26},{10... | collective-permute-start | bytes 786440 | tf_op jit(solution)/shard_map/ppermute | solution.py:25
  185.6 22.8 %collective-permute-start.33 = (bf16[16,64,128]{2,1,0:T(8,128)(2,1)S(1)}, bf16[16,64,128]{2,1,0:T(8,128)(2,1)S(1)}, u32[]{:S(2)}, u32[]{:S(2)}) collective-permute-start(bf16[16,64,128]{2,1,0:T(8,128)(2,1)S(1)} %get-tuple-element.61.rest_7_), channel_id=1, source_target_pairs={{0,16},{8,24},{16,0},{24,8},{1,17},{9,25},{17,1},{25,9},{2,18},{10... | collective-permute-start | bytes 786440 | tf_op jit(solution)/shard_map/ppermute | solution.py:25
  197.3 11.1 %collective-permute-start.32 = (f32[64,64]{1,0:T(8,128)S(1)}, f32[64,64]{1,0:T(8,128)S(1)}, u32[]{:S(2)}, u32[]{:S(2)}) collective-permute-start(f32[64,64]{1,0:T(8,128)S(1)} %add.75.rest_1_), channel_id=1, source_target_pairs={{0,6},{1,7},{2,4},{3,5},{4,2},{5,3},{6,0},{7,1},{8,14},{9,15},{10,... | collective-permute-start | bytes 49160 | tf_op jit(solution)/shard_map/ppermute | solution.py:25
  199.7 8.7 %collective-permute-start.31 = (f32[64,64]{1,0:T(8,128)S(1)}, f32[64,64]{1,0:T(8,128)S(1)}, u32[]{:S(2)}, u32[]{:S(2)}) collective-permute-start(f32[64,64]{1,0:T(8,128)S(1)} %add.75.rest_1_), channel_id=1, source_target_pairs={{0,4},{1,5},{2,6},{3,7},{4,0},{5,1},{6,2},{7,3},{8,12},{9,13},{10,... | collective-permute-start | bytes 49160 | tf_op jit(solution)/shard_map/ppermute | solution.py:25
  199.7 8.7 %collective-permute-start.30 = (f32[64,64]{1,0:T(8,128)S(1)}, f32[64,64]{1,0:T(8,128)S(1)}, u32[]{:S(2)}, u32[]{:S(2)}) collective-permute-start(f32[64,64]{1,0:T(8,128)S(1)} %add.75.rest_1_), channel_id=1, source_target_pairs={{0,2},{1,3},{2,0},{3,1},{4,6},{5,7},{6,4},{7,5},{8,10},{9,11},{10,... | collective-permute-start | bytes 49160 | tf_op jit(solution)/shard_map/ppermute | solution.py:25
  213.6 2.7 %collective-permute-start.35 = (bf16[4,16,64,128]{3,2,1,0:T(8,128)(2,1)S(1)}, bf16[4,16,64,128]{3,2,1,0:T(8,128)(2,1)S(1)}, u32[]{:S(2)}, u32[]{:S(2)}) collective-permute-start(bf16[4,16,64,128]{3,2,1,0:T(8,128)(2,1)S(1)} %get-tuple-element.63), channel_id=1, source_target_pairs={{0,1},{1,0},{2,3},{3,2},{4,5},{5,4},{6,7},{7,6},{8,9},{9,8},{10,11... | collective-permute-start | bytes 3145736 | tf_op jit(solution)/shard_map/ppermute | solution.py:25
  216.7 15.1 %collective-permute-start.39 = (bf16[16,64,128]{2,1,0:T(8,128)(2,1)S(1)}, bf16[16,64,128]{2,1,0:T(8,128)(2,1)S(1)}, u32[]{:S(2)}, u32[]{:S(2)}) collective-permute-start(bf16[16,64,128]{2,1,0:T(8,128)(2,1)S(1)} %get-tuple-element.66), channel_id=1, source_target_pairs={{0,2},{1,3},{2,0},{3,1},{4,6},{5,7},{6,4},{7,5},{8,10},{9,11},{10,... | collective-permute-start | bytes 786440 | tf_op jit(solution)/shard_map/ppermute | solution.py:25
  217.8 14.0 %collective-permute-start.40 = (bf16[16,64,128]{2,1,0:T(8,128)(2,1)S(1)}, bf16[16,64,128]{2,1,0:T(8,128)(2,1)S(1)}, u32[]{:S(2)}, u32[]{:S(2)}) collective-permute-start(bf16[16,64,128]{2,1,0:T(8,128)(2,1)S(1)} %get-tuple-element.67), channel_id=1, source_target_pairs={{0,4},{1,5},{2,6},{3,7},{4,0},{5,1},{6,2},{7,3},{8,12},{9,13},{10,... | collective-permute-start | bytes 786440 | tf_op jit(solution)/shard_map/ppermute | solution.py:25
  219.3 12.5 %collective-permute-start.41 = (bf16[16,64,128]{2,1,0:T(8,128)(2,1)S(1)}, bf16[16,64,128]{2,1,0:T(8,128)(2,1)S(1)}, u32[]{:S(2)}, u32[]{:S(2)}) collective-permute-start(bf16[16,64,128]{2,1,0:T(8,128)(2,1)S(1)} %get-tuple-element.68), channel_id=1, source_target_pairs={{0,6},{1,7},{2,4},{3,5},{4,2},{5,3},{6,0},{7,1},{8,14},{9,15},{10,... | collective-permute-start | bytes 786440 | tf_op jit(solution)/shard_map/ppermute | solution.py:25
  220.2 5.7 %collective-permute-start.38 = (f32[64,64]{1,0:T(8,128)S(1)}, f32[64,64]{1,0:T(8,128)S(1)}, u32[]{:S(2)}, u32[]{:S(2)}) collective-permute-start(f32[64,64]{1,0:T(8,128)S(1)} %get-tuple-element.65.refs_0_), channel_id=1, source_target_pairs={{0,24},{8,16},{16,8},{24,0},{1,25},{9,17},{17,9},{25,1},{2,26},{10... | collective-permute-start | bytes 49160 | tf_op jit(solution)/shard_map/ppermute | solution.py:25
  222.1 4.8 %collective-permute-start.37 = (f32[64,64]{1,0:T(8,128)S(1)}, f32[64,64]{1,0:T(8,128)S(1)}, u32[]{:S(2)}, u32[]{:S(2)}) collective-permute-start(f32[64,64]{1,0:T(8,128)S(1)} %get-tuple-element.65.refs_0_), channel_id=1, source_target_pairs={{0,16},{8,24},{16,0},{24,8},{1,17},{9,25},{17,1},{25,9},{2,18},{10... | collective-permute-start | bytes 49160 | tf_op jit(solution)/shard_map/ppermute | solution.py:25
  226.0 3.9 %collective-permute-start.36 = (f32[64,64]{1,0:T(8,128)S(1)}, f32[64,64]{1,0:T(8,128)S(1)}, u32[]{:S(2)}, u32[]{:S(2)}) collective-permute-start(f32[64,64]{1,0:T(8,128)S(1)} %get-tuple-element.65.refs_0_), channel_id=1, source_target_pairs={{0,8},{8,0},{16,24},{24,16},{1,9},{9,1},{17,25},{25,17},{2,10},{10... | collective-permute-start | bytes 49160 | tf_op jit(solution)/shard_map/ppermute | solution.py:25
  235.6 4.9 %collective-permute-start.45 = (f32[64,64]{1,0:T(8,128)S(1)}, f32[64,64]{1,0:T(8,128)S(1)}, u32[]{:S(2)}, u32[]{:S(2)}) collective-permute-start(f32[64,64]{1,0:T(8,128)S(1)} %add.76), channel_id=1, source_target_pairs={{0,6},{1,7},{2,4},{3,5},{4,2},{5,3},{6,0},{7,1},{8,14},{9,15},{10,... | collective-permute-start | bytes 49160 | tf_op jit(solution)/shard_map/ppermute | solution.py:25
  237.6 3.9 %collective-permute-start.44 = (f32[64,64]{1,0:T(8,128)S(1)}, f32[64,64]{1,0:T(8,128)S(1)}, u32[]{:S(2)}, u32[]{:S(2)}) collective-permute-start(f32[64,64]{1,0:T(8,128)S(1)} %add.76), channel_id=1, source_target_pairs={{0,4},{1,5},{2,6},{3,7},{4,0},{5,1},{6,2},{7,3},{8,12},{9,13},{10,... | collective-permute-start | bytes 49160 | tf_op jit(solution)/shard_map/ppermute | solution.py:25
  238.1 3.9 %collective-permute-start.43 = (f32[64,64]{1,0:T(8,128)S(1)}, f32[64,64]{1,0:T(8,128)S(1)}, u32[]{:S(2)}, u32[]{:S(2)}) collective-permute-start(f32[64,64]{1,0:T(8,128)S(1)} %add.76), channel_id=1, source_target_pairs={{0,2},{1,3},{2,0},{3,1},{4,6},{5,7},{6,4},{7,5},{8,10},{9,11},{10,... | collective-permute-start | bytes 49160 | tf_op jit(solution)/shard_map/ppermute | solution.py:25
  242.0 5.8 %collective-permute-start.48 = (f32[64,64]{1,0:T(8,128)S(1)}, f32[64,64]{1,0:T(8,128)S(1)}, u32[]{:S(2)}, u32[]{:S(2)}) collective-permute-start(f32[64,64]{1,0:T(8,128)S(1)} %add_add_fusion.refs_0_), channel_id=1, source_target_pairs={{0,24},{8,16},{16,8},{24,0},{1,25},{9,17},{17,9},{25,1},{2,26},{10... | collective-permute-start | bytes 49160 | tf_op jit(solution)/shard_map/ppermute | solution.py:25
  243.8 4.9 %collective-permute-start.47 = (f32[64,64]{1,0:T(8,128)S(1)}, f32[64,64]{1,0:T(8,128)S(1)}, u32[]{:S(2)}, u32[]{:S(2)}) collective-permute-start(f32[64,64]{1,0:T(8,128)S(1)} %add_add_fusion.refs_0_), channel_id=1, source_target_pairs={{0,16},{8,24},{16,0},{24,8},{1,17},{9,25},{17,1},{25,9},{2,18},{10... | collective-permute-start | bytes 49160 | tf_op jit(solution)/shard_map/ppermute | solution.py:25
  243.8 4.9 %collective-permute-start.46 = (f32[64,64]{1,0:T(8,128)S(1)}, f32[64,64]{1,0:T(8,128)S(1)}, u32[]{:S(2)}, u32[]{:S(2)}) collective-permute-start(f32[64,64]{1,0:T(8,128)S(1)} %add_add_fusion.refs_0_), channel_id=1, source_target_pairs={{0,8},{8,0},{16,24},{24,16},{1,9},{9,1},{17,25},{25,17},{2,10},{10... | collective-permute-start | bytes 49160 | tf_op jit(solution)/shard_map/ppermute | solution.py:25
  (8 other events, 91.1 us)

commit v4 on v3

--- a/solution.py
+++ b/solution.py
@@ -9,6 +9,7 @@
 
 ITERS = 3
 CAP = 3
+PARTS = 2
 F32 = jnp.float32
 BF16 = jnp.bfloat16
 VMEM = pl.BlockSpec(memory_space=pltpu.VMEM)
@@ -68,7 +69,7 @@
     lax.fori_loop(0, devices, note, 0, unroll=2)
 
 
-def stock_kernel(tile_rows, tiles, *refs):
+def stock_kernel(early, row_size, tile_rows, tiles, *refs):
     pieces, (stock, degree) = refs[:-2], refs[-2:]
     tile, count = tiles.shape[1], tiles.shape[0]
     features = stock.shape[1]
@@ -84,9 +85,18 @@
 
     lax.fori_loop(0, count, own, 0, unroll=4)
     at = count * per_tile
-    for piece in pieces:
-        stock[at : at + piece.shape[0]] = piece[...]
-        at += piece.shape[0]
+    families = len(pieces) - (row_size - len(early))
+    late = list(pieces[families:])
+    for d in range(row_size):
+        if d in early:
+            start = early.index(d) * row_size
+            for family in range(families):
+                stock[at : at + row_size] = pieces[family][start : start + row_size]
+                at += row_size
+        else:
+            piece = late.pop(0)
+            stock[at : at + piece.shape[0]] = piece[...]
+            at += piece.shape[0]
     high, low = two_parts(degree[...])
     for part in (high, low):
         for k in range(0, part.shape[0], features):
@@ -103,14 +113,14 @@
     return block[at : at + rows].astype(F32) + block[at + rows : at + 2 * rows].astype(F32)
 
 
-def merge_kernel(row_size, sub, place, *refs):
+def merge_kernel(count, row_size, sub, place, *refs):
     features, tile = refs[-1].shape[1:]
     groups = tile // sub
-    sources, outs = refs[: row_size * groups], refs[row_size * groups :]
+    sources, outs = refs[: count * groups], refs[count * groups :]
     member, family = place[0] % groups, place[0] // groups
     lane = lax.broadcasted_iota(jnp.int32, (features, tile), 1) // sub
     for distance, out in enumerate(outs):
-        for source in range(row_size):
+        for source in range(count):
 
             def join(r, carry, distance=distance, out=out, source=source):
                 block = r * len(outs) + jnp.bitwise_xor(family, distance)
@@ -149,7 +159,7 @@
         per_row_bits, per_device_bits = per_row.bit_length() - 1, per_device.bit_length() - 1
         inner, outer = jnp.bitwise_and(note, per_row - 1), jnp.right_shift(note, per_device_bits)
         source = jnp.bitwise_xor(jnp.right_shift(jnp.bitwise_and(note, per_device - 1), per_row_bits), place[2])
-        block = (jnp.bitwise_xor(inner, place[1]) * row_size + source) * row_size + outer
+        block = (source * per_row + jnp.bitwise_xor(inner, place[1])) * row_size + outer
         even = jnp.bitwise_and(lane, 1) == 0
         number_buf[...] = jnp.where(even, note, block)
         found[...] = jnp.where(even, note, source * per_device + outer * per_row + inner)
@@ -157,8 +167,9 @@
         numbers_copy.start()
     else:
         found[...] = sum(gram[...] for gram in grams)
+        size = per_device // PARTS
         for i, piece in enumerate(pieces):
-            x_buf[i * per_device : (i + 1) * per_device] = piece[...]
+            x_buf[i * size : (i + 1) * size] = piece[...]
 
     def x_block(block):
         return stock[x_start + block] if first else x_buf[block]
@@ -251,8 +262,8 @@
 
 def scale_kernel(normalize, last, first, own, *rest):
     if first:
-        received, (out, scaled, degrees) = rest[:-3], rest[-3:]
-        per_device = out.shape[0]
+        received, (*out, scaled, degrees) = rest[: -2 - PARTS], rest[-2 - PARTS :]
+        per_device = scaled.shape[0]
         parts = [own[per_device]] + [piece[per_device] for piece in received]
         for i in range(2):
             degrees[i] = 1.0 + sum(one_part(part, 2 * i * per_device, per_device) for part in parts)
@@ -260,11 +271,14 @@
         gram = jnp.zeros((1, 1), F32)
     else:
         degrees, inverse, rest = rest[0], rest[1], rest[2:]
-        received, (out, scaled) = rest[:-2], rest[-2:]
+        made = 1 if last else PARTS
+        received, (*out, scaled) = rest[: -1 - made], rest[-1 - made :]
         degree = degrees.at[1 if last else 0]
         gram = jnp.zeros(inverse.shape, F32)
 
-    def add(b, gram):
+    size = scaled.shape[0] // PARTS
+
+    def add(b, gram, part=0):
         total = own[b]
         for piece in received:
             total = total + piece[b].astype(F32)
@@ -276,12 +290,14 @@
             return gram + lax.dot_general(
                 total, total, (((1,), (1,)), ((), ())), precision=lax.Precision.HIGHEST, preferred_element_type=F32
             )
-        out[b] = total.astype(BF16)
+        out[part][b - part * size] = total.astype(BF16)
         return gram
 
-    gram = lax.fori_loop(0, scaled.shape[0], add, gram, unroll=scaled.shape[0] if last else 4)
     if last:
-        out[...] = gram
+        out[0][...] = lax.fori_loop(0, scaled.shape[0], add, gram, unroll=scaled.shape[0])
+        return
+    for part in range(PARTS):
+        lax.fori_loop(part * size, (part + 1) * size, functools.partial(add, part=part), gram, unroll=4)
 
 
 def gram_kernel(scaled, mark, gram):
@@ -369,7 +385,8 @@
 
     member, family = col % groups, col // groups
     embed_t = embed.T
-    raw = [embed_t] + [exchange(embed_t, "row", d) for d in range(1, row_size)]
+    early = [d for d in range(row_size) if d & (d - 1) == 0]
+    raw = [embed_t] + [exchange(embed_t, "row", d) for d in early[1:]]
     slots = pl.pallas_call(
         functools.partial(pack_kernel, devices, row_blocks, col_blocks, col_size),
         out_shape=jax.ShapeDtypeStruct((devices, CAP * tile + 16, tile), BF16),
@@ -386,19 +403,27 @@
         cost_estimate=NONE,
         name="pack",
     )(chg_rows, chg_cols, chg_tiles)
-    gathered = pl.pallas_call(
-        functools.partial(merge_kernel, row_size, sub),
-        out_shape=(jax.ShapeDtypeStruct((row_size * row_size, features, tile), BF16),) * per_row,
-        in_specs=[SMEM] + [VMEM] * (row_size * groups),
+    merged = pl.pallas_call(
+        functools.partial(merge_kernel, len(early), row_size, sub),
+        out_shape=(jax.ShapeDtypeStruct((len(early) * row_size, features, tile), BF16),) * per_row,
+        in_specs=[SMEM] + [VMEM] * (len(early) * groups),
         out_specs=(VMEM,) * per_row,
-        compiler_params=params(2 * rows_dev * features * row_size * (groups + row_size) + 8 * MIB),
+        compiler_params=params(2 * rows_dev * features * len(early) * (groups + row_size) + 8 * MIB),
         cost_estimate=NONE,
         name="merge",
     )(
         col.reshape(1),
         *[piece if d == 0 else exchange(piece, "col", d) for piece in raw for d in range(groups)],
     )
-    gathered = [gathered[0]] + [exchange(gathered[d], "col", d * groups) for d in range(1, per_row)]
+    gathered = [merged[0]] + [exchange(merged[d], "col", d * groups) for d in range(1, per_row)]
+    complete = {}
+    for d in range(1, row_size):
+        if d in early:
+            at = early.index(d) * row_size
+            complete[d] = jnp.concatenate([piece[at : at + row_size] for piece in gathered], axis=0)
+        else:
+            complete[d] = exchange(complete[d & (d - 1)], "row", d & -d)
+    late = [complete[d] for d in range(row_size) if d not in early]
     slots = lax.optimization_barrier((slots, *raw[1:]))[0]
     taken = lax.all_to_all(slots, ("row", "col"), split_axis=0, concat_axis=0, tiled=True)
 
@@ -406,22 +431,22 @@
         source = position % per_device // per_row
         outer, inner = position // per_device, position % per_row
         if first:
-            return (jnp.bitwise_xor(inner, family) * row_size + jnp.bitwise_xor(source, row)) * row_size + outer
+            return (jnp.bitwise_xor(source, row) * per_row + jnp.bitwise_xor(inner, family)) * row_size + outer
         return jnp.bitwise_xor(source, row) * per_device + outer * per_row + inner
 
     own_rows, own_cols = tile_rows % row_blocks, tile_cols % col_blocks
     per_tile = tile // features
     stock_blocks = tiles.shape[0] * per_tile + col_blocks + 2 * row_blocks // features
     stock = pl.pallas_call(
-        stock_kernel,
+        functools.partial(stock_kernel, early, row_size),
         out_shape=jax.ShapeDtypeStruct((stock_blocks, features, tile), BF16),
-        in_specs=[SMEM] + [VMEM] * (1 + len(gathered)),
+        in_specs=[SMEM] + [VMEM] * (1 + len(gathered) + len(late)),
         out_specs=VMEM,
         scratch_shapes=[pltpu.VMEM((row_blocks, tile), F32)],
         compiler_params=params(4 * tiles.size + 4 * stock_blocks * features * tile + 4 * MIB),
         cost_estimate=NONE,
         name="stock",
-    )(own_rows, tiles, *gathered)
+    )(own_rows, tiles, *gathered, *late)
 
     place = jnp.stack([col % 2, family, row])
     square = jax.ShapeDtypeStruct((features, features), F32)
@@ -431,7 +456,12 @@
         blocks = per_device + 1 if first else per_device
         shape = (blocks, features, tile)
         if iteration:
-            gathered = [current] + [exchange(current, "row", d) for d in range(1, row_size)]
+            gathered = {0: current}
+            for d in sorted(range(1, row_size), key=lambda d: (d & (d - 1) != 0, -d if d & (d - 1) == 0 else d)):
+                low = d & -d
+                gathered[d] = [exchange(part, "row", low) for part in gathered[d ^ low]]
+            first_part = gathered[row_size // 2][0]
+            gathered = [part for d in range(row_size) for part in gathered[d]]
             gram = pl.pallas_call(
                 gram_kernel,
                 out_shape=jax.ShapeDtypeStruct((features, features), F32),
@@ -440,12 +470,12 @@
                 compiler_params=params(),
                 cost_estimate=NONE,
                 name="gram",
-            )(scaled, gathered[1])
+            )(scaled, first_part)
             grams = chip_parts(gram + exchange(gram, "col", 1))
         keep, send, found = pl.pallas_call(
             functools.partial(product_kernel, not last, first, sub, per_device, row_size, half, 0 if first else len(gathered)),
             out_shape=(jax.ShapeDtypeStruct((half, *shape), BF16),) * 2 + (numbers_shape if first else square,),
-            in_specs=[SMEM] * 3 + ([VMEM] * 2 if first else [SMEM] + [VMEM] * (2 + half + row_size)),
+            in_specs=[SMEM] * 3 + ([VMEM] * 2 if first else [SMEM] + [VMEM] * (2 + half + len(gathered))),
             out_specs=(VMEM, VMEM, VMEM),
             scratch_shapes=[
                 pltpu.VMEM((1 if first else col_blocks, features, tile), BF16),
@@ -490,17 +520,18 @@
                 name="factor",
             )(*grams)
         both = jax.ShapeDtypeStruct((2, per_device, tile), F32)
-        current, scaled, *rest = pl.pallas_call(
+        piece = jax.ShapeDtypeStruct((per_device // PARTS, features, tile), BF16)
+        *current, scaled = pl.pallas_call(
             functools.partial(scale_kernel, not first, last, first),
-            out_shape=(square if last else block, block32) + ((both,) if first else ()),
+            out_shape=((square,) if last else (piece,) * PARTS) + (block32,) + ((both,) if first else ()),
             in_specs=[VMEM] * ((1 if first else 3) + half - 1),
-            out_specs=(VMEM,) * (3 if first else 2),
+            out_specs=(VMEM,) * (2 if last else PARTS + 2 if first else PARTS + 1),
             compiler_params=params(),
             cost_estimate=NONE,
             name="scale",
         )(paired[-1], *([] if first else [degrees, inverse]), *received)
         if first:
-            degrees = rest[0]
+            *current, scaled, degrees = *current, scaled
     out = pl.pallas_call(
         functools.partial(final_kernel, nodes),
         out_shape=jax.ShapeDtypeStruct((features, rows_dev), F32),
@@ -509,7 +540,7 @@
         compiler_params=params(),
         cost_estimate=NONE,
         name="final",
-    )(scaled, *along_row(sum(chip_parts(current + exchange(current, "col", 1)))))
+    )(scaled, *along_row(sum(chip_parts(current[0] + exchange(current[0], "col", 1)))))
     return out.T
 
 

time: 252 us -> 236 us (0.937)
  waiting for transfers between devices: 158 us -> 127 us
  starting transfers between devices: 52 us -> 59.1 us
  local copies, waits for them, and re-layouts: 3.63 us -> 8.72 us
    all_to_all x1, waiting for transfers between devices: 24.6 us -> 8.73 us  [local(): lax.all_to_all(slots, ('row', 'col'), split_axis=0, concat_axis=0, tiled=...]
    ppermute x49 -> x54, waiting for transfers between devices: 133 us -> 119 us  [exchange(): return lax.ppermute(value, axis, [(i, i ^ distance) for i in range(size)])]
    ppermute x49 -> x54, starting transfers between devices: 47.3 us -> 53.6 us  [exchange(): return lax.ppermute(value, axis, [(i, i ^ distance) for i in range(size)])]
    unnamed x12 -> x14, local copies, waits for them, and re-layouts: 3.63 us -> 6.18 us
    slice x0 -> x4, local copies, waits for them, and re-layouts: none -> 2.54 us  [local(): piece[at:at + row_size]]
  transfers between devices with their start and end apart: 50 -> 55, of which waited for: 34 -> 38; matrix products, arithmetic and copies ran while one was open for 0% -> 1% of each run, Pallas kernels for 6% -> 6%
where the time goes in v4:
time: 236 us; the launch traced here: 235 us
  waiting for transfers between devices  127 us (54%)
  starting transfers between devices  59.1 us (25%)
  Pallas kernels  39.4 us (17%)
  local copies, waits for them, and re-layouts  8.72 us (4%)
    ppermute x54, waiting for transfers between devices, exchange(): return lax.ppermute(value, axis, [(i, i ^ distance) for i in range(size)])  119 us
    ppermute x54, starting transfers between devices, exchange(): return lax.ppermute(value, axis, [(i, i ^ distance) for i in range(size)])  53.6 us
    pallas_call x3, Pallas kernels, local(): pl.pallas_call(functools.partial(product_kernel, not last, first, sub, pe...  16.4 us
    all_to_all x1, waiting for transfers between devices, local(): lax.all_to_all(slots, ('row', 'col'), split_axis=0, concat_axis=0, tiled=...  8.73 us
    unnamed x14, local copies, waits for them, and re-layouts  6.18 us
    all_to_all x1, starting transfers between devices, local(): lax.all_to_all(slots, ('row', 'col'), split_axis=0, concat_axis=0, tiled=...  5.5 us
  transfers between devices with their start and end apart: 55, of which 38 were waited for; matrix products, arithmetic and copies ran while one was open for 1% of the time, Pallas kernels for 6%

profile of v4, /device:TPU:0, one launch (start us, length us, event | category | flops | bytes accessed | tf_op | source)
XLA Modules:
  0.0 235.1 jit_solution(11454323881716623122)
XLA Ops:
  0.0 4.0 %collective-permute-start.3 = (bf16[64,2048]{1,0:T(8,128)(2,1)}, bf16[64,2048]{1,0:T(8,128)(2,1)}, u32[]{:S(2)}, u32[]{:S(2)}) collective-permute-start(bf16[64,2048]{1,0:T(8,128)(2,1)} %bitcast.6), channel_id=1, source_target_pairs={{0,16},{8,24},{16,0},{24,8},{1,17},{9,25},{17,1},{25,9},{2,18},{10... | collective-permute-start | bytes 786440 | tf_op jit(solution)/shard_map/ppermute | solution.py:26
  4.0 1.6 collective-permute-start.1
  5.6 4.1 %pack.1 = bf16[32,400,128]{2,1,0:T(8,128)(2,1)} custom-call(s32[48]{0:T(128)} %rows_in.1, s32[48]{0:T(128)} %cols_in.1, bf16[48,128,128]{2,1,0:T(8,128)(2,1)} %chg.1), custom_call_target="tpu_custom_call" | custom-call | tf_op jit(solution)/shard_map/pack/pallas_call | solution.py:390
  9.8 6.6 %collective-permute-done.3.refs_4_ = bf16[64,2048]{1,0:T(8,128)(2,1)} collective-permute-done((bf16[64,2048]{1,0:T(8,128)(2,1)}, bf16[64,2048]{1,0:T(8,128)(2,1)}, u32[]{:S(2)}, u32[]{:S(2)}) %collective-permute-start.3) | collective-permute-done | bytes 262176 | tf_op jit(solution)/shard_map/ppermute | solution.py:26
  16.6 5.5 %all-to-all-start = ((bf16[32,400,128]{2,1,0:T(8,128)(2,1)}), bf16[32,400,128]{2,1,0:T(8,128)(2,1)S(1)}, u32[]{:S(2)}, u32[]{:S(2)}) async-start(bf16[32,400,128]{2,1,0:T(8,128)(2,1)} %pack.1), calls=%async_computation | async-start | bytes 6553600 | tf_op jit(solution)/shard_map/all_to_all | solution.py:428
  25.8 2.5 %merge.1 = (bf16[12,64,128]{2,1,0:T(8,128)(2,1)S(1)}, bf16[12,64,128]{2,1,0:T(8,128)(2,1)}, bf16[12,64,128]{2,1,0:T(8,128)(2,1)}, bf16[12,64,128]{2,1,0:T(8,128)(2,1)}) custom-call(s32[1]{0:T(128)} %bitcast.3.place, bf16[64,2048]{1,0:T(8,128)(2,1)S(1)} %bitcast.9, bf16[64,2048]{1,0:T(8,128)(2,1)} %collective-permute-done.refs_1_, ...), custom_call_target="tpu_custom_call" | custom-call | tf_op jit(solution)/shard_map/merge/pallas_call | solution.py:406
  28.2 1.8 collective-permute-start.5
  30.0 1.5 collective-permute-start.6
  31.7 18.9 %collective-permute-done.5.refs_1_ = bf16[12,64,128]{2,1,0:T(8,128)(2,1)} collective-permute-done((bf16[12,64,128]{2,1,0:T(8,128)(2,1)}, bf16[12,64,128]{2,1,0:T(8,128)(2,1)}, u32[]{:S(2)}, u32[]{:S(2)}) %collective-permute-start.5) | collective-permute-done | bytes 196640 | tf_op jit(solution)/shard_map/ppermute | solution.py:26
  52.3 11.4 %collective-permute-done.7.refs_3_ = bf16[12,64,128]{2,1,0:T(8,128)(2,1)} collective-permute-done((bf16[12,64,128]{2,1,0:T(8,128)(2,1)}, bf16[12,64,128]{2,1,0:T(8,128)(2,1)}, u32[]{:S(2)}, u32[]{:S(2)}) %collective-permute-start.7) | collective-permute-done | bytes 196640 | tf_op jit(solution)/shard_map/ppermute | solution.py:26
  64.8 17.0 %collective-permute-done.8.refs_4_ = bf16[16,64,128]{2,1,0:T(8,128)(2,1)S(1)} collective-permute-done((bf16[16,64,128]{2,1,0:T(8,128)(2,1)S(1)}, bf16[16,64,128]{2,1,0:T(8,128)(2,1)S(1)}, u32[]{:S(2)}, u32[]{:S(2)}) %collective-permute-start.8) | collective-permute-done | bytes 262176 | tf_op jit(solution)/shard_map/ppermute | solution.py:26
  81.8 1.6 copy-done.2
  83.3 2.8 %stock.1.rest_0_.rest_5_ = bf16[196,64,128]{2,1,0:T(8,128)(2,1)S(1)} custom-call(s32[64]{0:T(128)S(1)} %get-tuple-element.79.tile_rows.own_rows, bf16[64,128,128]{2,1,0:T(8,128)(2,1)S(1)} %copy-done.2, bf16[12,64,128]{2,1,0:T(8,128)(2,1)S(1)} %get-tuple-element.40.refs_0_, bf16[12,64,128]{2,1,0:T(8,128)(2,1)} %collective-permute-done.5.refs_1_, ...), custom_call_target="tpu_custom_call" | custom-call | tf_op jit(solution)/shard_map/stock/pallas_call | solution.py:440
  86.2 1.7 copy-done
  87.9 8.7 %all-to-all-done.rest_1_.rest_6_ = bf16[32,400,128]{2,1,0:T(8,128)(2,1)S(1)} async-done(((bf16[32,400,128]{2,1,0:T(8,128)(2,1)}), bf16[32,400,128]{2,1,0:T(8,128)(2,1)S(1)}, u32[]{:S(2)}, u32[]{:S(2)}) %all-to-all-start) | async-done | bytes 3276832 | tf_op jit(solution)/shard_map/all_to_all | solution.py:428
  96.6 1.9 copy-done.1
  98.5 5.6 %product.3 = (bf16[4,17,64,128]{3,2,1,0:T(8,128)(2,1)S(1)}, bf16[4,17,64,128]{3,2,1,0:T(8,128)(2,1)S(1)}, s32[32,128]{1,0:T(8,128)S(1)}) custom-call(s32[3]{0:T(128)S(1)} %pad_add_fusion.place, s32[64]{0:T(128)S(1)} %get-tuple-element.79.tile_rows.own_rows, s32[64]{0:T(128)S(1)} %get-tuple-element.75.own_x, bf16[196,64,128]{2,1,0:T(8,128)(2,1)S(1)} %copy-done.1, ...), custom_call_target="tpu_custom_call" | custom-call | tf_op jit(solution)/shard_map/product/pallas_call | solution.py:475
  104.2 2.7 %collective-permute-done.9.other = bf16[4,17,64,128]{3,2,1,0:T(8,128)(2,1)S(1)} collective-permute-done((bf16[4,17,64,128]{3,2,1,0:T(8,128)(2,1)S(1)}, bf16[4,17,64,128]{3,2,1,0:T(8,128)(2,1)S(1)}, u32[]{:S(2)}, u32[]{:S(2)}) %collective-permute-start.9) | collective-permute-done | bytes 1114144 | tf_op jit(solution)/shard_map/ppermute | solution.py:26
  108.3 1.5 collective-permute-start.11
  110.9 6.0 %collective-permute-done.10.rest_0_ = bf16[17,64,128]{2,1,0:T(8,128)(2,1)S(1)} collective-permute-done((bf16[17,64,128]{2,1,0:T(8,128)(2,1)S(1)}, bf16[17,64,128]{2,1,0:T(8,128)(2,1)S(1)}, u32[]{:S(2)}, u32[]{:S(2)}) %collective-permute-start.10) | collective-permute-done | bytes 278560 | tf_op jit(solution)/shard_map/ppermute | solution.py:26
  116.9 5.8 %collective-permute-done.11.rest_1_ = bf16[17,64,128]{2,1,0:T(8,128)(2,1)S(1)} collective-permute-done((bf16[17,64,128]{2,1,0:T(8,128)(2,1)S(1)}, bf16[17,64,128]{2,1,0:T(8,128)(2,1)S(1)}, u32[]{:S(2)}, u32[]{:S(2)}) %collective-permute-start.11) | collective-permute-done | bytes 278560 | tf_op jit(solution)/shard_map/ppermute | solution.py:26
  123.0 2.9 %collective-permute-start.20 = (bf16[8,64,128]{2,1,0:T(8,128)(2,1)S(1)}, bf16[8,64,128]{2,1,0:T(8,128)(2,1)S(1)}, u32[]{:S(2)}, u32[]{:S(2)}) collective-permute-start(bf16[8,64,128]{2,1,0:T(8,128)(2,1)S(1)} %get-tuple-element.54.rest_8_), channel_id=1, source_target_pairs={{0,16},{8,24},{16,0},{24,8},{1,17},{9,25},{17,1},{25,9},{2,18},{10... | collective-permute-start | bytes 393224 | tf_op jit(solution)/shard_map/ppermute | solution.py:26
  125.9 2.0 collective-permute-start.19
  127.9 5.6 %collective-permute-done.13.mark.rest_11_ = bf16[8,64,128]{2,1,0:T(8,128)(2,1)S(1)} collective-permute-done((bf16[8,64,128]{2,1,0:T(8,128)(2,1)S(1)}, bf16[8,64,128]{2,1,0:T(8,128)(2,1)S(1)}, u32[]{:S(2)}, u32[]{:S(2)}) %collective-permute-start.13) | collective-permute-done | bytes 131104 | tf_op jit(solution)/shard_map/ppermute | solution.py:26
  134.6 1.6 collective-permute-done.20.rest_12_
  142.0 1.4 collective-permute-done.15.rest_2_
  143.8 5.6 %product.4 = (bf16[4,16,64,128]{3,2,1,0:T(8,128)(2,1)S(1)}, bf16[4,16,64,128]{3,2,1,0:T(8,128)(2,1)S(1)}, f32[64,64]{1,0:T(8,128)S(1)}) custom-call(s32[3]{0:T(128)S(1)} %pad_add_fusion.place, s32[64]{0:T(128)S(1)} %get-tuple-element.79.tile_rows.own_rows, s32[64]{0:T(128)S(1)} %add_add_fusion.1.own_x, s32[32,128]{1,0:T(8,128)S(1)} %get-tuple-element.45.rest_0_, ...), custom_call_target="tpu_custom_call" | custom-call | tf_op jit(solution)/shard_map/product/pallas_call | solution.py:475
  149.5 2.6 %collective-permute-done.23.other = bf16[4,16,64,128]{3,2,1,0:T(8,128)(2,1)S(1)} collective-permute-done((bf16[4,16,64,128]{3,2,1,0:T(8,128)(2,1)S(1)}, bf16[4,16,64,128]{3,2,1,0:T(8,128)(2,1)S(1)}, u32[]{:S(2)}, u32[]{:S(2)}) %collective-permute-start.23) | collective-permute-done | bytes 1048608 | tf_op jit(solution)/shard_map/ppermute | solution.py:26
  154.5 1.5 collective-permute-start.29
  156.0 1.9 collective-permute-start.26
  158.8 2.9 %collective-permute-done.26.refs_3_ = f32[64,64]{1,0:T(8,128)S(1)} collective-permute-done((f32[64,64]{1,0:T(8,128)S(1)}, f32[64,64]{1,0:T(8,128)S(1)}, u32[]{:S(2)}, u32[]{:S(2)}) %collective-permute-start.26) | collective-permute-done | bytes 16416 | tf_op jit(solution)/shard_map/ppermute | solution.py:26
  162.9 2.7 %collective-permute-done.24.refs_1_ = f32[64,64]{1,0:T(8,128)S(1)} collective-permute-done((f32[64,64]{1,0:T(8,128)S(1)}, f32[64,64]{1,0:T(8,128)S(1)}, u32[]{:S(2)}, u32[]{:S(2)}) %collective-permute-start.24) | collective-permute-done | bytes 16416 | tf_op jit(solution)/shard_map/ppermute | solution.py:26
  165.6 1.9 factor.2.rest_1_
  169.6 2.0 collective-permute-start.37
  173.6 6.0 %collective-permute-done.30.mark.rest_11_ = bf16[8,64,128]{2,1,0:T(8,128)(2,1)S(1)} collective-permute-done((bf16[8,64,128]{2,1,0:T(8,128)(2,1)S(1)}, bf16[8,64,128]{2,1,0:T(8,128)(2,1)S(1)}, u32[]{:S(2)}, u32[]{:S(2)}) %collective-permute-start.30) | collective-permute-done | bytes 131104 | tf_op jit(solution)/shard_map/ppermute | solution.py:26
  179.7 2.6 %collective-permute-done.37.rest_12_ = bf16[8,64,128]{2,1,0:T(8,128)(2,1)S(1)} collective-permute-done((bf16[8,64,128]{2,1,0:T(8,128)(2,1)S(1)}, bf16[8,64,128]{2,1,0:T(8,128)(2,1)S(1)}, u32[]{:S(2)}, u32[]{:S(2)}) %collective-permute-start.37) | collective-permute-done | bytes 131104 | tf_op jit(solution)/shard_map/ppermute | solution.py:26
  184.4 1.8 collective-permute-start.34
  190.9 5.2 %product.5 = (bf16[4,16,64,128]{3,2,1,0:T(8,128)(2,1)S(1)}, bf16[4,16,64,128]{3,2,1,0:T(8,128)(2,1)S(1)}, f32[64,64]{1,0:T(8,128)S(1)}) custom-call(s32[3]{0:T(128)S(1)} %pad_add_fusion.place, s32[64]{0:T(128)S(1)} %get-tuple-element.79.tile_rows.own_rows, s32[64]{0:T(128)S(1)} %add_add_fusion.1.own_x, s32[32,128]{1,0:T(8,128)S(1)} %get-tuple-element.45.rest_0_, ...), custom_call_target="tpu_custom_call" | custom-call | tf_op jit(solution)/shard_map/product/pallas_call | solution.py:475
  196.2 2.6 %collective-permute-done.40.other = bf16[4,16,64,128]{3,2,1,0:T(8,128)(2,1)S(1)} collective-permute-done((bf16[4,16,64,128]{3,2,1,0:T(8,128)(2,1)S(1)}, bf16[4,16,64,128]{3,2,1,0:T(8,128)(2,1)S(1)}, u32[]{:S(2)}, u32[]{:S(2)}) %collective-permute-start.40) | collective-permute-done | bytes 1048608 | tf_op jit(solution)/shard_map/ppermute | solution.py:26
  202.7 1.8 collective-permute-start.43
  204.5 1.7 collective-permute-start.42
  206.2 2.3 collective-permute-done.43.refs_3_
  209.3 3.0 %collective-permute-done.41.refs_1_ = f32[64,64]{1,0:T(8,128)S(1)} collective-permute-done((f32[64,64]{1,0:T(8,128)S(1)}, f32[64,64]{1,0:T(8,128)S(1)}, u32[]{:S(2)}, u32[]{:S(2)}) %collective-permute-start.41) | collective-permute-done | bytes 16416 | tf_op jit(solution)/shard_map/ppermute | solution.py:26
  212.4 1.9 factor.3.rest_1_
  214.3 2.5 %scale.5 = (f32[64,64]{1,0:T(8,128)S(1)}, f32[16,64,128]{2,1,0:T(8,128)S(1)}) custom-call(f32[16,64,128]{2,1,0:T(8,128)S(1)} %get-tuple-element.68.own, f32[2,16,128]{2,1,0:T(8,128)S(1)} %get-tuple-element.58.rest_0_, f32[64,64]{1,0:T(8,128)S(1)} %factor.3.rest_1_, bf16[16,64,128]{2,1,0:T(8,128)(2,1)S(1)} %collective-permute-done.44.rest_2_, ...), custom_call_target="tpu_custom_call" | custom-call | tf_op jit(solution)/shard_map/scale/pallas_call | solution.py:524
  218.1 1.5 collective-permute-start.50
  224.5 2.0 collective-permute-start.53
  231.8 3.3 %final.1 = f32[64,2048]{1,0:T(8,128)} custom-call(f32[16,64,128]{2,1,0:T(8,128)S(1)} %get-tuple-element.73.scaled, f32[64,64]{1,0:T(8,128)S(1)} %add_add_fusion.refs_0_, f32[64,64]{1,0:T(8,128)S(1)} %collective-permute-done.51.refs_1_, f32[64,64]{1,0:T(8,128)S(1)} %collective-permute-done.52.refs_2_, f32[64,64]{1,0:T(8,128)S(1)} %collective-permute-done.53.refs_3_), custom_call_target="tpu_custom_call" | custom-call | tf_op jit(solution)/shard_map/final/pallas_call | solution.py:535
  (105 shorter events, 48.5 us)
Async XLA Ops:
  0.0 16.4 %collective-permute-start.3 = (bf16[64,2048]{1,0:T(8,128)(2,1)}, bf16[64,2048]{1,0:T(8,128)(2,1)}, u32[]{:S(2)}, u32[]{:S(2)}) collective-permute-start(bf16[64,2048]{1,0:T(8,128)(2,1)} %bitcast.6), channel_id=1, source_target_pairs={{0,16},{8,24},{16,0},{24,8},{1,17},{9,25},{17,1},{25,9},{2,18},{10... | collective-permute-start | bytes 786440 | tf_op jit(solution)/shard_map/ppermute | solution.py:26
  4.0 12.5 %collective-permute-start.1 = (bf16[64,2048]{1,0:T(8,128)(2,1)}, bf16[64,2048]{1,0:T(8,128)(2,1)}, u32[]{:S(2)}, u32[]{:S(2)}) collective-permute-start(bf16[64,2048]{1,0:T(8,128)(2,1)} %bitcast.7), channel_id=1, source_target_pairs={{0,8},{8,0},{16,24},{24,16},{1,9},{9,1},{17,25},{25,17},{2,10},{10... | collective-permute-start | bytes 786440 | tf_op jit(solution)/shard_map/ppermute | solution.py:26
  16.6 80.1 %all-to-all-start = ((bf16[32,400,128]{2,1,0:T(8,128)(2,1)}), bf16[32,400,128]{2,1,0:T(8,128)(2,1)S(1)}, u32[]{:S(2)}, u32[]{:S(2)}) async-start(bf16[32,400,128]{2,1,0:T(8,128)(2,1)} %pack.1), calls=%async_computation | async-start | bytes 6553600 | tf_op jit(solution)/shard_map/all_to_all | solution.py:428
  28.2 22.4 %collective-permute-start.5 = (bf16[12,64,128]{2,1,0:T(8,128)(2,1)}, bf16[12,64,128]{2,1,0:T(8,128)(2,1)}, u32[]{:S(2)}, u32[]{:S(2)}) collective-permute-start(bf16[12,64,128]{2,1,0:T(8,128)(2,1)} %get-tuple-element.41), channel_id=1, source_target_pairs={{0,2},{1,3},{2,0},{3,1},{4,6},{5,7},{6,4},{7,5},{8,10},{9,11},{10,... | collective-permute-start | bytes 589832 | tf_op jit(solution)/shard_map/ppermute | solution.py:26
  30.0 21.4 %collective-permute-start.6 = (bf16[12,64,128]{2,1,0:T(8,128)(2,1)}, bf16[12,64,128]{2,1,0:T(8,128)(2,1)}, u32[]{:S(2)}, u32[]{:S(2)}) collective-permute-start(bf16[12,64,128]{2,1,0:T(8,128)(2,1)} %get-tuple-element.42), channel_id=1, source_target_pairs={{0,4},{1,5},{2,6},{3,7},{4,0},{5,1},{6,2},{7,3},{8,12},{9,13},{10,... | collective-permute-start | bytes 589832 | tf_op jit(solution)/shard_map/ppermute | solution.py:26
  31.5 32.2 %collective-permute-start.7 = (bf16[12,64,128]{2,1,0:T(8,128)(2,1)}, bf16[12,64,128]{2,1,0:T(8,128)(2,1)}, u32[]{:S(2)}, u32[]{:S(2)}) collective-permute-start(bf16[12,64,128]{2,1,0:T(8,128)(2,1)} %get-tuple-element.43), channel_id=1, source_target_pairs={{0,6},{1,7},{2,4},{3,5},{4,2},{5,3},{6,0},{7,1},{8,14},{9,15},{10,... | collective-permute-start | bytes 589832 | tf_op jit(solution)/shard_map/ppermute | solution.py:26
  64.6 17.2 %collective-permute-start.8 = (bf16[16,64,128]{2,1,0:T(8,128)(2,1)S(1)}, bf16[16,64,128]{2,1,0:T(8,128)(2,1)S(1)}, u32[]{:S(2)}, u32[]{:S(2)}) collective-permute-start(bf16[16,64,128]{2,1,0:T(8,128)(2,1)S(1)} %pad_maximum_fusion), channel_id=1, source_target_pairs={{0,8},{8,0},{16,24},{24,16},{1,9},{9,1},{17,25},{25,17},{2,10},{10... | collective-permute-start | bytes 786440 | tf_op jit(solution)/shard_map/ppermute | solution.py:26
  104.1 2.8 %collective-permute-start.9 = (bf16[4,17,64,128]{3,2,1,0:T(8,128)(2,1)S(1)}, bf16[4,17,64,128]{3,2,1,0:T(8,128)(2,1)S(1)}, u32[]{:S(2)}, u32[]{:S(2)}) collective-permute-start(bf16[4,17,64,128]{3,2,1,0:T(8,128)(2,1)S(1)} %get-tuple-element.47), channel_id=1, source_target_pairs={{0,1},{1,0},{2,3},{3,2},{4,5},{5,4},{6,7},{7,6},{8,9},{9,8},{10,11... | collective-permute-start | bytes 3342344 | tf_op jit(solution)/shard_map/ppermute | solution.py:26
  107.3 9.6 %collective-permute-start.10 = (bf16[17,64,128]{2,1,0:T(8,128)(2,1)S(1)}, bf16[17,64,128]{2,1,0:T(8,128)(2,1)S(1)}, u32[]{:S(2)}, u32[]{:S(2)}) collective-permute-start(bf16[17,64,128]{2,1,0:T(8,128)(2,1)S(1)} %get-tuple-element.49), channel_id=1, source_target_pairs={{0,2},{1,3},{2,0},{3,1},{4,6},{5,7},{6,4},{7,5},{8,10},{9,11},{10,... | collective-permute-start | bytes 835592 | tf_op jit(solution)/shard_map/ppermute | solution.py:26
  108.3 14.4 %collective-permute-start.11 = (bf16[17,64,128]{2,1,0:T(8,128)(2,1)S(1)}, bf16[17,64,128]{2,1,0:T(8,128)(2,1)S(1)}, u32[]{:S(2)}, u32[]{:S(2)}) collective-permute-start(bf16[17,64,128]{2,1,0:T(8,128)(2,1)S(1)} %get-tuple-element.50), channel_id=1, source_target_pairs={{0,4},{1,5},{2,6},{3,7},{4,0},{5,1},{6,2},{7,3},{8,12},{9,13},{10,... | collective-permute-start | bytes 835592 | tf_op jit(solution)/shard_map/ppermute | solution.py:26
  109.8 12.9 %collective-permute-start.12 = (bf16[17,64,128]{2,1,0:T(8,128)(2,1)S(1)}, bf16[17,64,128]{2,1,0:T(8,128)(2,1)S(1)}, u32[]{:S(2)}, u32[]{:S(2)}) collective-permute-start(bf16[17,64,128]{2,1,0:T(8,128)(2,1)S(1)} %get-tuple-element.51), channel_id=1, source_target_pairs={{0,6},{1,7},{2,4},{3,5},{4,2},{5,3},{6,0},{7,1},{8,14},{9,15},{10,... | collective-permute-start | bytes 835592 | tf_op jit(solution)/shard_map/ppermute | solution.py:26
  122.9 10.7 %collective-permute-start.13 = (bf16[8,64,128]{2,1,0:T(8,128)(2,1)S(1)}, bf16[8,64,128]{2,1,0:T(8,128)(2,1)S(1)}, u32[]{:S(2)}, u32[]{:S(2)}) collective-permute-start(bf16[8,64,128]{2,1,0:T(8,128)(2,1)S(1)} %get-tuple-element.53.rest_7_), channel_id=1, source_target_pairs={{0,16},{8,24},{16,0},{24,8},{1,17},{9,25},{17,1},{25,9},{2,18},{10... | collective-permute-start | bytes 393224 | tf_op jit(solution)/shard_map/ppermute | solution.py:26
  123.0 13.3 %collective-permute-start.20 = (bf16[8,64,128]{2,1,0:T(8,128)(2,1)S(1)}, bf16[8,64,128]{2,1,0:T(8,128)(2,1)S(1)}, u32[]{:S(2)}, u32[]{:S(2)}) collective-permute-start(bf16[8,64,128]{2,1,0:T(8,128)(2,1)S(1)} %get-tuple-element.54.rest_8_), channel_id=1, source_target_pairs={{0,16},{8,24},{16,0},{24,8},{1,17},{9,25},{17,1},{25,9},{2,18},{10... | collective-permute-start | bytes 393224 | tf_op jit(solution)/shard_map/ppermute | solution.py:26
  125.9 12.2 %collective-permute-start.18 = (bf16[8,64,128]{2,1,0:T(8,128)(2,1)S(1)}, bf16[8,64,128]{2,1,0:T(8,128)(2,1)S(1)}, u32[]{:S(2)}, u32[]{:S(2)}) collective-permute-start(bf16[8,64,128]{2,1,0:T(8,128)(2,1)S(1)} %get-tuple-element.53.rest_7_), channel_id=1, source_target_pairs={{0,8},{8,0},{16,24},{24,16},{1,9},{9,1},{17,25},{25,17},{2,10},{10... | collective-permute-start | bytes 393224 | tf_op jit(solution)/shard_map/ppermute | solution.py:26
  125.9 13.6 %collective-permute-start.19 = (bf16[8,64,128]{2,1,0:T(8,128)(2,1)S(1)}, bf16[8,64,128]{2,1,0:T(8,128)(2,1)S(1)}, u32[]{:S(2)}, u32[]{:S(2)}) collective-permute-start(bf16[8,64,128]{2,1,0:T(8,128)(2,1)S(1)} %get-tuple-element.54.rest_8_), channel_id=1, source_target_pairs={{0,8},{8,0},{16,24},{24,16},{1,9},{9,1},{17,25},{25,17},{2,10},{10... | collective-permute-start | bytes 393224 | tf_op jit(solution)/shard_map/ppermute | solution.py:26
  134.6 8.9 %collective-permute-start.21 = (bf16[8,64,128]{2,1,0:T(8,128)(2,1)S(1)}, bf16[8,64,128]{2,1,0:T(8,128)(2,1)S(1)}, u32[]{:S(2)}, u32[]{:S(2)}) collective-permute-start(bf16[8,64,128]{2,1,0:T(8,128)(2,1)S(1)} %collective-permute-done.13.mark.rest_11_), channel_id=1, source_target_pairs={{0,8},{8,0},{16,24},{24,16},{1,9},{9,1},{17,25},{25,17},{2,10},{10... | collective-permute-start | bytes 393224 | tf_op jit(solution)/shard_map/ppermute | solution.py:26
  136.3 7.5 %collective-permute-start.22 = (bf16[8,64,128]{2,1,0:T(8,128)(2,1)S(1)}, bf16[8,64,128]{2,1,0:T(8,128)(2,1)S(1)}, u32[]{:S(2)}, u32[]{:S(2)}) collective-permute-start(bf16[8,64,128]{2,1,0:T(8,128)(2,1)S(1)} %collective-permute-done.20.rest_12_), channel_id=1, source_target_pairs={{0,8},{8,0},{16,24},{24,16},{1,9},{9,1},{17,25},{25,17},{2,10},{10... | collective-permute-start | bytes 393224 | tf_op jit(solution)/shard_map/ppermute | solution.py:26
  136.7 4.9 %collective-permute-start.17 = (f32[64,64]{1,0:T(8,128)S(1)}, f32[64,64]{1,0:T(8,128)S(1)}, u32[]{:S(2)}, u32[]{:S(2)}) collective-permute-start(f32[64,64]{1,0:T(8,128)S(1)} %add.74.rest_1_), channel_id=1, source_target_pairs={{0,6},{1,7},{2,4},{3,5},{4,2},{5,3},{6,0},{7,1},{8,14},{9,15},{10,... | collective-permute-start | bytes 49160 | tf_op jit(solution)/shard_map/ppermute | solution.py:26
  138.1 3.9 %collective-permute-start.16 = (f32[64,64]{1,0:T(8,128)S(1)}, f32[64,64]{1,0:T(8,128)S(1)}, u32[]{:S(2)}, u32[]{:S(2)}) collective-permute-start(f32[64,64]{1,0:T(8,128)S(1)} %add.74.rest_1_), channel_id=1, source_target_pairs={{0,4},{1,5},{2,6},{3,7},{4,0},{5,1},{6,2},{7,3},{8,12},{9,13},{10,... | collective-permute-start | bytes 49160 | tf_op jit(solution)/shard_map/ppermute | solution.py:26
  139.5 3.9 %collective-permute-start.15 = (f32[64,64]{1,0:T(8,128)S(1)}, f32[64,64]{1,0:T(8,128)S(1)}, u32[]{:S(2)}, u32[]{:S(2)}) collective-permute-start(f32[64,64]{1,0:T(8,128)S(1)} %add.74.rest_1_), channel_id=1, source_target_pairs={{0,2},{1,3},{2,0},{3,1},{4,6},{5,7},{6,4},{7,5},{8,10},{9,11},{10,... | collective-permute-start | bytes 49160 | tf_op jit(solution)/shard_map/ppermute | solution.py:26
  149.4 2.7 %collective-permute-start.23 = (bf16[4,16,64,128]{3,2,1,0:T(8,128)(2,1)S(1)}, bf16[4,16,64,128]{3,2,1,0:T(8,128)(2,1)S(1)}, u32[]{:S(2)}, u32[]{:S(2)}) collective-permute-start(bf16[4,16,64,128]{3,2,1,0:T(8,128)(2,1)S(1)} %get-tuple-element.56), channel_id=1, source_target_pairs={{0,1},{1,0},{2,3},{3,2},{4,5},{5,4},{6,7},{7,6},{8,9},{9,8},{10,11... | collective-permute-start | bytes 3145736 | tf_op jit(solution)/shard_map/ppermute | solution.py:26
  152.4 15.1 %collective-permute-start.27 = (bf16[16,64,128]{2,1,0:T(8,128)(2,1)S(1)}, bf16[16,64,128]{2,1,0:T(8,128)(2,1)S(1)}, u32[]{:S(2)}, u32[]{:S(2)}) collective-permute-start(bf16[16,64,128]{2,1,0:T(8,128)(2,1)S(1)} %get-tuple-element.60), channel_id=1, source_target_pairs={{0,2},{1,3},{2,0},{3,1},{4,6},{5,7},{6,4},{7,5},{8,10},{9,11},{10,... | collective-permute-start | bytes 786440 | tf_op jit(solution)/shard_map/ppermute | solution.py:26
  153.9 13.7 %collective-permute-start.28 = (bf16[16,64,128]{2,1,0:T(8,128)(2,1)S(1)}, bf16[16,64,128]{2,1,0:T(8,128)(2,1)S(1)}, u32[]{:S(2)}, u32[]{:S(2)}) collective-permute-start(bf16[16,64,128]{2,1,0:T(8,128)(2,1)S(1)} %get-tuple-element.61), channel_id=1, source_target_pairs={{0,4},{1,5},{2,6},{3,7},{4,0},{5,1},{6,2},{7,3},{8,12},{9,13},{10,... | collective-permute-start | bytes 786440 | tf_op jit(solution)/shard_map/ppermute | solution.py:26
  154.5 13.0 %collective-permute-start.29 = (bf16[16,64,128]{2,1,0:T(8,128)(2,1)S(1)}, bf16[16,64,128]{2,1,0:T(8,128)(2,1)S(1)}, u32[]{:S(2)}, u32[]{:S(2)}) collective-permute-start(bf16[16,64,128]{2,1,0:T(8,128)(2,1)S(1)} %get-tuple-element.62), channel_id=1, source_target_pairs={{0,6},{1,7},{2,4},{3,5},{4,2},{5,3},{6,0},{7,1},{8,14},{9,15},{10,... | collective-permute-start | bytes 786440 | tf_op jit(solution)/shard_map/ppermute | solution.py:26
  156.0 5.7 %collective-permute-start.26 = (f32[64,64]{1,0:T(8,128)S(1)}, f32[64,64]{1,0:T(8,128)S(1)}, u32[]{:S(2)}, u32[]{:S(2)}) collective-permute-start(f32[64,64]{1,0:T(8,128)S(1)} %get-tuple-element.59.refs_0_), channel_id=1, source_target_pairs={{0,24},{8,16},{16,8},{24,0},{1,25},{9,17},{17,9},{25,1},{2,26},{10... | collective-permute-start | bytes 49160 | tf_op jit(solution)/shard_map/ppermute | solution.py:26
  157.9 5.0 %collective-permute-start.25 = (f32[64,64]{1,0:T(8,128)S(1)}, f32[64,64]{1,0:T(8,128)S(1)}, u32[]{:S(2)}, u32[]{:S(2)}) collective-permute-start(f32[64,64]{1,0:T(8,128)S(1)} %get-tuple-element.59.refs_0_), channel_id=1, source_target_pairs={{0,16},{8,24},{16,0},{24,8},{1,17},{9,25},{17,1},{25,9},{2,18},{10... | collective-permute-start | bytes 49160 | tf_op jit(solution)/shard_map/ppermute | solution.py:26
  161.7 3.9 %collective-permute-start.24 = (f32[64,64]{1,0:T(8,128)S(1)}, f32[64,64]{1,0:T(8,128)S(1)}, u32[]{:S(2)}, u32[]{:S(2)}) collective-permute-start(f32[64,64]{1,0:T(8,128)S(1)} %get-tuple-element.59.refs_0_), channel_id=1, source_target_pairs={{0,8},{8,0},{16,24},{24,16},{1,9},{9,1},{17,25},{25,17},{2,10},{10... | collective-permute-start | bytes 49160 | tf_op jit(solution)/shard_map/ppermute | solution.py:26
  168.6 11.1 %collective-permute-start.30 = (bf16[8,64,128]{2,1,0:T(8,128)(2,1)S(1)}, bf16[8,64,128]{2,1,0:T(8,128)(2,1)S(1)}, u32[]{:S(2)}, u32[]{:S(2)}) collective-permute-start(bf16[8,64,128]{2,1,0:T(8,128)(2,1)S(1)} %get-tuple-element.64.rest_7_), channel_id=1, source_target_pairs={{0,16},{8,24},{16,0},{24,8},{1,17},{9,25},{17,1},{25,9},{2,18},{10... | collective-permute-start | bytes 393224 | tf_op jit(solution)/shard_map/ppermute | solution.py:26
  169.6 12.6 %collective-permute-start.37 = (bf16[8,64,128]{2,1,0:T(8,128)(2,1)S(1)}, bf16[8,64,128]{2,1,0:T(8,128)(2,1)S(1)}, u32[]{:S(2)}, u32[]{:S(2)}) collective-permute-start(bf16[8,64,128]{2,1,0:T(8,128)(2,1)S(1)} %get-tuple-element.65.rest_8_), channel_id=1, source_target_pairs={{0,16},{8,24},{16,0},{24,8},{1,17},{9,25},{17,1},{25,9},{2,18},{10... | collective-permute-start | bytes 393224 | tf_op jit(solution)/shard_map/ppermute | solution.py:26
  171.6 14.6 %collective-permute-start.35 = (bf16[8,64,128]{2,1,0:T(8,128)(2,1)S(1)}, bf16[8,64,128]{2,1,0:T(8,128)(2,1)S(1)}, u32[]{:S(2)}, u32[]{:S(2)}) collective-permute-start(bf16[8,64,128]{2,1,0:T(8,128)(2,1)S(1)} %get-tuple-element.64.rest_7_), channel_id=1, source_target_pairs={{0,8},{8,0},{16,24},{24,16},{1,9},{9,1},{17,25},{25,17},{2,10},{10... | collective-permute-start | bytes 393224 | tf_op jit(solution)/shard_map/ppermute | solution.py:26
  172.2 14.7 %collective-permute-start.36 = (bf16[8,64,128]{2,1,0:T(8,128)(2,1)S(1)}, bf16[8,64,128]{2,1,0:T(8,128)(2,1)S(1)}, u32[]{:S(2)}, u32[]{:S(2)}) collective-permute-start(bf16[8,64,128]{2,1,0:T(8,128)(2,1)S(1)} %get-tuple-element.65.rest_8_), channel_id=1, source_target_pairs={{0,8},{8,0},{16,24},{24,16},{1,9},{9,1},{17,25},{25,17},{2,10},{10... | collective-permute-start | bytes 393224 | tf_op jit(solution)/shard_map/ppermute | solution.py:26
  179.7 11.2 %collective-permute-start.38 = (bf16[8,64,128]{2,1,0:T(8,128)(2,1)S(1)}, bf16[8,64,128]{2,1,0:T(8,128)(2,1)S(1)}, u32[]{:S(2)}, u32[]{:S(2)}) collective-permute-start(bf16[8,64,128]{2,1,0:T(8,128)(2,1)S(1)} %collective-permute-done.30.mark.rest_11_), channel_id=1, source_target_pairs={{0,8},{8,0},{16,24},{24,16},{1,9},{9,1},{17,25},{25,17},{2,10},{10... | collective-permute-start | bytes 393224 | tf_op jit(solution)/shard_map/ppermute | solution.py:26
  182.2 8.6 %collective-permute-start.39 = (bf16[8,64,128]{2,1,0:T(8,128)(2,1)S(1)}, bf16[8,64,128]{2,1,0:T(8,128)(2,1)S(1)}, u32[]{:S(2)}, u32[]{:S(2)}) collective-permute-start(bf16[8,64,128]{2,1,0:T(8,128)(2,1)S(1)} %collective-permute-done.37.rest_12_), channel_id=1, source_target_pairs={{0,8},{8,0},{16,24},{24,16},{1,9},{9,1},{17,25},{25,17},{2,10},{10... | collective-permute-start | bytes 393224 | tf_op jit(solution)/shard_map/ppermute | solution.py:26
  184.4 4.9 %collective-permute-start.34 = (f32[64,64]{1,0:T(8,128)S(1)}, f32[64,64]{1,0:T(8,128)S(1)}, u32[]{:S(2)}, u32[]{:S(2)}) collective-permute-start(f32[64,64]{1,0:T(8,128)S(1)} %add.75.rest_1_), channel_id=1, source_target_pairs={{0,6},{1,7},{2,4},{3,5},{4,2},{5,3},{6,0},{7,1},{8,14},{9,15},{10,... | collective-permute-start | bytes 49160 | tf_op jit(solution)/shard_map/ppermute | solution.py:26
  186.2 3.9 %collective-permute-start.33 = (f32[64,64]{1,0:T(8,128)S(1)}, f32[64,64]{1,0:T(8,128)S(1)}, u32[]{:S(2)}, u32[]{:S(2)}) collective-permute-start(f32[64,64]{1,0:T(8,128)S(1)} %add.75.rest_1_), channel_id=1, source_target_pairs={{0,4},{1,5},{2,6},{3,7},{4,0},{5,1},{6,2},{7,3},{8,12},{9,13},{10,... | collective-permute-start | bytes 49160 | tf_op jit(solution)/shard_map/ppermute | solution.py:26
  186.9 3.9 %collective-permute-start.32 = (f32[64,64]{1,0:T(8,128)S(1)}, f32[64,64]{1,0:T(8,128)S(1)}, u32[]{:S(2)}, u32[]{:S(2)}) collective-permute-start(f32[64,64]{1,0:T(8,128)S(1)} %add.75.rest_1_), channel_id=1, source_target_pairs={{0,2},{1,3},{2,0},{3,1},{4,6},{5,7},{6,4},{7,5},{8,10},{9,11},{10,... | collective-permute-start | bytes 49160 | tf_op jit(solution)/shard_map/ppermute | solution.py:26
  199.1 15.1 %collective-permute-start.44 = (bf16[16,64,128]{2,1,0:T(8,128)(2,1)S(1)}, bf16[16,64,128]{2,1,0:T(8,128)(2,1)S(1)}, u32[]{:S(2)}, u32[]{:S(2)}) collective-permute-start(bf16[16,64,128]{2,1,0:T(8,128)(2,1)S(1)} %get-tuple-element.70), channel_id=1, source_target_pairs={{0,2},{1,3},{2,0},{3,1},{4,6},{5,7},{6,4},{7,5},{8,10},{9,11},{10,... | collective-permute-start | bytes 786440 | tf_op jit(solution)/shard_map/ppermute | solution.py:26
  200.2 14.1 %collective-permute-start.45 = (bf16[16,64,128]{2,1,0:T(8,128)(2,1)S(1)}, bf16[16,64,128]{2,1,0:T(8,128)(2,1)S(1)}, u32[]{:S(2)}, u32[]{:S(2)}) collective-permute-start(bf16[16,64,128]{2,1,0:T(8,128)(2,1)S(1)} %get-tuple-element.71), channel_id=1, source_target_pairs={{0,4},{1,5},{2,6},{3,7},{4,0},{5,1},{6,2},{7,3},{8,12},{9,13},{10,... | collective-permute-start | bytes 786440 | tf_op jit(solution)/shard_map/ppermute | solution.py:26
  201.3 13.0 %collective-permute-start.46 = (bf16[16,64,128]{2,1,0:T(8,128)(2,1)S(1)}, bf16[16,64,128]{2,1,0:T(8,128)(2,1)S(1)}, u32[]{:S(2)}, u32[]{:S(2)}) collective-permute-start(bf16[16,64,128]{2,1,0:T(8,128)(2,1)S(1)} %get-tuple-element.72), channel_id=1, source_target_pairs={{0,6},{1,7},{2,4},{3,5},{4,2},{5,3},{6,0},{7,1},{8,14},{9,15},{10,... | collective-permute-start | bytes 786440 | tf_op jit(solution)/shard_map/ppermute | solution.py:26
  202.7 5.8 %collective-permute-start.43 = (f32[64,64]{1,0:T(8,128)S(1)}, f32[64,64]{1,0:T(8,128)S(1)}, u32[]{:S(2)}, u32[]{:S(2)}) collective-permute-start(f32[64,64]{1,0:T(8,128)S(1)} %get-tuple-element.69.refs_0_), channel_id=1, source_target_pairs={{0,24},{8,16},{16,8},{24,0},{1,25},{9,17},{17,9},{25,1},{2,26},{10... | collective-permute-start | bytes 49160 | tf_op jit(solution)/shard_map/ppermute | solution.py:26
  204.5 4.8 %collective-permute-start.42 = (f32[64,64]{1,0:T(8,128)S(1)}, f32[64,64]{1,0:T(8,128)S(1)}, u32[]{:S(2)}, u32[]{:S(2)}) collective-permute-start(f32[64,64]{1,0:T(8,128)S(1)} %get-tuple-element.69.refs_0_), channel_id=1, source_target_pairs={{0,16},{8,24},{16,0},{24,8},{1,17},{9,25},{17,1},{25,9},{2,18},{10... | collective-permute-start | bytes 49160 | tf_op jit(solution)/shard_map/ppermute | solution.py:26
  208.4 3.9 %collective-permute-start.41 = (f32[64,64]{1,0:T(8,128)S(1)}, f32[64,64]{1,0:T(8,128)S(1)}, u32[]{:S(2)}, u32[]{:S(2)}) collective-permute-start(f32[64,64]{1,0:T(8,128)S(1)} %get-tuple-element.69.refs_0_), channel_id=1, source_target_pairs={{0,8},{8,0},{16,24},{24,16},{1,9},{9,1},{17,25},{25,17},{2,10},{10... | collective-permute-start | bytes 49160 | tf_op jit(solution)/shard_map/ppermute | solution.py:26
  218.1 4.8 %collective-permute-start.50 = (f32[64,64]{1,0:T(8,128)S(1)}, f32[64,64]{1,0:T(8,128)S(1)}, u32[]{:S(2)}, u32[]{:S(2)}) collective-permute-start(f32[64,64]{1,0:T(8,128)S(1)} %add.76), channel_id=1, source_target_pairs={{0,6},{1,7},{2,4},{3,5},{4,2},{5,3},{6,0},{7,1},{8,14},{9,15},{10,... | collective-permute-start | bytes 49160 | tf_op jit(solution)/shard_map/ppermute | solution.py:26
  219.6 3.9 %collective-permute-start.49 = (f32[64,64]{1,0:T(8,128)S(1)}, f32[64,64]{1,0:T(8,128)S(1)}, u32[]{:S(2)}, u32[]{:S(2)}) collective-permute-start(f32[64,64]{1,0:T(8,128)S(1)} %add.76), channel_id=1, source_target_pairs={{0,4},{1,5},{2,6},{3,7},{4,0},{5,1},{6,2},{7,3},{8,12},{9,13},{10,... | collective-permute-start | bytes 49160 | tf_op jit(solution)/shard_map/ppermute | solution.py:26
  220.6 3.9 %collective-permute-start.48 = (f32[64,64]{1,0:T(8,128)S(1)}, f32[64,64]{1,0:T(8,128)S(1)}, u32[]{:S(2)}, u32[]{:S(2)}) collective-permute-start(f32[64,64]{1,0:T(8,128)S(1)} %add.76), channel_id=1, source_target_pairs={{0,2},{1,3},{2,0},{3,1},{4,6},{5,7},{6,4},{7,5},{8,10},{9,11},{10,... | collective-permute-start | bytes 49160 | tf_op jit(solution)/shard_map/ppermute | solution.py:26
  224.5 5.8 %collective-permute-start.53 = (f32[64,64]{1,0:T(8,128)S(1)}, f32[64,64]{1,0:T(8,128)S(1)}, u32[]{:S(2)}, u32[]{:S(2)}) collective-permute-start(f32[64,64]{1,0:T(8,128)S(1)} %add_add_fusion.refs_0_), channel_id=1, source_target_pairs={{0,24},{8,16},{16,8},{24,0},{1,25},{9,17},{17,9},{25,1},{2,26},{10... | collective-permute-start | bytes 49160 | tf_op jit(solution)/shard_map/ppermute | solution.py:26
  226.5 5.3 %collective-permute-start.52 = (f32[64,64]{1,0:T(8,128)S(1)}, f32[64,64]{1,0:T(8,128)S(1)}, u32[]{:S(2)}, u32[]{:S(2)}) collective-permute-start(f32[64,64]{1,0:T(8,128)S(1)} %add_add_fusion.refs_0_), channel_id=1, source_target_pairs={{0,16},{8,24},{16,0},{24,8},{1,17},{9,25},{17,1},{25,9},{2,18},{10... | collective-permute-start | bytes 49160 | tf_op jit(solution)/shard_map/ppermute | solution.py:26
  227.7 4.1 %collective-permute-start.51 = (f32[64,64]{1,0:T(8,128)S(1)}, f32[64,64]{1,0:T(8,128)S(1)}, u32[]{:S(2)}, u32[]{:S(2)}) collective-permute-start(f32[64,64]{1,0:T(8,128)S(1)} %add_add_fusion.refs_0_), channel_id=1, source_target_pairs={{0,8},{8,0},{16,24},{24,16},{1,9},{9,1},{17,25},{25,17},{2,10},{10... | collective-permute-start | bytes 49160 | tf_op jit(solution)/shard_map/ppermute | solution.py:26
  (14 other events, 117.1 us)

commit v5 on v4

--- a/solution.py
+++ b/solution.py
@@ -179,7 +179,7 @@
         total[own_rows[i]] += jnp.dot(x_block(own_x[i]), value, preferred_element_type=F32)
         return carry
 
-    lax.fori_loop(0, tile_count, add_own, 0, unroll=8)
+    lax.fori_loop(0, tile_count, add_own, 0, unroll=64)
     if first:
         numbers_copy.wait()
 
@@ -192,7 +192,7 @@
             total[row] += jnp.dot(x_block(block), value, preferred_element_type=F32)
         return carry
 
-    lax.fori_loop(0, taken.shape[0], add_taken, 0, unroll=4)
+    lax.fori_loop(0, taken.shape[0], add_taken, 0, unroll=16 if first else 32)
 
     def write(mine):
         lane = lax.broadcasted_iota(jnp.int32, total.shape[1:], 1) // sub
@@ -218,9 +218,9 @@
             return carry
 
         if by_column:
-            lax.fori_loop(0, row_size, regroup, 0)
+            lax.fori_loop(0, row_size, regroup, 0, unroll=2)
         else:
-            lax.fori_loop(0, per_device, straight, 0)
+            lax.fori_loop(0, per_device, straight, 0, unroll=4)
         if not first:
             return
         lane = lax.broadcasted_iota(jnp.int32, (row_size, tile), 1) // sub
@@ -268,46 +268,59 @@
         for i in range(2):
             degrees[i] = 1.0 + sum(one_part(part, 2 * i * per_device, per_device) for part in parts)
         degree = degrees.at[0]
-        gram = jnp.zeros((1, 1), F32)
     else:
         degrees, inverse, rest = rest[0], rest[1], rest[2:]
         made = 1 if last else PARTS
         received, (*out, scaled) = rest[: -1 - made], rest[-1 - made :]
         degree = degrees.at[1 if last else 0]
-        gram = jnp.zeros(inverse.shape, F32)
 
     size = scaled.shape[0] // PARTS
 
-    def add(b, gram, part=0):
+    def add(b, carry, part=0):
         total = own[b]
         for piece in received:
             total = total + piece[b].astype(F32)
         total = total / degree[pl.ds(b, 1), :]
         if normalize:
-            total = jnp.dot(inverse[...], total, precision=lax.Precision.HIGHEST, preferred_element_type=F32)
+            total = split_dot(inverse[...], total)
         scaled[b] = total
-        if last:
-            return gram + lax.dot_general(
-                total, total, (((1,), (1,)), ((), ())), precision=lax.Precision.HIGHEST, preferred_element_type=F32
-            )
-        out[part][b - part * size] = total.astype(BF16)
-        return gram
+        if not last:
+            out[part][b - part * size] = total.astype(BF16)
+        return carry
 
     if last:
-        out[0][...] = lax.fori_loop(0, scaled.shape[0], add, gram, unroll=scaled.shape[0])
+        lax.fori_loop(0, scaled.shape[0], add, 0, unroll=scaled.shape[0])
+        out[0][...] = gram_of(scaled)
         return
     for part in range(PARTS):
-        lax.fori_loop(part * size, (part + 1) * size, functools.partial(add, part=part), gram, unroll=4)
+        lax.fori_loop(part * size, (part + 1) * size, functools.partial(add, part=part), 0, unroll=size)
+
+
+def split_dot(left, right):
+    (left_high, left_low), (right_high, right_low) = two_parts(left), two_parts(right)
+    both = jnp.concatenate([left_high, left_low], axis=0)
+    upper = jnp.dot(both, right_high, preferred_element_type=F32)
+    lower = jnp.dot(left_high, right_low, preferred_element_type=F32)
+    return upper[: left.shape[0]] + (upper[left.shape[0] :] + lower)
+
+
+def gram_of(scaled):
+    features = scaled.shape[1]
+    contract = (((1,), (1,)), ((), ()))
+    with_first, second = jnp.zeros((3 * features, features), F32), jnp.zeros((features, features), F32)
+    for b in range(scaled.shape[0]):
+        value = scaled[b]
+        high = value.astype(BF16)
+        middle, low = two_parts(value - high.astype(F32))
+        parts = jnp.concatenate([high, middle, low], axis=0)
+        with_first = with_first + lax.dot_general(parts, high, contract, preferred_element_type=F32)
+        second = second + lax.dot_general(middle, middle, contract, preferred_element_type=F32)
+    cross = with_first[features : 2 * features] + with_first[2 * features :]
+    return with_first[:features] + (cross + cross.T) + second
 
 
 def gram_kernel(scaled, mark, gram):
-    total = jnp.zeros(gram.shape, F32)
-    for b in range(scaled.shape[0]):
-        block = scaled[b]
-        total = total + lax.dot_general(
-            block, block, (((1,), (1,)), ((), ())), precision=lax.Precision.HIGHEST, preferred_element_type=F32
-        )
-    gram[...] = total
+    gram[...] = gram_of(scaled)
 
 
 def inverse_factor(gram):
@@ -348,9 +361,7 @@
     inverse = inverse_factor(sum(g[...] for g in grams) / nodes)
     tile = scaled.shape[2]
     for b in range(scaled.shape[0]):
-        out[:, b * tile : (b + 1) * tile] = jnp.dot(
-            inverse, scaled[b], precision=lax.Precision.HIGHEST, preferred_element_type=F32
-        )
+        out[:, b * tile : (b + 1) * tile] = split_dot(inverse, scaled[b])
 
 
 def params(limit=LIMIT):

time: 236 us -> 226 us (0.958)
  Pallas kernels: 39.4 us -> 30.1 us
    pallas_call x3, Pallas kernels: 16.4 us -> 10.5 us  [local(): pl.pallas_call(functools.partial(product_kernel, not last, first, sub, pe...]
    pallas_call x3, Pallas kernels: 3.75 us -> 1.31 us  [local(): pl.pallas_call(functools.partial(scale_kernel, not first, last, first), o...]
  transfers between devices with their start and end apart: 55 -> 55, of which waited for: 38 -> 39; matrix products, arithmetic and copies ran while one was open for 1% -> 1% of each run, Pallas kernels for 6% -> 6%
where the time goes in v5:
time: 226 us
  waiting for transfers between devices  127 us (56%)
  starting transfers between devices  59.2 us (26%)
  Pallas kernels  30.1 us (13%)
  local copies, waits for them, and re-layouts  8.72 us (4%)
    ppermute x54, waiting for transfers between devices, exchange(): return lax.ppermute(value, axis, [(i, i ^ distance) for i in range(size)])  119 us
    ppermute x54, starting transfers between devices, exchange(): return lax.ppermute(value, axis, [(i, i ^ distance) for i in range(size)])  53.7 us
    pallas_call x3, Pallas kernels, local(): pl.pallas_call(functools.partial(product_kernel, not last, first, sub, pe...  10.5 us
    all_to_all x1, waiting for transfers between devices, local(): lax.all_to_all(slots, ('row', 'col'), split_axis=0, concat_axis=0, tiled=...  8.72 us
    unnamed x14, local copies, waits for them, and re-layouts  6.18 us
    all_to_all x1, starting transfers between devices, local(): lax.all_to_all(slots, ('row', 'col'), split_axis=0, concat_axis=0, tiled=...  5.5 us
  transfers between devices with their start and end apart: 55, of which 39 were waited for; matrix products, arithmetic and copies ran while one was open for 1% of the time, Pallas kernels for 6%

profile of v5, /device:TPU:0, one launch (start us, length us, event | category | flops | bytes accessed | tf_op | source)
XLA Modules:
  0.0 225.9 jit_solution(8688874572358017252)
XLA Ops:
  0.0 4.0 %collective-permute-start.3 = (bf16[64,2048]{1,0:T(8,128)(2,1)}, bf16[64,2048]{1,0:T(8,128)(2,1)}, u32[]{:S(2)}, u32[]{:S(2)}) collective-permute-start(bf16[64,2048]{1,0:T(8,128)(2,1)} %bitcast.6), channel_id=1, source_target_pairs={{0,16},{8,24},{16,0},{24,8},{1,17},{9,25},{17,1},{25,9},{2,18},{10... | collective-permute-start | bytes 786440 | tf_op jit(solution)/shard_map/ppermute | solution.py:26
  4.0 1.6 collective-permute-start.1
  5.6 4.1 %pack.1 = bf16[32,400,128]{2,1,0:T(8,128)(2,1)} custom-call(s32[48]{0:T(128)} %rows_in.1, s32[48]{0:T(128)} %cols_in.1, bf16[48,128,128]{2,1,0:T(8,128)(2,1)} %chg.1), custom_call_target="tpu_custom_call" | custom-call | tf_op jit(solution)/shard_map/pack/pallas_call | solution.py:401
  9.8 6.6 %collective-permute-done.3.refs_4_ = bf16[64,2048]{1,0:T(8,128)(2,1)} collective-permute-done((bf16[64,2048]{1,0:T(8,128)(2,1)}, bf16[64,2048]{1,0:T(8,128)(2,1)}, u32[]{:S(2)}, u32[]{:S(2)}) %collective-permute-start.3) | collective-permute-done | bytes 262176 | tf_op jit(solution)/shard_map/ppermute | solution.py:26
  16.6 5.5 %all-to-all-start = ((bf16[32,400,128]{2,1,0:T(8,128)(2,1)}), bf16[32,400,128]{2,1,0:T(8,128)(2,1)S(1)}, u32[]{:S(2)}, u32[]{:S(2)}) async-start(bf16[32,400,128]{2,1,0:T(8,128)(2,1)} %pack.1), calls=%async_computation | async-start | bytes 6553600 | tf_op jit(solution)/shard_map/all_to_all | solution.py:439
  25.8 2.5 %merge.1 = (bf16[12,64,128]{2,1,0:T(8,128)(2,1)S(1)}, bf16[12,64,128]{2,1,0:T(8,128)(2,1)}, bf16[12,64,128]{2,1,0:T(8,128)(2,1)}, bf16[12,64,128]{2,1,0:T(8,128)(2,1)}) custom-call(s32[1]{0:T(128)} %bitcast.3.place, bf16[64,2048]{1,0:T(8,128)(2,1)S(1)} %bitcast.9, bf16[64,2048]{1,0:T(8,128)(2,1)} %collective-permute-done.refs_1_, ...), custom_call_target="tpu_custom_call" | custom-call | tf_op jit(solution)/shard_map/merge/pallas_call | solution.py:417
  28.2 1.8 collective-permute-start.5
  30.0 1.5 collective-permute-start.6
  31.7 18.9 %collective-permute-done.5.refs_1_ = bf16[12,64,128]{2,1,0:T(8,128)(2,1)} collective-permute-done((bf16[12,64,128]{2,1,0:T(8,128)(2,1)}, bf16[12,64,128]{2,1,0:T(8,128)(2,1)}, u32[]{:S(2)}, u32[]{:S(2)}) %collective-permute-start.5) | collective-permute-done | bytes 196640 | tf_op jit(solution)/shard_map/ppermute | solution.py:26
  52.3 11.4 %collective-permute-done.7.refs_3_ = bf16[12,64,128]{2,1,0:T(8,128)(2,1)} collective-permute-done((bf16[12,64,128]{2,1,0:T(8,128)(2,1)}, bf16[12,64,128]{2,1,0:T(8,128)(2,1)}, u32[]{:S(2)}, u32[]{:S(2)}) %collective-permute-start.7) | collective-permute-done | bytes 196640 | tf_op jit(solution)/shard_map/ppermute | solution.py:26
  64.8 17.0 %collective-permute-done.8.refs_4_ = bf16[16,64,128]{2,1,0:T(8,128)(2,1)S(1)} collective-permute-done((bf16[16,64,128]{2,1,0:T(8,128)(2,1)S(1)}, bf16[16,64,128]{2,1,0:T(8,128)(2,1)S(1)}, u32[]{:S(2)}, u32[]{:S(2)}) %collective-permute-start.8) | collective-permute-done | bytes 262176 | tf_op jit(solution)/shard_map/ppermute | solution.py:26
  81.8 1.6 copy-done.2
  83.3 2.8 %stock.1.rest_0_.rest_5_ = bf16[196,64,128]{2,1,0:T(8,128)(2,1)S(1)} custom-call(s32[64]{0:T(128)S(1)} %get-tuple-element.79.tile_rows.own_rows, bf16[64,128,128]{2,1,0:T(8,128)(2,1)S(1)} %copy-done.2, bf16[12,64,128]{2,1,0:T(8,128)(2,1)S(1)} %get-tuple-element.40.refs_0_, bf16[12,64,128]{2,1,0:T(8,128)(2,1)} %collective-permute-done.5.refs_1_, ...), custom_call_target="tpu_custom_call" | custom-call | tf_op jit(solution)/shard_map/stock/pallas_call | solution.py:451
  86.2 1.7 copy-done
  87.9 8.7 %all-to-all-done.rest_1_.rest_6_ = bf16[32,400,128]{2,1,0:T(8,128)(2,1)S(1)} async-done(((bf16[32,400,128]{2,1,0:T(8,128)(2,1)}), bf16[32,400,128]{2,1,0:T(8,128)(2,1)S(1)}, u32[]{:S(2)}, u32[]{:S(2)}) %all-to-all-start) | async-done | bytes 3276832 | tf_op jit(solution)/shard_map/all_to_all | solution.py:439
  96.6 1.9 copy-done.1
  98.5 4.2 %product.3 = (bf16[4,17,64,128]{3,2,1,0:T(8,128)(2,1)S(1)}, bf16[4,17,64,128]{3,2,1,0:T(8,128)(2,1)S(1)}, s32[32,128]{1,0:T(8,128)S(1)}) custom-call(s32[3]{0:T(128)S(1)} %pad_add_fusion.place, s32[64]{0:T(128)S(1)} %get-tuple-element.79.tile_rows.own_rows, s32[64]{0:T(128)S(1)} %get-tuple-element.75.own_x, bf16[196,64,128]{2,1,0:T(8,128)(2,1)S(1)} %copy-done.1, ...), custom_call_target="tpu_custom_call" | custom-call | tf_op jit(solution)/shard_map/product/pallas_call | solution.py:486
  102.8 2.7 %collective-permute-done.9.other = bf16[4,17,64,128]{3,2,1,0:T(8,128)(2,1)S(1)} collective-permute-done((bf16[4,17,64,128]{3,2,1,0:T(8,128)(2,1)S(1)}, bf16[4,17,64,128]{3,2,1,0:T(8,128)(2,1)S(1)}, u32[]{:S(2)}, u32[]{:S(2)}) %collective-permute-start.9) | collective-permute-done | bytes 1114144 | tf_op jit(solution)/shard_map/ppermute | solution.py:26
  109.5 6.0 %collective-permute-done.10.rest_0_ = bf16[17,64,128]{2,1,0:T(8,128)(2,1)S(1)} collective-permute-done((bf16[17,64,128]{2,1,0:T(8,128)(2,1)S(1)}, bf16[17,64,128]{2,1,0:T(8,128)(2,1)S(1)}, u32[]{:S(2)}, u32[]{:S(2)}) %collective-permute-start.10) | collective-permute-done | bytes 278560 | tf_op jit(solution)/shard_map/ppermute | solution.py:26
  115.5 5.9 %collective-permute-done.11.rest_1_ = bf16[17,64,128]{2,1,0:T(8,128)(2,1)S(1)} collective-permute-done((bf16[17,64,128]{2,1,0:T(8,128)(2,1)S(1)}, bf16[17,64,128]{2,1,0:T(8,128)(2,1)S(1)}, u32[]{:S(2)}, u32[]{:S(2)}) %collective-permute-start.11) | collective-permute-done | bytes 278560 | tf_op jit(solution)/shard_map/ppermute | solution.py:26
  121.6 2.9 %collective-permute-start.20 = (bf16[8,64,128]{2,1,0:T(8,128)(2,1)S(1)}, bf16[8,64,128]{2,1,0:T(8,128)(2,1)S(1)}, u32[]{:S(2)}, u32[]{:S(2)}) collective-permute-start(bf16[8,64,128]{2,1,0:T(8,128)(2,1)S(1)} %get-tuple-element.54.rest_8_), channel_id=1, source_target_pairs={{0,16},{8,24},{16,0},{24,8},{1,17},{9,25},{17,1},{25,9},{2,18},{10... | collective-permute-start | bytes 393224 | tf_op jit(solution)/shard_map/ppermute | solution.py:26
  124.5 2.0 collective-permute-start.19
  126.5 5.6 %collective-permute-done.13.mark.rest_11_ = bf16[8,64,128]{2,1,0:T(8,128)(2,1)S(1)} collective-permute-done((bf16[8,64,128]{2,1,0:T(8,128)(2,1)S(1)}, bf16[8,64,128]{2,1,0:T(8,128)(2,1)S(1)}, u32[]{:S(2)}, u32[]{:S(2)}) %collective-permute-start.13) | collective-permute-done | bytes 131104 | tf_op jit(solution)/shard_map/ppermute | solution.py:26
  132.9 2.0 collective-permute-done.20.rest_12_
  136.3 1.5 collective-permute-start.16
  140.2 1.5 collective-permute-done.15.rest_2_
  142.4 3.4 %product.4 = (bf16[4,16,64,128]{3,2,1,0:T(8,128)(2,1)S(1)}, bf16[4,16,64,128]{3,2,1,0:T(8,128)(2,1)S(1)}, f32[64,64]{1,0:T(8,128)S(1)}) custom-call(s32[3]{0:T(128)S(1)} %pad_add_fusion.place, s32[64]{0:T(128)S(1)} %get-tuple-element.79.tile_rows.own_rows, s32[64]{0:T(128)S(1)} %add_add_fusion.1.own_x, s32[32,128]{1,0:T(8,128)S(1)} %get-tuple-element.45.rest_0_, ...), custom_call_target="tpu_custom_call" | custom-call | tf_op jit(solution)/shard_map/product/pallas_call | solution.py:486
  145.9 2.6 %collective-permute-done.23.other = bf16[4,16,64,128]{3,2,1,0:T(8,128)(2,1)S(1)} collective-permute-done((bf16[4,16,64,128]{3,2,1,0:T(8,128)(2,1)S(1)}, bf16[4,16,64,128]{3,2,1,0:T(8,128)(2,1)S(1)}, u32[]{:S(2)}, u32[]{:S(2)}) %collective-permute-start.23) | collective-permute-done | bytes 1048608 | tf_op jit(solution)/shard_map/ppermute | solution.py:26
  150.7 1.7 collective-permute-start.29
  152.4 1.9 collective-permute-start.26
  155.2 2.9 %collective-permute-done.26.refs_3_ = f32[64,64]{1,0:T(8,128)S(1)} collective-permute-done((f32[64,64]{1,0:T(8,128)S(1)}, f32[64,64]{1,0:T(8,128)S(1)}, u32[]{:S(2)}, u32[]{:S(2)}) %collective-permute-start.26) | collective-permute-done | bytes 16416 | tf_op jit(solution)/shard_map/ppermute | solution.py:26
  159.4 2.7 %collective-permute-done.24.refs_1_ = f32[64,64]{1,0:T(8,128)S(1)} collective-permute-done((f32[64,64]{1,0:T(8,128)S(1)}, f32[64,64]{1,0:T(8,128)S(1)}, u32[]{:S(2)}, u32[]{:S(2)}) %collective-permute-start.24) | collective-permute-done | bytes 16416 | tf_op jit(solution)/shard_map/ppermute | solution.py:26
  162.1 1.9 factor.2.rest_1_
  165.4 2.0 collective-permute-start.37
  169.4 6.0 %collective-permute-done.30.mark.rest_11_ = bf16[8,64,128]{2,1,0:T(8,128)(2,1)S(1)} collective-permute-done((bf16[8,64,128]{2,1,0:T(8,128)(2,1)S(1)}, bf16[8,64,128]{2,1,0:T(8,128)(2,1)S(1)}, u32[]{:S(2)}, u32[]{:S(2)}) %collective-permute-start.30) | collective-permute-done | bytes 131104 | tf_op jit(solution)/shard_map/ppermute | solution.py:26
  175.4 2.4 %collective-permute-done.37.rest_12_ = bf16[8,64,128]{2,1,0:T(8,128)(2,1)S(1)} collective-permute-done((bf16[8,64,128]{2,1,0:T(8,128)(2,1)S(1)}, bf16[8,64,128]{2,1,0:T(8,128)(2,1)S(1)}, u32[]{:S(2)}, u32[]{:S(2)}) %collective-permute-start.37) | collective-permute-done | bytes 131104 | tf_op jit(solution)/shard_map/ppermute | solution.py:26
  179.6 2.0 collective-permute-start.34
  186.0 2.8 %product.5 = (bf16[4,16,64,128]{3,2,1,0:T(8,128)(2,1)S(1)}, bf16[4,16,64,128]{3,2,1,0:T(8,128)(2,1)S(1)}, f32[64,64]{1,0:T(8,128)S(1)}) custom-call(s32[3]{0:T(128)S(1)} %pad_add_fusion.place, s32[64]{0:T(128)S(1)} %get-tuple-element.79.tile_rows.own_rows, s32[64]{0:T(128)S(1)} %add_add_fusion.1.own_x, s32[32,128]{1,0:T(8,128)S(1)} %get-tuple-element.45.rest_0_, ...), custom_call_target="tpu_custom_call" | custom-call | tf_op jit(solution)/shard_map/product/pallas_call | solution.py:486
  188.9 2.6 %collective-permute-done.40.other = bf16[4,16,64,128]{3,2,1,0:T(8,128)(2,1)S(1)} collective-permute-done((bf16[4,16,64,128]{3,2,1,0:T(8,128)(2,1)S(1)}, bf16[4,16,64,128]{3,2,1,0:T(8,128)(2,1)S(1)}, u32[]{:S(2)}, u32[]{:S(2)}) %collective-permute-start.40) | collective-permute-done | bytes 1048608 | tf_op jit(solution)/shard_map/ppermute | solution.py:26
  195.4 1.8 collective-permute-start.43
  197.2 1.7 collective-permute-start.42
  198.9 2.3 %collective-permute-done.43.refs_3_ = f32[64,64]{1,0:T(8,128)S(1)} collective-permute-done((f32[64,64]{1,0:T(8,128)S(1)}, f32[64,64]{1,0:T(8,128)S(1)}, u32[]{:S(2)}, u32[]{:S(2)}) %collective-permute-start.43) | collective-permute-done | bytes 16416 | tf_op jit(solution)/shard_map/ppermute | solution.py:26
  202.0 3.0 %collective-permute-done.41.refs_1_ = f32[64,64]{1,0:T(8,128)S(1)} collective-permute-done((f32[64,64]{1,0:T(8,128)S(1)}, f32[64,64]{1,0:T(8,128)S(1)}, u32[]{:S(2)}, u32[]{:S(2)}) %collective-permute-start.41) | collective-permute-done | bytes 16416 | tf_op jit(solution)/shard_map/ppermute | solution.py:26
  205.1 1.9 factor.3.rest_1_
  209.1 1.8 collective-permute-start.50
  215.6 2.0 collective-permute-start.53
  220.0 1.6 collective-permute-done.53.refs_3_
  222.8 3.0 %final.1 = f32[64,2048]{1,0:T(8,128)} custom-call(f32[16,64,128]{2,1,0:T(8,128)S(1)} %get-tuple-element.73.scaled, f32[64,64]{1,0:T(8,128)S(1)} %add_add_fusion.refs_0_, f32[64,64]{1,0:T(8,128)S(1)} %collective-permute-done.51.refs_1_, f32[64,64]{1,0:T(8,128)S(1)} %collective-permute-done.52.refs_2_, f32[64,64]{1,0:T(8,128)S(1)} %collective-permute-done.53.refs_3_), custom_call_target="tpu_custom_call" | custom-call | tf_op jit(solution)/shard_map/final/pallas_call | solution.py:546
  (105 shorter events, 45.5 us)
Async XLA Ops:
  0.0 16.4 %collective-permute-start.3 = (bf16[64,2048]{1,0:T(8,128)(2,1)}, bf16[64,2048]{1,0:T(8,128)(2,1)}, u32[]{:S(2)}, u32[]{:S(2)}) collective-permute-start(bf16[64,2048]{1,0:T(8,128)(2,1)} %bitcast.6), channel_id=1, source_target_pairs={{0,16},{8,24},{16,0},{24,8},{1,17},{9,25},{17,1},{25,9},{2,18},{10... | collective-permute-start | bytes 786440 | tf_op jit(solution)/shard_map/ppermute | solution.py:26
  4.0 12.5 %collective-permute-start.1 = (bf16[64,2048]{1,0:T(8,128)(2,1)}, bf16[64,2048]{1,0:T(8,128)(2,1)}, u32[]{:S(2)}, u32[]{:S(2)}) collective-permute-start(bf16[64,2048]{1,0:T(8,128)(2,1)} %bitcast.7), channel_id=1, source_target_pairs={{0,8},{8,0},{16,24},{24,16},{1,9},{9,1},{17,25},{25,17},{2,10},{10... | collective-permute-start | bytes 786440 | tf_op jit(solution)/shard_map/ppermute | solution.py:26
  16.6 80.1 %all-to-all-start = ((bf16[32,400,128]{2,1,0:T(8,128)(2,1)}), bf16[32,400,128]{2,1,0:T(8,128)(2,1)S(1)}, u32[]{:S(2)}, u32[]{:S(2)}) async-start(bf16[32,400,128]{2,1,0:T(8,128)(2,1)} %pack.1), calls=%async_computation | async-start | bytes 6553600 | tf_op jit(solution)/shard_map/all_to_all | solution.py:439
  28.2 22.4 %collective-permute-start.5 = (bf16[12,64,128]{2,1,0:T(8,128)(2,1)}, bf16[12,64,128]{2,1,0:T(8,128)(2,1)}, u32[]{:S(2)}, u32[]{:S(2)}) collective-permute-start(bf16[12,64,128]{2,1,0:T(8,128)(2,1)} %get-tuple-element.41), channel_id=1, source_target_pairs={{0,2},{1,3},{2,0},{3,1},{4,6},{5,7},{6,4},{7,5},{8,10},{9,11},{10,... | collective-permute-start | bytes 589832 | tf_op jit(solution)/shard_map/ppermute | solution.py:26
  30.0 21.4 %collective-permute-start.6 = (bf16[12,64,128]{2,1,0:T(8,128)(2,1)}, bf16[12,64,128]{2,1,0:T(8,128)(2,1)}, u32[]{:S(2)}, u32[]{:S(2)}) collective-permute-start(bf16[12,64,128]{2,1,0:T(8,128)(2,1)} %get-tuple-element.42), channel_id=1, source_target_pairs={{0,4},{1,5},{2,6},{3,7},{4,0},{5,1},{6,2},{7,3},{8,12},{9,13},{10,... | collective-permute-start | bytes 589832 | tf_op jit(solution)/shard_map/ppermute | solution.py:26
  31.5 32.2 %collective-permute-start.7 = (bf16[12,64,128]{2,1,0:T(8,128)(2,1)}, bf16[12,64,128]{2,1,0:T(8,128)(2,1)}, u32[]{:S(2)}, u32[]{:S(2)}) collective-permute-start(bf16[12,64,128]{2,1,0:T(8,128)(2,1)} %get-tuple-element.43), channel_id=1, source_target_pairs={{0,6},{1,7},{2,4},{3,5},{4,2},{5,3},{6,0},{7,1},{8,14},{9,15},{10,... | collective-permute-start | bytes 589832 | tf_op jit(solution)/shard_map/ppermute | solution.py:26
  64.6 17.2 %collective-permute-start.8 = (bf16[16,64,128]{2,1,0:T(8,128)(2,1)S(1)}, bf16[16,64,128]{2,1,0:T(8,128)(2,1)S(1)}, u32[]{:S(2)}, u32[]{:S(2)}) collective-permute-start(bf16[16,64,128]{2,1,0:T(8,128)(2,1)S(1)} %pad_maximum_fusion), channel_id=1, source_target_pairs={{0,8},{8,0},{16,24},{24,16},{1,9},{9,1},{17,25},{25,17},{2,10},{10... | collective-permute-start | bytes 786440 | tf_op jit(solution)/shard_map/ppermute | solution.py:26
  102.7 2.8 %collective-permute-start.9 = (bf16[4,17,64,128]{3,2,1,0:T(8,128)(2,1)S(1)}, bf16[4,17,64,128]{3,2,1,0:T(8,128)(2,1)S(1)}, u32[]{:S(2)}, u32[]{:S(2)}) collective-permute-start(bf16[4,17,64,128]{3,2,1,0:T(8,128)(2,1)S(1)} %get-tuple-element.47), channel_id=1, source_target_pairs={{0,1},{1,0},{2,3},{3,2},{4,5},{5,4},{6,7},{7,6},{8,9},{9,8},{10,11... | collective-permute-start | bytes 3342344 | tf_op jit(solution)/shard_map/ppermute | solution.py:26
  105.9 9.6 %collective-permute-start.10 = (bf16[17,64,128]{2,1,0:T(8,128)(2,1)S(1)}, bf16[17,64,128]{2,1,0:T(8,128)(2,1)S(1)}, u32[]{:S(2)}, u32[]{:S(2)}) collective-permute-start(bf16[17,64,128]{2,1,0:T(8,128)(2,1)S(1)} %get-tuple-element.49), channel_id=1, source_target_pairs={{0,2},{1,3},{2,0},{3,1},{4,6},{5,7},{6,4},{7,5},{8,10},{9,11},{10,... | collective-permute-start | bytes 835592 | tf_op jit(solution)/shard_map/ppermute | solution.py:26
  107.0 14.4 %collective-permute-start.11 = (bf16[17,64,128]{2,1,0:T(8,128)(2,1)S(1)}, bf16[17,64,128]{2,1,0:T(8,128)(2,1)S(1)}, u32[]{:S(2)}, u32[]{:S(2)}) collective-permute-start(bf16[17,64,128]{2,1,0:T(8,128)(2,1)S(1)} %get-tuple-element.50), channel_id=1, source_target_pairs={{0,4},{1,5},{2,6},{3,7},{4,0},{5,1},{6,2},{7,3},{8,12},{9,13},{10,... | collective-permute-start | bytes 835592 | tf_op jit(solution)/shard_map/ppermute | solution.py:26
  108.4 13.0 %collective-permute-start.12 = (bf16[17,64,128]{2,1,0:T(8,128)(2,1)S(1)}, bf16[17,64,128]{2,1,0:T(8,128)(2,1)S(1)}, u32[]{:S(2)}, u32[]{:S(2)}) collective-permute-start(bf16[17,64,128]{2,1,0:T(8,128)(2,1)S(1)} %get-tuple-element.51), channel_id=1, source_target_pairs={{0,6},{1,7},{2,4},{3,5},{4,2},{5,3},{6,0},{7,1},{8,14},{9,15},{10,... | collective-permute-start | bytes 835592 | tf_op jit(solution)/shard_map/ppermute | solution.py:26
  121.5 10.6 %collective-permute-start.13 = (bf16[8,64,128]{2,1,0:T(8,128)(2,1)S(1)}, bf16[8,64,128]{2,1,0:T(8,128)(2,1)S(1)}, u32[]{:S(2)}, u32[]{:S(2)}) collective-permute-start(bf16[8,64,128]{2,1,0:T(8,128)(2,1)S(1)} %get-tuple-element.53.rest_7_), channel_id=1, source_target_pairs={{0,16},{8,24},{16,0},{24,8},{1,17},{9,25},{17,1},{25,9},{2,18},{10... | collective-permute-start | bytes 393224 | tf_op jit(solution)/shard_map/ppermute | solution.py:26
  121.6 13.3 %collective-permute-start.20 = (bf16[8,64,128]{2,1,0:T(8,128)(2,1)S(1)}, bf16[8,64,128]{2,1,0:T(8,128)(2,1)S(1)}, u32[]{:S(2)}, u32[]{:S(2)}) collective-permute-start(bf16[8,64,128]{2,1,0:T(8,128)(2,1)S(1)} %get-tuple-element.54.rest_8_), channel_id=1, source_target_pairs={{0,16},{8,24},{16,0},{24,8},{1,17},{9,25},{17,1},{25,9},{2,18},{10... | collective-permute-start | bytes 393224 | tf_op jit(solution)/shard_map/ppermute | solution.py:26
  124.5 11.8 %collective-permute-start.18 = (bf16[8,64,128]{2,1,0:T(8,128)(2,1)S(1)}, bf16[8,64,128]{2,1,0:T(8,128)(2,1)S(1)}, u32[]{:S(2)}, u32[]{:S(2)}) collective-permute-start(bf16[8,64,128]{2,1,0:T(8,128)(2,1)S(1)} %get-tuple-element.53.rest_7_), channel_id=1, source_target_pairs={{0,8},{8,0},{16,24},{24,16},{1,9},{9,1},{17,25},{25,17},{2,10},{10... | collective-permute-start | bytes 393224 | tf_op jit(solution)/shard_map/ppermute | solution.py:26
  124.5 13.3 %collective-permute-start.19 = (bf16[8,64,128]{2,1,0:T(8,128)(2,1)S(1)}, bf16[8,64,128]{2,1,0:T(8,128)(2,1)S(1)}, u32[]{:S(2)}, u32[]{:S(2)}) collective-permute-start(bf16[8,64,128]{2,1,0:T(8,128)(2,1)S(1)} %get-tuple-element.54.rest_8_), channel_id=1, source_target_pairs={{0,8},{8,0},{16,24},{24,16},{1,9},{9,1},{17,25},{25,17},{2,10},{10... | collective-permute-start | bytes 393224 | tf_op jit(solution)/shard_map/ppermute | solution.py:26
  132.8 8.9 %collective-permute-start.21 = (bf16[8,64,128]{2,1,0:T(8,128)(2,1)S(1)}, bf16[8,64,128]{2,1,0:T(8,128)(2,1)S(1)}, u32[]{:S(2)}, u32[]{:S(2)}) collective-permute-start(bf16[8,64,128]{2,1,0:T(8,128)(2,1)S(1)} %collective-permute-done.13.mark.rest_11_), channel_id=1, source_target_pairs={{0,8},{8,0},{16,24},{24,16},{1,9},{9,1},{17,25},{25,17},{2,10},{10... | collective-permute-start | bytes 393224 | tf_op jit(solution)/shard_map/ppermute | solution.py:26
  134.9 7.5 %collective-permute-start.22 = (bf16[8,64,128]{2,1,0:T(8,128)(2,1)S(1)}, bf16[8,64,128]{2,1,0:T(8,128)(2,1)S(1)}, u32[]{:S(2)}, u32[]{:S(2)}) collective-permute-start(bf16[8,64,128]{2,1,0:T(8,128)(2,1)S(1)} %collective-permute-done.20.rest_12_), channel_id=1, source_target_pairs={{0,8},{8,0},{16,24},{24,16},{1,9},{9,1},{17,25},{25,17},{2,10},{10... | collective-permute-start | bytes 393224 | tf_op jit(solution)/shard_map/ppermute | solution.py:26
  134.9 4.9 %collective-permute-start.17 = (f32[64,64]{1,0:T(8,128)S(1)}, f32[64,64]{1,0:T(8,128)S(1)}, u32[]{:S(2)}, u32[]{:S(2)}) collective-permute-start(f32[64,64]{1,0:T(8,128)S(1)} %add.74.rest_1_), channel_id=1, source_target_pairs={{0,6},{1,7},{2,4},{3,5},{4,2},{5,3},{6,0},{7,1},{8,14},{9,15},{10,... | collective-permute-start | bytes 49160 | tf_op jit(solution)/shard_map/ppermute | solution.py:26
  136.3 3.9 %collective-permute-start.16 = (f32[64,64]{1,0:T(8,128)S(1)}, f32[64,64]{1,0:T(8,128)S(1)}, u32[]{:S(2)}, u32[]{:S(2)}) collective-permute-start(f32[64,64]{1,0:T(8,128)S(1)} %add.74.rest_1_), channel_id=1, source_target_pairs={{0,4},{1,5},{2,6},{3,7},{4,0},{5,1},{6,2},{7,3},{8,12},{9,13},{10,... | collective-permute-start | bytes 49160 | tf_op jit(solution)/shard_map/ppermute | solution.py:26
  137.8 3.9 %collective-permute-start.15 = (f32[64,64]{1,0:T(8,128)S(1)}, f32[64,64]{1,0:T(8,128)S(1)}, u32[]{:S(2)}, u32[]{:S(2)}) collective-permute-start(f32[64,64]{1,0:T(8,128)S(1)} %add.74.rest_1_), channel_id=1, source_target_pairs={{0,2},{1,3},{2,0},{3,1},{4,6},{5,7},{6,4},{7,5},{8,10},{9,11},{10,... | collective-permute-start | bytes 49160 | tf_op jit(solution)/shard_map/ppermute | solution.py:26
  145.8 2.7 %collective-permute-start.23 = (bf16[4,16,64,128]{3,2,1,0:T(8,128)(2,1)S(1)}, bf16[4,16,64,128]{3,2,1,0:T(8,128)(2,1)S(1)}, u32[]{:S(2)}, u32[]{:S(2)}) collective-permute-start(bf16[4,16,64,128]{3,2,1,0:T(8,128)(2,1)S(1)} %get-tuple-element.56), channel_id=1, source_target_pairs={{0,1},{1,0},{2,3},{3,2},{4,5},{5,4},{6,7},{7,6},{8,9},{9,8},{10,11... | collective-permute-start | bytes 3145736 | tf_op jit(solution)/shard_map/ppermute | solution.py:26
  148.9 15.1 %collective-permute-start.27 = (bf16[16,64,128]{2,1,0:T(8,128)(2,1)S(1)}, bf16[16,64,128]{2,1,0:T(8,128)(2,1)S(1)}, u32[]{:S(2)}, u32[]{:S(2)}) collective-permute-start(bf16[16,64,128]{2,1,0:T(8,128)(2,1)S(1)} %get-tuple-element.60), channel_id=1, source_target_pairs={{0,2},{1,3},{2,0},{3,1},{4,6},{5,7},{6,4},{7,5},{8,10},{9,11},{10,... | collective-permute-start | bytes 786440 | tf_op jit(solution)/shard_map/ppermute | solution.py:26
  150.3 13.7 %collective-permute-start.28 = (bf16[16,64,128]{2,1,0:T(8,128)(2,1)S(1)}, bf16[16,64,128]{2,1,0:T(8,128)(2,1)S(1)}, u32[]{:S(2)}, u32[]{:S(2)}) collective-permute-start(bf16[16,64,128]{2,1,0:T(8,128)(2,1)S(1)} %get-tuple-element.61), channel_id=1, source_target_pairs={{0,4},{1,5},{2,6},{3,7},{4,0},{5,1},{6,2},{7,3},{8,12},{9,13},{10,... | collective-permute-start | bytes 786440 | tf_op jit(solution)/shard_map/ppermute | solution.py:26
  150.7 13.3 %collective-permute-start.29 = (bf16[16,64,128]{2,1,0:T(8,128)(2,1)S(1)}, bf16[16,64,128]{2,1,0:T(8,128)(2,1)S(1)}, u32[]{:S(2)}, u32[]{:S(2)}) collective-permute-start(bf16[16,64,128]{2,1,0:T(8,128)(2,1)S(1)} %get-tuple-element.62), channel_id=1, source_target_pairs={{0,6},{1,7},{2,4},{3,5},{4,2},{5,3},{6,0},{7,1},{8,14},{9,15},{10,... | collective-permute-start | bytes 786440 | tf_op jit(solution)/shard_map/ppermute | solution.py:26
  152.4 5.7 %collective-permute-start.26 = (f32[64,64]{1,0:T(8,128)S(1)}, f32[64,64]{1,0:T(8,128)S(1)}, u32[]{:S(2)}, u32[]{:S(2)}) collective-permute-start(f32[64,64]{1,0:T(8,128)S(1)} %get-tuple-element.59.refs_0_), channel_id=1, source_target_pairs={{0,24},{8,16},{16,8},{24,0},{1,25},{9,17},{17,9},{25,1},{2,26},{10... | collective-permute-start | bytes 49160 | tf_op jit(solution)/shard_map/ppermute | solution.py:26
  154.3 5.0 %collective-permute-start.25 = (f32[64,64]{1,0:T(8,128)S(1)}, f32[64,64]{1,0:T(8,128)S(1)}, u32[]{:S(2)}, u32[]{:S(2)}) collective-permute-start(f32[64,64]{1,0:T(8,128)S(1)} %get-tuple-element.59.refs_0_), channel_id=1, source_target_pairs={{0,16},{8,24},{16,0},{24,8},{1,17},{9,25},{17,1},{25,9},{2,18},{10... | collective-permute-start | bytes 49160 | tf_op jit(solution)/shard_map/ppermute | solution.py:26
  158.1 3.9 %collective-permute-start.24 = (f32[64,64]{1,0:T(8,128)S(1)}, f32[64,64]{1,0:T(8,128)S(1)}, u32[]{:S(2)}, u32[]{:S(2)}) collective-permute-start(f32[64,64]{1,0:T(8,128)S(1)} %get-tuple-element.59.refs_0_), channel_id=1, source_target_pairs={{0,8},{8,0},{16,24},{24,16},{1,9},{9,1},{17,25},{25,17},{2,10},{10... | collective-permute-start | bytes 49160 | tf_op jit(solution)/shard_map/ppermute | solution.py:26
  164.4 11.0 %collective-permute-start.30 = (bf16[8,64,128]{2,1,0:T(8,128)(2,1)S(1)}, bf16[8,64,128]{2,1,0:T(8,128)(2,1)S(1)}, u32[]{:S(2)}, u32[]{:S(2)}) collective-permute-start(bf16[8,64,128]{2,1,0:T(8,128)(2,1)S(1)} %get-tuple-element.64.rest_7_), channel_id=1, source_target_pairs={{0,16},{8,24},{16,0},{24,8},{1,17},{9,25},{17,1},{25,9},{2,18},{10... | collective-permute-start | bytes 393224 | tf_op jit(solution)/shard_map/ppermute | solution.py:26
  165.4 12.4 %collective-permute-start.37 = (bf16[8,64,128]{2,1,0:T(8,128)(2,1)S(1)}, bf16[8,64,128]{2,1,0:T(8,128)(2,1)S(1)}, u32[]{:S(2)}, u32[]{:S(2)}) collective-permute-start(bf16[8,64,128]{2,1,0:T(8,128)(2,1)S(1)} %get-tuple-element.65.rest_8_), channel_id=1, source_target_pairs={{0,16},{8,24},{16,0},{24,8},{1,17},{9,25},{17,1},{25,9},{2,18},{10... | collective-permute-start | bytes 393224 | tf_op jit(solution)/shard_map/ppermute | solution.py:26
  167.4 14.2 %collective-permute-start.35 = (bf16[8,64,128]{2,1,0:T(8,128)(2,1)S(1)}, bf16[8,64,128]{2,1,0:T(8,128)(2,1)S(1)}, u32[]{:S(2)}, u32[]{:S(2)}) collective-permute-start(bf16[8,64,128]{2,1,0:T(8,128)(2,1)S(1)} %get-tuple-element.64.rest_7_), channel_id=1, source_target_pairs={{0,8},{8,0},{16,24},{24,16},{1,9},{9,1},{17,25},{25,17},{2,10},{10... | collective-permute-start | bytes 393224 | tf_op jit(solution)/shard_map/ppermute | solution.py:26
  168.0 14.1 %collective-permute-start.36 = (bf16[8,64,128]{2,1,0:T(8,128)(2,1)S(1)}, bf16[8,64,128]{2,1,0:T(8,128)(2,1)S(1)}, u32[]{:S(2)}, u32[]{:S(2)}) collective-permute-start(bf16[8,64,128]{2,1,0:T(8,128)(2,1)S(1)} %get-tuple-element.65.rest_8_), channel_id=1, source_target_pairs={{0,8},{8,0},{16,24},{24,16},{1,9},{9,1},{17,25},{25,17},{2,10},{10... | collective-permute-start | bytes 393224 | tf_op jit(solution)/shard_map/ppermute | solution.py:26
  175.4 10.6 %collective-permute-start.38 = (bf16[8,64,128]{2,1,0:T(8,128)(2,1)S(1)}, bf16[8,64,128]{2,1,0:T(8,128)(2,1)S(1)}, u32[]{:S(2)}, u32[]{:S(2)}) collective-permute-start(bf16[8,64,128]{2,1,0:T(8,128)(2,1)S(1)} %collective-permute-done.30.mark.rest_11_), channel_id=1, source_target_pairs={{0,8},{8,0},{16,24},{24,16},{1,9},{9,1},{17,25},{25,17},{2,10},{10... | collective-permute-start | bytes 393224 | tf_op jit(solution)/shard_map/ppermute | solution.py:26
  177.8 8.2 %collective-permute-start.39 = (bf16[8,64,128]{2,1,0:T(8,128)(2,1)S(1)}, bf16[8,64,128]{2,1,0:T(8,128)(2,1)S(1)}, u32[]{:S(2)}, u32[]{:S(2)}) collective-permute-start(bf16[8,64,128]{2,1,0:T(8,128)(2,1)S(1)} %collective-permute-done.37.rest_12_), channel_id=1, source_target_pairs={{0,8},{8,0},{16,24},{24,16},{1,9},{9,1},{17,25},{25,17},{2,10},{10... | collective-permute-start | bytes 393224 | tf_op jit(solution)/shard_map/ppermute | solution.py:26
  179.6 4.9 %collective-permute-start.34 = (f32[64,64]{1,0:T(8,128)S(1)}, f32[64,64]{1,0:T(8,128)S(1)}, u32[]{:S(2)}, u32[]{:S(2)}) collective-permute-start(f32[64,64]{1,0:T(8,128)S(1)} %add.75.rest_1_), channel_id=1, source_target_pairs={{0,6},{1,7},{2,4},{3,5},{4,2},{5,3},{6,0},{7,1},{8,14},{9,15},{10,... | collective-permute-start | bytes 49160 | tf_op jit(solution)/shard_map/ppermute | solution.py:26
  181.6 3.9 %collective-permute-start.33 = (f32[64,64]{1,0:T(8,128)S(1)}, f32[64,64]{1,0:T(8,128)S(1)}, u32[]{:S(2)}, u32[]{:S(2)}) collective-permute-start(f32[64,64]{1,0:T(8,128)S(1)} %add.75.rest_1_), channel_id=1, source_target_pairs={{0,4},{1,5},{2,6},{3,7},{4,0},{5,1},{6,2},{7,3},{8,12},{9,13},{10,... | collective-permute-start | bytes 49160 | tf_op jit(solution)/shard_map/ppermute | solution.py:26
  182.1 3.9 %collective-permute-start.32 = (f32[64,64]{1,0:T(8,128)S(1)}, f32[64,64]{1,0:T(8,128)S(1)}, u32[]{:S(2)}, u32[]{:S(2)}) collective-permute-start(f32[64,64]{1,0:T(8,128)S(1)} %add.75.rest_1_), channel_id=1, source_target_pairs={{0,2},{1,3},{2,0},{3,1},{4,6},{5,7},{6,4},{7,5},{8,10},{9,11},{10,... | collective-permute-start | bytes 49160 | tf_op jit(solution)/shard_map/ppermute | solution.py:26
  191.9 15.1 %collective-permute-start.44 = (bf16[16,64,128]{2,1,0:T(8,128)(2,1)S(1)}, bf16[16,64,128]{2,1,0:T(8,128)(2,1)S(1)}, u32[]{:S(2)}, u32[]{:S(2)}) collective-permute-start(bf16[16,64,128]{2,1,0:T(8,128)(2,1)S(1)} %get-tuple-element.70), channel_id=1, source_target_pairs={{0,2},{1,3},{2,0},{3,1},{4,6},{5,7},{6,4},{7,5},{8,10},{9,11},{10,... | collective-permute-start | bytes 786440 | tf_op jit(solution)/shard_map/ppermute | solution.py:26
  193.0 14.0 %collective-permute-start.45 = (bf16[16,64,128]{2,1,0:T(8,128)(2,1)S(1)}, bf16[16,64,128]{2,1,0:T(8,128)(2,1)S(1)}, u32[]{:S(2)}, u32[]{:S(2)}) collective-permute-start(bf16[16,64,128]{2,1,0:T(8,128)(2,1)S(1)} %get-tuple-element.71), channel_id=1, source_target_pairs={{0,4},{1,5},{2,6},{3,7},{4,0},{5,1},{6,2},{7,3},{8,12},{9,13},{10,... | collective-permute-start | bytes 786440 | tf_op jit(solution)/shard_map/ppermute | solution.py:26
  194.3 12.7 %collective-permute-start.46 = (bf16[16,64,128]{2,1,0:T(8,128)(2,1)S(1)}, bf16[16,64,128]{2,1,0:T(8,128)(2,1)S(1)}, u32[]{:S(2)}, u32[]{:S(2)}) collective-permute-start(bf16[16,64,128]{2,1,0:T(8,128)(2,1)S(1)} %get-tuple-element.72), channel_id=1, source_target_pairs={{0,6},{1,7},{2,4},{3,5},{4,2},{5,3},{6,0},{7,1},{8,14},{9,15},{10,... | collective-permute-start | bytes 786440 | tf_op jit(solution)/shard_map/ppermute | solution.py:26
  195.4 5.8 %collective-permute-start.43 = (f32[64,64]{1,0:T(8,128)S(1)}, f32[64,64]{1,0:T(8,128)S(1)}, u32[]{:S(2)}, u32[]{:S(2)}) collective-permute-start(f32[64,64]{1,0:T(8,128)S(1)} %get-tuple-element.69.refs_0_), channel_id=1, source_target_pairs={{0,24},{8,16},{16,8},{24,0},{1,25},{9,17},{17,9},{25,1},{2,26},{10... | collective-permute-start | bytes 49160 | tf_op jit(solution)/shard_map/ppermute | solution.py:26
  197.2 4.8 %collective-permute-start.42 = (f32[64,64]{1,0:T(8,128)S(1)}, f32[64,64]{1,0:T(8,128)S(1)}, u32[]{:S(2)}, u32[]{:S(2)}) collective-permute-start(f32[64,64]{1,0:T(8,128)S(1)} %get-tuple-element.69.refs_0_), channel_id=1, source_target_pairs={{0,16},{8,24},{16,0},{24,8},{1,17},{9,25},{17,1},{25,9},{2,18},{10... | collective-permute-start | bytes 49160 | tf_op jit(solution)/shard_map/ppermute | solution.py:26
  201.2 3.9 %collective-permute-start.41 = (f32[64,64]{1,0:T(8,128)S(1)}, f32[64,64]{1,0:T(8,128)S(1)}, u32[]{:S(2)}, u32[]{:S(2)}) collective-permute-start(f32[64,64]{1,0:T(8,128)S(1)} %get-tuple-element.69.refs_0_), channel_id=1, source_target_pairs={{0,8},{8,0},{16,24},{24,16},{1,9},{9,1},{17,25},{25,17},{2,10},{10... | collective-permute-start | bytes 49160 | tf_op jit(solution)/shard_map/ppermute | solution.py:26
  209.1 4.9 %collective-permute-start.50 = (f32[64,64]{1,0:T(8,128)S(1)}, f32[64,64]{1,0:T(8,128)S(1)}, u32[]{:S(2)}, u32[]{:S(2)}) collective-permute-start(f32[64,64]{1,0:T(8,128)S(1)} %add.76), channel_id=1, source_target_pairs={{0,6},{1,7},{2,4},{3,5},{4,2},{5,3},{6,0},{7,1},{8,14},{9,15},{10,... | collective-permute-start | bytes 49160 | tf_op jit(solution)/shard_map/ppermute | solution.py:26
  210.9 3.9 %collective-permute-start.49 = (f32[64,64]{1,0:T(8,128)S(1)}, f32[64,64]{1,0:T(8,128)S(1)}, u32[]{:S(2)}, u32[]{:S(2)}) collective-permute-start(f32[64,64]{1,0:T(8,128)S(1)} %add.76), channel_id=1, source_target_pairs={{0,4},{1,5},{2,6},{3,7},{4,0},{5,1},{6,2},{7,3},{8,12},{9,13},{10,... | collective-permute-start | bytes 49160 | tf_op jit(solution)/shard_map/ppermute | solution.py:26
  211.6 3.9 %collective-permute-start.48 = (f32[64,64]{1,0:T(8,128)S(1)}, f32[64,64]{1,0:T(8,128)S(1)}, u32[]{:S(2)}, u32[]{:S(2)}) collective-permute-start(f32[64,64]{1,0:T(8,128)S(1)} %add.76), channel_id=1, source_target_pairs={{0,2},{1,3},{2,0},{3,1},{4,6},{5,7},{6,4},{7,5},{8,10},{9,11},{10,... | collective-permute-start | bytes 49160 | tf_op jit(solution)/shard_map/ppermute | solution.py:26
  215.6 6.0 %collective-permute-start.53 = (f32[64,64]{1,0:T(8,128)S(1)}, f32[64,64]{1,0:T(8,128)S(1)}, u32[]{:S(2)}, u32[]{:S(2)}) collective-permute-start(f32[64,64]{1,0:T(8,128)S(1)} %add_add_fusion.refs_0_), channel_id=1, source_target_pairs={{0,24},{8,16},{16,8},{24,0},{1,25},{9,17},{17,9},{25,1},{2,26},{10... | collective-permute-start | bytes 49160 | tf_op jit(solution)/shard_map/ppermute | solution.py:26
  217.6 5.3 %collective-permute-start.52 = (f32[64,64]{1,0:T(8,128)S(1)}, f32[64,64]{1,0:T(8,128)S(1)}, u32[]{:S(2)}, u32[]{:S(2)}) collective-permute-start(f32[64,64]{1,0:T(8,128)S(1)} %add_add_fusion.refs_0_), channel_id=1, source_target_pairs={{0,16},{8,24},{16,0},{24,8},{1,17},{9,25},{17,1},{25,9},{2,18},{10... | collective-permute-start | bytes 49160 | tf_op jit(solution)/shard_map/ppermute | solution.py:26
  218.7 4.2 %collective-permute-start.51 = (f32[64,64]{1,0:T(8,128)S(1)}, f32[64,64]{1,0:T(8,128)S(1)}, u32[]{:S(2)}, u32[]{:S(2)}) collective-permute-start(f32[64,64]{1,0:T(8,128)S(1)} %add_add_fusion.refs_0_), channel_id=1, source_target_pairs={{0,8},{8,0},{16,24},{24,16},{1,9},{9,1},{17,25},{25,17},{2,10},{10... | collective-permute-start | bytes 49160 | tf_op jit(solution)/shard_map/ppermute | solution.py:26
  (14 other events, 117.1 us)

commit v6 on v5

--- a/solution.py
+++ b/solution.py
@@ -179,7 +179,7 @@
         total[own_rows[i]] += jnp.dot(x_block(own_x[i]), value, preferred_element_type=F32)
         return carry
 
-    lax.fori_loop(0, tile_count, add_own, 0, unroll=64)
+    lax.fori_loop(0, tile_count, add_own, 0, unroll=32 if first else 64)
     if first:
         numbers_copy.wait()
 
@@ -192,7 +192,7 @@
             total[row] += jnp.dot(x_block(block), value, preferred_element_type=F32)
         return carry
 
-    lax.fori_loop(0, taken.shape[0], add_taken, 0, unroll=16 if first else 32)
+    lax.fori_loop(0, taken.shape[0], add_taken, 0, unroll=8 if first else 32)
 
     def write(mine):
         lane = lax.broadcasted_iota(jnp.int32, total.shape[1:], 1) // sub
@@ -218,9 +218,9 @@
             return carry
 
         if by_column:
-            lax.fori_loop(0, row_size, regroup, 0, unroll=2)
+            lax.fori_loop(0, row_size, regroup, 0, unroll=row_size)
         else:
-            lax.fori_loop(0, per_device, straight, 0, unroll=4)
+            lax.fori_loop(0, per_device, straight, 0, unroll=8)
         if not first:
             return
         lane = lax.broadcasted_iota(jnp.int32, (row_size, tile), 1) // sub

time: 226 us -> 226 us (level)
  transfers between devices with their start and end apart: 55 -> 55, of which waited for: 39 -> 40; matrix products, arithmetic and copies ran while one was open for 1% -> 1% of each run, Pallas kernels for 6% -> 6%
where the time goes in v6:
time: 226 us
  waiting for transfers between devices  127 us (56%)
  starting transfers between devices  59.3 us (26%)
  Pallas kernels  29.6 us (13%)
  local copies, waits for them, and re-layouts  8.72 us (4%)
    ppermute x54, waiting for transfers between devices, exchange(): return lax.ppermute(value, axis, [(i, i ^ distance) for i in range(size)])  119 us
    ppermute x54, starting transfers between devices, exchange(): return lax.ppermute(value, axis, [(i, i ^ distance) for i in range(size)])  53.8 us
    pallas_call x3, Pallas kernels, local(): pl.pallas_call(functools.partial(product_kernel, not last, first, sub, pe...  9.99 us
    all_to_all x1, waiting for transfers between devices, local(): lax.all_to_all(slots, ('row', 'col'), split_axis=0, concat_axis=0, tiled=...  8.72 us
    unnamed x14, local copies, waits for them, and re-layouts  6.18 us
    all_to_all x1, starting transfers between devices, local(): lax.all_to_all(slots, ('row', 'col'), split_axis=0, concat_axis=0, tiled=...  5.5 us
  transfers between devices with their start and end apart: 55, of which 40 were waited for; matrix products, arithmetic and copies ran while one was open for 1% of the time, Pallas kernels for 6%

profile of v6, /device:TPU:0, one launch (start us, length us, event | category | flops | bytes accessed | tf_op | source)
XLA Modules:
  0.0 225.5 jit_solution(12237964859094966654)
XLA Ops:
  0.0 4.0 %collective-permute-start.3 = (bf16[64,2048]{1,0:T(8,128)(2,1)}, bf16[64,2048]{1,0:T(8,128)(2,1)}, u32[]{:S(2)}, u32[]{:S(2)}) collective-permute-start(bf16[64,2048]{1,0:T(8,128)(2,1)} %bitcast.6), channel_id=1, source_target_pairs={{0,16},{8,24},{16,0},{24,8},{1,17},{9,25},{17,1},{25,9},{2,18},{10... | collective-permute-start | bytes 786440 | tf_op jit(solution)/shard_map/ppermute | solution.py:26
  4.0 1.6 collective-permute-start.1
  5.6 4.1 %pack.1 = bf16[32,400,128]{2,1,0:T(8,128)(2,1)} custom-call(s32[48]{0:T(128)} %rows_in.1, s32[48]{0:T(128)} %cols_in.1, bf16[48,128,128]{2,1,0:T(8,128)(2,1)} %chg.1), custom_call_target="tpu_custom_call" | custom-call | tf_op jit(solution)/shard_map/pack/pallas_call | solution.py:401
  9.8 6.6 %collective-permute-done.3.refs_4_ = bf16[64,2048]{1,0:T(8,128)(2,1)} collective-permute-done((bf16[64,2048]{1,0:T(8,128)(2,1)}, bf16[64,2048]{1,0:T(8,128)(2,1)}, u32[]{:S(2)}, u32[]{:S(2)}) %collective-permute-start.3) | collective-permute-done | bytes 262176 | tf_op jit(solution)/shard_map/ppermute | solution.py:26
  16.6 5.5 %all-to-all-start = ((bf16[32,400,128]{2,1,0:T(8,128)(2,1)}), bf16[32,400,128]{2,1,0:T(8,128)(2,1)S(1)}, u32[]{:S(2)}, u32[]{:S(2)}) async-start(bf16[32,400,128]{2,1,0:T(8,128)(2,1)} %pack.1), calls=%async_computation | async-start | bytes 6553600 | tf_op jit(solution)/shard_map/all_to_all | solution.py:439
  25.8 2.5 %merge.1 = (bf16[12,64,128]{2,1,0:T(8,128)(2,1)S(1)}, bf16[12,64,128]{2,1,0:T(8,128)(2,1)}, bf16[12,64,128]{2,1,0:T(8,128)(2,1)}, bf16[12,64,128]{2,1,0:T(8,128)(2,1)}) custom-call(s32[1]{0:T(128)} %bitcast.3.place, bf16[64,2048]{1,0:T(8,128)(2,1)S(1)} %bitcast.9, bf16[64,2048]{1,0:T(8,128)(2,1)} %collective-permute-done.refs_1_, ...), custom_call_target="tpu_custom_call" | custom-call | tf_op jit(solution)/shard_map/merge/pallas_call | solution.py:417
  28.2 1.8 collective-permute-start.5
  30.0 1.5 collective-permute-start.6
  31.7 18.9 %collective-permute-done.5.refs_1_ = bf16[12,64,128]{2,1,0:T(8,128)(2,1)} collective-permute-done((bf16[12,64,128]{2,1,0:T(8,128)(2,1)}, bf16[12,64,128]{2,1,0:T(8,128)(2,1)}, u32[]{:S(2)}, u32[]{:S(2)}) %collective-permute-start.5) | collective-permute-done | bytes 196640 | tf_op jit(solution)/shard_map/ppermute | solution.py:26
  52.3 11.4 %collective-permute-done.7.refs_3_ = bf16[12,64,128]{2,1,0:T(8,128)(2,1)} collective-permute-done((bf16[12,64,128]{2,1,0:T(8,128)(2,1)}, bf16[12,64,128]{2,1,0:T(8,128)(2,1)}, u32[]{:S(2)}, u32[]{:S(2)}) %collective-permute-start.7) | collective-permute-done | bytes 196640 | tf_op jit(solution)/shard_map/ppermute | solution.py:26
  64.8 17.0 %collective-permute-done.8.refs_4_ = bf16[16,64,128]{2,1,0:T(8,128)(2,1)S(1)} collective-permute-done((bf16[16,64,128]{2,1,0:T(8,128)(2,1)S(1)}, bf16[16,64,128]{2,1,0:T(8,128)(2,1)S(1)}, u32[]{:S(2)}, u32[]{:S(2)}) %collective-permute-start.8) | collective-permute-done | bytes 262176 | tf_op jit(solution)/shard_map/ppermute | solution.py:26
  81.8 1.6 copy-done.2
  83.3 2.8 %stock.1.rest_0_.rest_5_ = bf16[196,64,128]{2,1,0:T(8,128)(2,1)S(1)} custom-call(s32[64]{0:T(128)S(1)} %get-tuple-element.79.tile_rows.own_rows, bf16[64,128,128]{2,1,0:T(8,128)(2,1)S(1)} %copy-done.2, bf16[12,64,128]{2,1,0:T(8,128)(2,1)S(1)} %get-tuple-element.40.refs_0_, bf16[12,64,128]{2,1,0:T(8,128)(2,1)} %collective-permute-done.5.refs_1_, ...), custom_call_target="tpu_custom_call" | custom-call | tf_op jit(solution)/shard_map/stock/pallas_call | solution.py:451
  86.2 1.7 copy-done
  87.9 8.7 %all-to-all-done.rest_1_.rest_6_ = bf16[32,400,128]{2,1,0:T(8,128)(2,1)S(1)} async-done(((bf16[32,400,128]{2,1,0:T(8,128)(2,1)}), bf16[32,400,128]{2,1,0:T(8,128)(2,1)S(1)}, u32[]{:S(2)}, u32[]{:S(2)}) %all-to-all-start) | async-done | bytes 3276832 | tf_op jit(solution)/shard_map/all_to_all | solution.py:439
  96.6 1.9 copy-done.1
  98.5 3.8 %product.3 = (bf16[4,17,64,128]{3,2,1,0:T(8,128)(2,1)S(1)}, bf16[4,17,64,128]{3,2,1,0:T(8,128)(2,1)S(1)}, s32[32,128]{1,0:T(8,128)S(1)}) custom-call(s32[3]{0:T(128)S(1)} %pad_add_fusion.place, s32[64]{0:T(128)S(1)} %get-tuple-element.79.tile_rows.own_rows, s32[64]{0:T(128)S(1)} %get-tuple-element.75.own_x, bf16[196,64,128]{2,1,0:T(8,128)(2,1)S(1)} %copy-done.1, ...), custom_call_target="tpu_custom_call" | custom-call | tf_op jit(solution)/shard_map/product/pallas_call | solution.py:486
  102.4 2.7 %collective-permute-done.9.other = bf16[4,17,64,128]{3,2,1,0:T(8,128)(2,1)S(1)} collective-permute-done((bf16[4,17,64,128]{3,2,1,0:T(8,128)(2,1)S(1)}, bf16[4,17,64,128]{3,2,1,0:T(8,128)(2,1)S(1)}, u32[]{:S(2)}, u32[]{:S(2)}) %collective-permute-start.9) | collective-permute-done | bytes 1114144 | tf_op jit(solution)/shard_map/ppermute | solution.py:26
  106.6 1.4 collective-permute-start.11
  109.1 6.0 %collective-permute-done.10.rest_0_ = bf16[17,64,128]{2,1,0:T(8,128)(2,1)S(1)} collective-permute-done((bf16[17,64,128]{2,1,0:T(8,128)(2,1)S(1)}, bf16[17,64,128]{2,1,0:T(8,128)(2,1)S(1)}, u32[]{:S(2)}, u32[]{:S(2)}) %collective-permute-start.10) | collective-permute-done | bytes 278560 | tf_op jit(solution)/shard_map/ppermute | solution.py:26
  115.1 5.9 %collective-permute-done.11.rest_1_ = bf16[17,64,128]{2,1,0:T(8,128)(2,1)S(1)} collective-permute-done((bf16[17,64,128]{2,1,0:T(8,128)(2,1)S(1)}, bf16[17,64,128]{2,1,0:T(8,128)(2,1)S(1)}, u32[]{:S(2)}, u32[]{:S(2)}) %collective-permute-start.11) | collective-permute-done | bytes 278560 | tf_op jit(solution)/shard_map/ppermute | solution.py:26
  121.3 2.9 %collective-permute-start.20 = (bf16[8,64,128]{2,1,0:T(8,128)(2,1)S(1)}, bf16[8,64,128]{2,1,0:T(8,128)(2,1)S(1)}, u32[]{:S(2)}, u32[]{:S(2)}) collective-permute-start(bf16[8,64,128]{2,1,0:T(8,128)(2,1)S(1)} %get-tuple-element.54.rest_8_), channel_id=1, source_target_pairs={{0,16},{8,24},{16,0},{24,8},{1,17},{9,25},{17,1},{25,9},{2,18},{10... | collective-permute-start | bytes 393224 | tf_op jit(solution)/shard_map/ppermute | solution.py:26
  124.2 2.0 collective-permute-start.19
  126.2 5.6 %collective-permute-done.13.mark.rest_11_ = bf16[8,64,128]{2,1,0:T(8,128)(2,1)S(1)} collective-permute-done((bf16[8,64,128]{2,1,0:T(8,128)(2,1)S(1)}, bf16[8,64,128]{2,1,0:T(8,128)(2,1)S(1)}, u32[]{:S(2)}, u32[]{:S(2)}) %collective-permute-start.13) | collective-permute-done | bytes 131104 | tf_op jit(solution)/shard_map/ppermute | solution.py:26
  132.5 2.0 collective-permute-done.20.rest_12_
  142.0 3.4 %product.4 = (bf16[4,16,64,128]{3,2,1,0:T(8,128)(2,1)S(1)}, bf16[4,16,64,128]{3,2,1,0:T(8,128)(2,1)S(1)}, f32[64,64]{1,0:T(8,128)S(1)}) custom-call(s32[3]{0:T(128)S(1)} %pad_add_fusion.place, s32[64]{0:T(128)S(1)} %get-tuple-element.79.tile_rows.own_rows, s32[64]{0:T(128)S(1)} %add_add_fusion.1.own_x, s32[32,128]{1,0:T(8,128)S(1)} %get-tuple-element.45.rest_0_, ...), custom_call_target="tpu_custom_call" | custom-call | tf_op jit(solution)/shard_map/product/pallas_call | solution.py:486
  145.5 2.6 %collective-permute-done.23.other = bf16[4,16,64,128]{3,2,1,0:T(8,128)(2,1)S(1)} collective-permute-done((bf16[4,16,64,128]{3,2,1,0:T(8,128)(2,1)S(1)}, bf16[4,16,64,128]{3,2,1,0:T(8,128)(2,1)S(1)}, u32[]{:S(2)}, u32[]{:S(2)}) %collective-permute-start.23) | collective-permute-done | bytes 1048608 | tf_op jit(solution)/shard_map/ppermute | solution.py:26
  148.5 1.5 collective-permute-start.27
  150.3 1.7 collective-permute-start.29
  152.0 1.9 collective-permute-start.26
  154.8 2.9 %collective-permute-done.26.refs_3_ = f32[64,64]{1,0:T(8,128)S(1)} collective-permute-done((f32[64,64]{1,0:T(8,128)S(1)}, f32[64,64]{1,0:T(8,128)S(1)}, u32[]{:S(2)}, u32[]{:S(2)}) %collective-permute-start.26) | collective-permute-done | bytes 16416 | tf_op jit(solution)/shard_map/ppermute | solution.py:26
  159.0 2.7 %collective-permute-done.24.refs_1_ = f32[64,64]{1,0:T(8,128)S(1)} collective-permute-done((f32[64,64]{1,0:T(8,128)S(1)}, f32[64,64]{1,0:T(8,128)S(1)}, u32[]{:S(2)}, u32[]{:S(2)}) %collective-permute-start.24) | collective-permute-done | bytes 16416 | tf_op jit(solution)/shard_map/ppermute | solution.py:26
  161.6 1.9 factor.2.rest_1_
  165.0 2.0 collective-permute-start.37
  169.0 5.9 %collective-permute-done.30.mark.rest_11_ = bf16[8,64,128]{2,1,0:T(8,128)(2,1)S(1)} collective-permute-done((bf16[8,64,128]{2,1,0:T(8,128)(2,1)S(1)}, bf16[8,64,128]{2,1,0:T(8,128)(2,1)S(1)}, u32[]{:S(2)}, u32[]{:S(2)}) %collective-permute-start.30) | collective-permute-done | bytes 131104 | tf_op jit(solution)/shard_map/ppermute | solution.py:26
  174.9 2.5 %collective-permute-done.37.rest_12_ = bf16[8,64,128]{2,1,0:T(8,128)(2,1)S(1)} collective-permute-done((bf16[8,64,128]{2,1,0:T(8,128)(2,1)S(1)}, bf16[8,64,128]{2,1,0:T(8,128)(2,1)S(1)}, u32[]{:S(2)}, u32[]{:S(2)}) %collective-permute-start.37) | collective-permute-done | bytes 131104 | tf_op jit(solution)/shard_map/ppermute | solution.py:26
  179.2 2.0 collective-permute-start.34
  185.6 2.8 %product.5 = (bf16[4,16,64,128]{3,2,1,0:T(8,128)(2,1)S(1)}, bf16[4,16,64,128]{3,2,1,0:T(8,128)(2,1)S(1)}, f32[64,64]{1,0:T(8,128)S(1)}) custom-call(s32[3]{0:T(128)S(1)} %pad_add_fusion.place, s32[64]{0:T(128)S(1)} %get-tuple-element.79.tile_rows.own_rows, s32[64]{0:T(128)S(1)} %add_add_fusion.1.own_x, s32[32,128]{1,0:T(8,128)S(1)} %get-tuple-element.45.rest_0_, ...), custom_call_target="tpu_custom_call" | custom-call | tf_op jit(solution)/shard_map/product/pallas_call | solution.py:486
  188.4 2.6 %collective-permute-done.40.other = bf16[4,16,64,128]{3,2,1,0:T(8,128)(2,1)S(1)} collective-permute-done((bf16[4,16,64,128]{3,2,1,0:T(8,128)(2,1)S(1)}, bf16[4,16,64,128]{3,2,1,0:T(8,128)(2,1)S(1)}, u32[]{:S(2)}, u32[]{:S(2)}) %collective-permute-start.40) | collective-permute-done | bytes 1048608 | tf_op jit(solution)/shard_map/ppermute | solution.py:26
  195.0 1.8 collective-permute-start.43
  196.8 1.7 collective-permute-start.42
  198.5 2.3 %collective-permute-done.43.refs_3_ = f32[64,64]{1,0:T(8,128)S(1)} collective-permute-done((f32[64,64]{1,0:T(8,128)S(1)}, f32[64,64]{1,0:T(8,128)S(1)}, u32[]{:S(2)}, u32[]{:S(2)}) %collective-permute-start.43) | collective-permute-done | bytes 16416 | tf_op jit(solution)/shard_map/ppermute | solution.py:26
  201.6 3.0 %collective-permute-done.41.refs_1_ = f32[64,64]{1,0:T(8,128)S(1)} collective-permute-done((f32[64,64]{1,0:T(8,128)S(1)}, f32[64,64]{1,0:T(8,128)S(1)}, u32[]{:S(2)}, u32[]{:S(2)}) %collective-permute-start.41) | collective-permute-done | bytes 16416 | tf_op jit(solution)/shard_map/ppermute | solution.py:26
  204.6 1.9 factor.3.rest_1_
  208.6 1.8 collective-permute-start.50
  215.1 2.0 collective-permute-start.53
  219.6 1.6 collective-permute-done.53.refs_3_
  222.5 3.0 %final.1 = f32[64,2048]{1,0:T(8,128)} custom-call(f32[16,64,128]{2,1,0:T(8,128)S(1)} %get-tuple-element.73.scaled, f32[64,64]{1,0:T(8,128)S(1)} %add_add_fusion.refs_0_, f32[64,64]{1,0:T(8,128)S(1)} %collective-permute-done.51.refs_1_, f32[64,64]{1,0:T(8,128)S(1)} %collective-permute-done.52.refs_2_, f32[64,64]{1,0:T(8,128)S(1)} %collective-permute-done.53.refs_3_), custom_call_target="tpu_custom_call" | custom-call | tf_op jit(solution)/shard_map/final/pallas_call | solution.py:546
  (105 shorter events, 45.6 us)
Async XLA Ops:
  0.0 16.4 %collective-permute-start.3 = (bf16[64,2048]{1,0:T(8,128)(2,1)}, bf16[64,2048]{1,0:T(8,128)(2,1)}, u32[]{:S(2)}, u32[]{:S(2)}) collective-permute-start(bf16[64,2048]{1,0:T(8,128)(2,1)} %bitcast.6), channel_id=1, source_target_pairs={{0,16},{8,24},{16,0},{24,8},{1,17},{9,25},{17,1},{25,9},{2,18},{10... | collective-permute-start | bytes 786440 | tf_op jit(solution)/shard_map/ppermute | solution.py:26
  4.0 12.5 %collective-permute-start.1 = (bf16[64,2048]{1,0:T(8,128)(2,1)}, bf16[64,2048]{1,0:T(8,128)(2,1)}, u32[]{:S(2)}, u32[]{:S(2)}) collective-permute-start(bf16[64,2048]{1,0:T(8,128)(2,1)} %bitcast.7), channel_id=1, source_target_pairs={{0,8},{8,0},{16,24},{24,16},{1,9},{9,1},{17,25},{25,17},{2,10},{10... | collective-permute-start | bytes 786440 | tf_op jit(solution)/shard_map/ppermute | solution.py:26
  16.6 80.1 %all-to-all-start = ((bf16[32,400,128]{2,1,0:T(8,128)(2,1)}), bf16[32,400,128]{2,1,0:T(8,128)(2,1)S(1)}, u32[]{:S(2)}, u32[]{:S(2)}) async-start(bf16[32,400,128]{2,1,0:T(8,128)(2,1)} %pack.1), calls=%async_computation | async-start | bytes 6553600 | tf_op jit(solution)/shard_map/all_to_all | solution.py:439
  28.2 22.4 %collective-permute-start.5 = (bf16[12,64,128]{2,1,0:T(8,128)(2,1)}, bf16[12,64,128]{2,1,0:T(8,128)(2,1)}, u32[]{:S(2)}, u32[]{:S(2)}) collective-permute-start(bf16[12,64,128]{2,1,0:T(8,128)(2,1)} %get-tuple-element.41), channel_id=1, source_target_pairs={{0,2},{1,3},{2,0},{3,1},{4,6},{5,7},{6,4},{7,5},{8,10},{9,11},{10,... | collective-permute-start | bytes 589832 | tf_op jit(solution)/shard_map/ppermute | solution.py:26
  30.0 21.4 %collective-permute-start.6 = (bf16[12,64,128]{2,1,0:T(8,128)(2,1)}, bf16[12,64,128]{2,1,0:T(8,128)(2,1)}, u32[]{:S(2)}, u32[]{:S(2)}) collective-permute-start(bf16[12,64,128]{2,1,0:T(8,128)(2,1)} %get-tuple-element.42), channel_id=1, source_target_pairs={{0,4},{1,5},{2,6},{3,7},{4,0},{5,1},{6,2},{7,3},{8,12},{9,13},{10,... | collective-permute-start | bytes 589832 | tf_op jit(solution)/shard_map/ppermute | solution.py:26
  31.5 32.2 %collective-permute-start.7 = (bf16[12,64,128]{2,1,0:T(8,128)(2,1)}, bf16[12,64,128]{2,1,0:T(8,128)(2,1)}, u32[]{:S(2)}, u32[]{:S(2)}) collective-permute-start(bf16[12,64,128]{2,1,0:T(8,128)(2,1)} %get-tuple-element.43), channel_id=1, source_target_pairs={{0,6},{1,7},{2,4},{3,5},{4,2},{5,3},{6,0},{7,1},{8,14},{9,15},{10,... | collective-permute-start | bytes 589832 | tf_op jit(solution)/shard_map/ppermute | solution.py:26
  64.6 17.2 %collective-permute-start.8 = (bf16[16,64,128]{2,1,0:T(8,128)(2,1)S(1)}, bf16[16,64,128]{2,1,0:T(8,128)(2,1)S(1)}, u32[]{:S(2)}, u32[]{:S(2)}) collective-permute-start(bf16[16,64,128]{2,1,0:T(8,128)(2,1)S(1)} %pad_maximum_fusion), channel_id=1, source_target_pairs={{0,8},{8,0},{16,24},{24,16},{1,9},{9,1},{17,25},{25,17},{2,10},{10... | collective-permute-start | bytes 786440 | tf_op jit(solution)/shard_map/ppermute | solution.py:26
  102.4 2.8 %collective-permute-start.9 = (bf16[4,17,64,128]{3,2,1,0:T(8,128)(2,1)S(1)}, bf16[4,17,64,128]{3,2,1,0:T(8,128)(2,1)S(1)}, u32[]{:S(2)}, u32[]{:S(2)}) collective-permute-start(bf16[4,17,64,128]{3,2,1,0:T(8,128)(2,1)S(1)} %get-tuple-element.47), channel_id=1, source_target_pairs={{0,1},{1,0},{2,3},{3,2},{4,5},{5,4},{6,7},{7,6},{8,9},{9,8},{10,11... | collective-permute-start | bytes 3342344 | tf_op jit(solution)/shard_map/ppermute | solution.py:26
  105.5 9.6 %collective-permute-start.10 = (bf16[17,64,128]{2,1,0:T(8,128)(2,1)S(1)}, bf16[17,64,128]{2,1,0:T(8,128)(2,1)S(1)}, u32[]{:S(2)}, u32[]{:S(2)}) collective-permute-start(bf16[17,64,128]{2,1,0:T(8,128)(2,1)S(1)} %get-tuple-element.49), channel_id=1, source_target_pairs={{0,2},{1,3},{2,0},{3,1},{4,6},{5,7},{6,4},{7,5},{8,10},{9,11},{10,... | collective-permute-start | bytes 835592 | tf_op jit(solution)/shard_map/ppermute | solution.py:26
  106.6 14.4 %collective-permute-start.11 = (bf16[17,64,128]{2,1,0:T(8,128)(2,1)S(1)}, bf16[17,64,128]{2,1,0:T(8,128)(2,1)S(1)}, u32[]{:S(2)}, u32[]{:S(2)}) collective-permute-start(bf16[17,64,128]{2,1,0:T(8,128)(2,1)S(1)} %get-tuple-element.50), channel_id=1, source_target_pairs={{0,4},{1,5},{2,6},{3,7},{4,0},{5,1},{6,2},{7,3},{8,12},{9,13},{10,... | collective-permute-start | bytes 835592 | tf_op jit(solution)/shard_map/ppermute | solution.py:26
  108.1 12.9 %collective-permute-start.12 = (bf16[17,64,128]{2,1,0:T(8,128)(2,1)S(1)}, bf16[17,64,128]{2,1,0:T(8,128)(2,1)S(1)}, u32[]{:S(2)}, u32[]{:S(2)}) collective-permute-start(bf16[17,64,128]{2,1,0:T(8,128)(2,1)S(1)} %get-tuple-element.51), channel_id=1, source_target_pairs={{0,6},{1,7},{2,4},{3,5},{4,2},{5,3},{6,0},{7,1},{8,14},{9,15},{10,... | collective-permute-start | bytes 835592 | tf_op jit(solution)/shard_map/ppermute | solution.py:26
  121.2 10.6 %collective-permute-start.13 = (bf16[8,64,128]{2,1,0:T(8,128)(2,1)S(1)}, bf16[8,64,128]{2,1,0:T(8,128)(2,1)S(1)}, u32[]{:S(2)}, u32[]{:S(2)}) collective-permute-start(bf16[8,64,128]{2,1,0:T(8,128)(2,1)S(1)} %get-tuple-element.53.rest_7_), channel_id=1, source_target_pairs={{0,16},{8,24},{16,0},{24,8},{1,17},{9,25},{17,1},{25,9},{2,18},{10... | collective-permute-start | bytes 393224 | tf_op jit(solution)/shard_map/ppermute | solution.py:26
  121.3 13.3 %collective-permute-start.20 = (bf16[8,64,128]{2,1,0:T(8,128)(2,1)S(1)}, bf16[8,64,128]{2,1,0:T(8,128)(2,1)S(1)}, u32[]{:S(2)}, u32[]{:S(2)}) collective-permute-start(bf16[8,64,128]{2,1,0:T(8,128)(2,1)S(1)} %get-tuple-element.54.rest_8_), channel_id=1, source_target_pairs={{0,16},{8,24},{16,0},{24,8},{1,17},{9,25},{17,1},{25,9},{2,18},{10... | collective-permute-start | bytes 393224 | tf_op jit(solution)/shard_map/ppermute | solution.py:26
  124.2 11.8 %collective-permute-start.18 = (bf16[8,64,128]{2,1,0:T(8,128)(2,1)S(1)}, bf16[8,64,128]{2,1,0:T(8,128)(2,1)S(1)}, u32[]{:S(2)}, u32[]{:S(2)}) collective-permute-start(bf16[8,64,128]{2,1,0:T(8,128)(2,1)S(1)} %get-tuple-element.53.rest_7_), channel_id=1, source_target_pairs={{0,8},{8,0},{16,24},{24,16},{1,9},{9,1},{17,25},{25,17},{2,10},{10... | collective-permute-start | bytes 393224 | tf_op jit(solution)/shard_map/ppermute | solution.py:26
  124.2 13.3 %collective-permute-start.19 = (bf16[8,64,128]{2,1,0:T(8,128)(2,1)S(1)}, bf16[8,64,128]{2,1,0:T(8,128)(2,1)S(1)}, u32[]{:S(2)}, u32[]{:S(2)}) collective-permute-start(bf16[8,64,128]{2,1,0:T(8,128)(2,1)S(1)} %get-tuple-element.54.rest_8_), channel_id=1, source_target_pairs={{0,8},{8,0},{16,24},{24,16},{1,9},{9,1},{17,25},{25,17},{2,10},{10... | collective-permute-start | bytes 393224 | tf_op jit(solution)/shard_map/ppermute | solution.py:26
  132.5 8.9 %collective-permute-start.21 = (bf16[8,64,128]{2,1,0:T(8,128)(2,1)S(1)}, bf16[8,64,128]{2,1,0:T(8,128)(2,1)S(1)}, u32[]{:S(2)}, u32[]{:S(2)}) collective-permute-start(bf16[8,64,128]{2,1,0:T(8,128)(2,1)S(1)} %collective-permute-done.13.mark.rest_11_), channel_id=1, source_target_pairs={{0,8},{8,0},{16,24},{24,16},{1,9},{9,1},{17,25},{25,17},{2,10},{10... | collective-permute-start | bytes 393224 | tf_op jit(solution)/shard_map/ppermute | solution.py:26
  134.5 7.5 %collective-permute-start.22 = (bf16[8,64,128]{2,1,0:T(8,128)(2,1)S(1)}, bf16[8,64,128]{2,1,0:T(8,128)(2,1)S(1)}, u32[]{:S(2)}, u32[]{:S(2)}) collective-permute-start(bf16[8,64,128]{2,1,0:T(8,128)(2,1)S(1)} %collective-permute-done.20.rest_12_), channel_id=1, source_target_pairs={{0,8},{8,0},{16,24},{24,16},{1,9},{9,1},{17,25},{25,17},{2,10},{10... | collective-permute-start | bytes 393224 | tf_op jit(solution)/shard_map/ppermute | solution.py:26
  134.6 4.9 %collective-permute-start.17 = (f32[64,64]{1,0:T(8,128)S(1)}, f32[64,64]{1,0:T(8,128)S(1)}, u32[]{:S(2)}, u32[]{:S(2)}) collective-permute-start(f32[64,64]{1,0:T(8,128)S(1)} %add.74.rest_1_), channel_id=1, source_target_pairs={{0,6},{1,7},{2,4},{3,5},{4,2},{5,3},{6,0},{7,1},{8,14},{9,15},{10,... | collective-permute-start | bytes 49160 | tf_op jit(solution)/shard_map/ppermute | solution.py:26
  136.0 3.9 %collective-permute-start.16 = (f32[64,64]{1,0:T(8,128)S(1)}, f32[64,64]{1,0:T(8,128)S(1)}, u32[]{:S(2)}, u32[]{:S(2)}) collective-permute-start(f32[64,64]{1,0:T(8,128)S(1)} %add.74.rest_1_), channel_id=1, source_target_pairs={{0,4},{1,5},{2,6},{3,7},{4,0},{5,1},{6,2},{7,3},{8,12},{9,13},{10,... | collective-permute-start | bytes 49160 | tf_op jit(solution)/shard_map/ppermute | solution.py:26
  137.4 3.9 %collective-permute-start.15 = (f32[64,64]{1,0:T(8,128)S(1)}, f32[64,64]{1,0:T(8,128)S(1)}, u32[]{:S(2)}, u32[]{:S(2)}) collective-permute-start(f32[64,64]{1,0:T(8,128)S(1)} %add.74.rest_1_), channel_id=1, source_target_pairs={{0,2},{1,3},{2,0},{3,1},{4,6},{5,7},{6,4},{7,5},{8,10},{9,11},{10,... | collective-permute-start | bytes 49160 | tf_op jit(solution)/shard_map/ppermute | solution.py:26
  145.4 2.7 %collective-permute-start.23 = (bf16[4,16,64,128]{3,2,1,0:T(8,128)(2,1)S(1)}, bf16[4,16,64,128]{3,2,1,0:T(8,128)(2,1)S(1)}, u32[]{:S(2)}, u32[]{:S(2)}) collective-permute-start(bf16[4,16,64,128]{3,2,1,0:T(8,128)(2,1)S(1)} %get-tuple-element.56), channel_id=1, source_target_pairs={{0,1},{1,0},{2,3},{3,2},{4,5},{5,4},{6,7},{7,6},{8,9},{9,8},{10,11... | collective-permute-start | bytes 3145736 | tf_op jit(solution)/shard_map/ppermute | solution.py:26
  148.5 15.1 %collective-permute-start.27 = (bf16[16,64,128]{2,1,0:T(8,128)(2,1)S(1)}, bf16[16,64,128]{2,1,0:T(8,128)(2,1)S(1)}, u32[]{:S(2)}, u32[]{:S(2)}) collective-permute-start(bf16[16,64,128]{2,1,0:T(8,128)(2,1)S(1)} %get-tuple-element.60), channel_id=1, source_target_pairs={{0,2},{1,3},{2,0},{3,1},{4,6},{5,7},{6,4},{7,5},{8,10},{9,11},{10,... | collective-permute-start | bytes 786440 | tf_op jit(solution)/shard_map/ppermute | solution.py:26
  149.9 13.7 %collective-permute-start.28 = (bf16[16,64,128]{2,1,0:T(8,128)(2,1)S(1)}, bf16[16,64,128]{2,1,0:T(8,128)(2,1)S(1)}, u32[]{:S(2)}, u32[]{:S(2)}) collective-permute-start(bf16[16,64,128]{2,1,0:T(8,128)(2,1)S(1)} %get-tuple-element.61), channel_id=1, source_target_pairs={{0,4},{1,5},{2,6},{3,7},{4,0},{5,1},{6,2},{7,3},{8,12},{9,13},{10,... | collective-permute-start | bytes 786440 | tf_op jit(solution)/shard_map/ppermute | solution.py:26
  150.3 13.3 %collective-permute-start.29 = (bf16[16,64,128]{2,1,0:T(8,128)(2,1)S(1)}, bf16[16,64,128]{2,1,0:T(8,128)(2,1)S(1)}, u32[]{:S(2)}, u32[]{:S(2)}) collective-permute-start(bf16[16,64,128]{2,1,0:T(8,128)(2,1)S(1)} %get-tuple-element.62), channel_id=1, source_target_pairs={{0,6},{1,7},{2,4},{3,5},{4,2},{5,3},{6,0},{7,1},{8,14},{9,15},{10,... | collective-permute-start | bytes 786440 | tf_op jit(solution)/shard_map/ppermute | solution.py:26
  152.0 5.7 %collective-permute-start.26 = (f32[64,64]{1,0:T(8,128)S(1)}, f32[64,64]{1,0:T(8,128)S(1)}, u32[]{:S(2)}, u32[]{:S(2)}) collective-permute-start(f32[64,64]{1,0:T(8,128)S(1)} %get-tuple-element.59.refs_0_), channel_id=1, source_target_pairs={{0,24},{8,16},{16,8},{24,0},{1,25},{9,17},{17,9},{25,1},{2,26},{10... | collective-permute-start | bytes 49160 | tf_op jit(solution)/shard_map/ppermute | solution.py:26
  153.9 5.0 %collective-permute-start.25 = (f32[64,64]{1,0:T(8,128)S(1)}, f32[64,64]{1,0:T(8,128)S(1)}, u32[]{:S(2)}, u32[]{:S(2)}) collective-permute-start(f32[64,64]{1,0:T(8,128)S(1)} %get-tuple-element.59.refs_0_), channel_id=1, source_target_pairs={{0,16},{8,24},{16,0},{24,8},{1,17},{9,25},{17,1},{25,9},{2,18},{10... | collective-permute-start | bytes 49160 | tf_op jit(solution)/shard_map/ppermute | solution.py:26
  157.7 3.9 %collective-permute-start.24 = (f32[64,64]{1,0:T(8,128)S(1)}, f32[64,64]{1,0:T(8,128)S(1)}, u32[]{:S(2)}, u32[]{:S(2)}) collective-permute-start(f32[64,64]{1,0:T(8,128)S(1)} %get-tuple-element.59.refs_0_), channel_id=1, source_target_pairs={{0,8},{8,0},{16,24},{24,16},{1,9},{9,1},{17,25},{25,17},{2,10},{10... | collective-permute-start | bytes 49160 | tf_op jit(solution)/shard_map/ppermute | solution.py:26
  164.0 10.9 %collective-permute-start.30 = (bf16[8,64,128]{2,1,0:T(8,128)(2,1)S(1)}, bf16[8,64,128]{2,1,0:T(8,128)(2,1)S(1)}, u32[]{:S(2)}, u32[]{:S(2)}) collective-permute-start(bf16[8,64,128]{2,1,0:T(8,128)(2,1)S(1)} %get-tuple-element.64.rest_7_), channel_id=1, source_target_pairs={{0,16},{8,24},{16,0},{24,8},{1,17},{9,25},{17,1},{25,9},{2,18},{10... | collective-permute-start | bytes 393224 | tf_op jit(solution)/shard_map/ppermute | solution.py:26
  165.0 12.4 %collective-permute-start.37 = (bf16[8,64,128]{2,1,0:T(8,128)(2,1)S(1)}, bf16[8,64,128]{2,1,0:T(8,128)(2,1)S(1)}, u32[]{:S(2)}, u32[]{:S(2)}) collective-permute-start(bf16[8,64,128]{2,1,0:T(8,128)(2,1)S(1)} %get-tuple-element.65.rest_8_), channel_id=1, source_target_pairs={{0,16},{8,24},{16,0},{24,8},{1,17},{9,25},{17,1},{25,9},{2,18},{10... | collective-permute-start | bytes 393224 | tf_op jit(solution)/shard_map/ppermute | solution.py:26
  167.0 14.2 %collective-permute-start.35 = (bf16[8,64,128]{2,1,0:T(8,128)(2,1)S(1)}, bf16[8,64,128]{2,1,0:T(8,128)(2,1)S(1)}, u32[]{:S(2)}, u32[]{:S(2)}) collective-permute-start(bf16[8,64,128]{2,1,0:T(8,128)(2,1)S(1)} %get-tuple-element.64.rest_7_), channel_id=1, source_target_pairs={{0,8},{8,0},{16,24},{24,16},{1,9},{9,1},{17,25},{25,17},{2,10},{10... | collective-permute-start | bytes 393224 | tf_op jit(solution)/shard_map/ppermute | solution.py:26
  167.6 14.0 %collective-permute-start.36 = (bf16[8,64,128]{2,1,0:T(8,128)(2,1)S(1)}, bf16[8,64,128]{2,1,0:T(8,128)(2,1)S(1)}, u32[]{:S(2)}, u32[]{:S(2)}) collective-permute-start(bf16[8,64,128]{2,1,0:T(8,128)(2,1)S(1)} %get-tuple-element.65.rest_8_), channel_id=1, source_target_pairs={{0,8},{8,0},{16,24},{24,16},{1,9},{9,1},{17,25},{25,17},{2,10},{10... | collective-permute-start | bytes 393224 | tf_op jit(solution)/shard_map/ppermute | solution.py:26
  174.9 10.7 %collective-permute-start.38 = (bf16[8,64,128]{2,1,0:T(8,128)(2,1)S(1)}, bf16[8,64,128]{2,1,0:T(8,128)(2,1)S(1)}, u32[]{:S(2)}, u32[]{:S(2)}) collective-permute-start(bf16[8,64,128]{2,1,0:T(8,128)(2,1)S(1)} %collective-permute-done.30.mark.rest_11_), channel_id=1, source_target_pairs={{0,8},{8,0},{16,24},{24,16},{1,9},{9,1},{17,25},{25,17},{2,10},{10... | collective-permute-start | bytes 393224 | tf_op jit(solution)/shard_map/ppermute | solution.py:26
  177.4 8.2 %collective-permute-start.39 = (bf16[8,64,128]{2,1,0:T(8,128)(2,1)S(1)}, bf16[8,64,128]{2,1,0:T(8,128)(2,1)S(1)}, u32[]{:S(2)}, u32[]{:S(2)}) collective-permute-start(bf16[8,64,128]{2,1,0:T(8,128)(2,1)S(1)} %collective-permute-done.37.rest_12_), channel_id=1, source_target_pairs={{0,8},{8,0},{16,24},{24,16},{1,9},{9,1},{17,25},{25,17},{2,10},{10... | collective-permute-start | bytes 393224 | tf_op jit(solution)/shard_map/ppermute | solution.py:26
  179.2 4.8 %collective-permute-start.34 = (f32[64,64]{1,0:T(8,128)S(1)}, f32[64,64]{1,0:T(8,128)S(1)}, u32[]{:S(2)}, u32[]{:S(2)}) collective-permute-start(f32[64,64]{1,0:T(8,128)S(1)} %add.75.rest_1_), channel_id=1, source_target_pairs={{0,6},{1,7},{2,4},{3,5},{4,2},{5,3},{6,0},{7,1},{8,14},{9,15},{10,... | collective-permute-start | bytes 49160 | tf_op jit(solution)/shard_map/ppermute | solution.py:26
  181.2 3.9 %collective-permute-start.33 = (f32[64,64]{1,0:T(8,128)S(1)}, f32[64,64]{1,0:T(8,128)S(1)}, u32[]{:S(2)}, u32[]{:S(2)}) collective-permute-start(f32[64,64]{1,0:T(8,128)S(1)} %add.75.rest_1_), channel_id=1, source_target_pairs={{0,4},{1,5},{2,6},{3,7},{4,0},{5,1},{6,2},{7,3},{8,12},{9,13},{10,... | collective-permute-start | bytes 49160 | tf_op jit(solution)/shard_map/ppermute | solution.py:26
  181.6 3.9 %collective-permute-start.32 = (f32[64,64]{1,0:T(8,128)S(1)}, f32[64,64]{1,0:T(8,128)S(1)}, u32[]{:S(2)}, u32[]{:S(2)}) collective-permute-start(f32[64,64]{1,0:T(8,128)S(1)} %add.75.rest_1_), channel_id=1, source_target_pairs={{0,2},{1,3},{2,0},{3,1},{4,6},{5,7},{6,4},{7,5},{8,10},{9,11},{10,... | collective-permute-start | bytes 49160 | tf_op jit(solution)/shard_map/ppermute | solution.py:26
  191.4 15.1 %collective-permute-start.44 = (bf16[16,64,128]{2,1,0:T(8,128)(2,1)S(1)}, bf16[16,64,128]{2,1,0:T(8,128)(2,1)S(1)}, u32[]{:S(2)}, u32[]{:S(2)}) collective-permute-start(bf16[16,64,128]{2,1,0:T(8,128)(2,1)S(1)} %get-tuple-element.70), channel_id=1, source_target_pairs={{0,2},{1,3},{2,0},{3,1},{4,6},{5,7},{6,4},{7,5},{8,10},{9,11},{10,... | collective-permute-start | bytes 786440 | tf_op jit(solution)/shard_map/ppermute | solution.py:26
  192.6 14.0 %collective-permute-start.45 = (bf16[16,64,128]{2,1,0:T(8,128)(2,1)S(1)}, bf16[16,64,128]{2,1,0:T(8,128)(2,1)S(1)}, u32[]{:S(2)}, u32[]{:S(2)}) collective-permute-start(bf16[16,64,128]{2,1,0:T(8,128)(2,1)S(1)} %get-tuple-element.71), channel_id=1, source_target_pairs={{0,4},{1,5},{2,6},{3,7},{4,0},{5,1},{6,2},{7,3},{8,12},{9,13},{10,... | collective-permute-start | bytes 786440 | tf_op jit(solution)/shard_map/ppermute | solution.py:26
  193.9 12.7 %collective-permute-start.46 = (bf16[16,64,128]{2,1,0:T(8,128)(2,1)S(1)}, bf16[16,64,128]{2,1,0:T(8,128)(2,1)S(1)}, u32[]{:S(2)}, u32[]{:S(2)}) collective-permute-start(bf16[16,64,128]{2,1,0:T(8,128)(2,1)S(1)} %get-tuple-element.72), channel_id=1, source_target_pairs={{0,6},{1,7},{2,4},{3,5},{4,2},{5,3},{6,0},{7,1},{8,14},{9,15},{10,... | collective-permute-start | bytes 786440 | tf_op jit(solution)/shard_map/ppermute | solution.py:26
  195.0 5.8 %collective-permute-start.43 = (f32[64,64]{1,0:T(8,128)S(1)}, f32[64,64]{1,0:T(8,128)S(1)}, u32[]{:S(2)}, u32[]{:S(2)}) collective-permute-start(f32[64,64]{1,0:T(8,128)S(1)} %get-tuple-element.69.refs_0_), channel_id=1, source_target_pairs={{0,24},{8,16},{16,8},{24,0},{1,25},{9,17},{17,9},{25,1},{2,26},{10... | collective-permute-start | bytes 49160 | tf_op jit(solution)/shard_map/ppermute | solution.py:26
  196.8 4.8 %collective-permute-start.42 = (f32[64,64]{1,0:T(8,128)S(1)}, f32[64,64]{1,0:T(8,128)S(1)}, u32[]{:S(2)}, u32[]{:S(2)}) collective-permute-start(f32[64,64]{1,0:T(8,128)S(1)} %get-tuple-element.69.refs_0_), channel_id=1, source_target_pairs={{0,16},{8,24},{16,0},{24,8},{1,17},{9,25},{17,1},{25,9},{2,18},{10... | collective-permute-start | bytes 49160 | tf_op jit(solution)/shard_map/ppermute | solution.py:26
  200.7 3.9 %collective-permute-start.41 = (f32[64,64]{1,0:T(8,128)S(1)}, f32[64,64]{1,0:T(8,128)S(1)}, u32[]{:S(2)}, u32[]{:S(2)}) collective-permute-start(f32[64,64]{1,0:T(8,128)S(1)} %get-tuple-element.69.refs_0_), channel_id=1, source_target_pairs={{0,8},{8,0},{16,24},{24,16},{1,9},{9,1},{17,25},{25,17},{2,10},{10... | collective-permute-start | bytes 49160 | tf_op jit(solution)/shard_map/ppermute | solution.py:26
  208.6 4.9 %collective-permute-start.50 = (f32[64,64]{1,0:T(8,128)S(1)}, f32[64,64]{1,0:T(8,128)S(1)}, u32[]{:S(2)}, u32[]{:S(2)}) collective-permute-start(f32[64,64]{1,0:T(8,128)S(1)} %add.76), channel_id=1, source_target_pairs={{0,6},{1,7},{2,4},{3,5},{4,2},{5,3},{6,0},{7,1},{8,14},{9,15},{10,... | collective-permute-start | bytes 49160 | tf_op jit(solution)/shard_map/ppermute | solution.py:26
  210.5 3.9 %collective-permute-start.49 = (f32[64,64]{1,0:T(8,128)S(1)}, f32[64,64]{1,0:T(8,128)S(1)}, u32[]{:S(2)}, u32[]{:S(2)}) collective-permute-start(f32[64,64]{1,0:T(8,128)S(1)} %add.76), channel_id=1, source_target_pairs={{0,4},{1,5},{2,6},{3,7},{4,0},{5,1},{6,2},{7,3},{8,12},{9,13},{10,... | collective-permute-start | bytes 49160 | tf_op jit(solution)/shard_map/ppermute | solution.py:26
  211.2 3.9 %collective-permute-start.48 = (f32[64,64]{1,0:T(8,128)S(1)}, f32[64,64]{1,0:T(8,128)S(1)}, u32[]{:S(2)}, u32[]{:S(2)}) collective-permute-start(f32[64,64]{1,0:T(8,128)S(1)} %add.76), channel_id=1, source_target_pairs={{0,2},{1,3},{2,0},{3,1},{4,6},{5,7},{6,4},{7,5},{8,10},{9,11},{10,... | collective-permute-start | bytes 49160 | tf_op jit(solution)/shard_map/ppermute | solution.py:26
  215.1 6.0 %collective-permute-start.53 = (f32[64,64]{1,0:T(8,128)S(1)}, f32[64,64]{1,0:T(8,128)S(1)}, u32[]{:S(2)}, u32[]{:S(2)}) collective-permute-start(f32[64,64]{1,0:T(8,128)S(1)} %add_add_fusion.refs_0_), channel_id=1, source_target_pairs={{0,24},{8,16},{16,8},{24,0},{1,25},{9,17},{17,9},{25,1},{2,26},{10... | collective-permute-start | bytes 49160 | tf_op jit(solution)/shard_map/ppermute | solution.py:26
  217.1 5.3 %collective-permute-start.52 = (f32[64,64]{1,0:T(8,128)S(1)}, f32[64,64]{1,0:T(8,128)S(1)}, u32[]{:S(2)}, u32[]{:S(2)}) collective-permute-start(f32[64,64]{1,0:T(8,128)S(1)} %add_add_fusion.refs_0_), channel_id=1, source_target_pairs={{0,16},{8,24},{16,0},{24,8},{1,17},{9,25},{17,1},{25,9},{2,18},{10... | collective-permute-start | bytes 49160 | tf_op jit(solution)/shard_map/ppermute | solution.py:26
  218.2 4.2 %collective-permute-start.51 = (f32[64,64]{1,0:T(8,128)S(1)}, f32[64,64]{1,0:T(8,128)S(1)}, u32[]{:S(2)}, u32[]{:S(2)}) collective-permute-start(f32[64,64]{1,0:T(8,128)S(1)} %add_add_fusion.refs_0_), channel_id=1, source_target_pairs={{0,8},{8,0},{16,24},{24,16},{1,9},{9,1},{17,25},{25,17},{2,10},{10... | collective-permute-start | bytes 49160 | tf_op jit(solution)/shard_map/ppermute | solution.py:26
  (14 other events, 117.1 us)
